TPU v7x, 32 devices: a whole 2x2x4 slice. The times are simulated.
32 devices in a mesh: dp: 4 (over x, core), seq: 8 (over z, y).
Axes of the slice: x: 2, y: 2, z: 4, core: 2. Of those that a mesh axis runs over, the one named last changes fastest.
Arguments:
- pre_gate: bfloat16 [4, 1024, 2048], P('dp', 'seq'), may hold values from -6 to 6
- post_gate: bfloat16 [4, 1024, 2048], P('dp', 'seq'), may hold values from -6 to 6
- values: bfloat16 [4, 1024, 2048], P('dp', 'seq'), may hold values from -6 to 6
- cotangent: bfloat16 [4, 1024, 2048], P('dp', 'seq'), may hold values from -6 to 6
- filters: bfloat16 [1024, 16], P(('dp', 'seq')), may hold values from -0.1875 to 0.1875
Outputs:
- output: bfloat16 [4, 1024, 2048], P('dp', 'seq')
- grad_pre: bfloat16 [4, 1024, 2048], P('dp', 'seq')
- grad_post: bfloat16 [4, 1024, 2048], P('dp', 'seq')
- grad_values: bfloat16 [4, 1024, 2048], P('dp', 'seq')
- grad_filters: float32 [1024, 16], P(('dp', 'seq'))
All inputs are finite; a program needn't handle non-finite values.
Results may differ from a plain program's by a relative error of at most 0.005.
Values may be sent and summed in bfloat16 or wider, within the bound.
No kernel may reach another device: no remote copies, remote signals or barrier semaphores. Data moves between devices by JAX's collectives and lax.ppermute only.
A program may use at most 128 MiB of HBM per device.

v0:
```python
import jax
import jax.numpy as jnp
import numpy as np
from jax import lax
from jax.sharding import PartitionSpec as P

K = 1024


def shifted(value, axis, steps):
    count = lax.axis_size(axis)
    first, last = (max(0, -steps), min(count, count - steps))
    return lax.ppermute(value, axis, [(source, source + steps) for source in range(first, last)])


def tile_index(lag_blocks, shard_len):
    offsets = np.arange(lag_blocks)[:, None, None] * shard_len
    rows_idx = np.arange(shard_len)[None, :, None]
    cols_idx = np.arange(shard_len)[None, None, :]
    return (offsets + rows_idx - cols_idx + shard_len).astype(np.int32)


def build_tiles(all_taps, lag_blocks, shard_len):
    tap_count = all_taps.shape[0]
    needed = (lag_blocks + 1) * shard_len
    trailing = max(needed - shard_len - tap_count, 0)
    padded = jnp.concatenate(
        [
            jnp.zeros((shard_len, all_taps.shape[1]), all_taps.dtype),
            all_taps,
            jnp.zeros((trailing, all_taps.shape[1]), all_taps.dtype),
        ],
        axis=0,
    )
    columns = padded.T
    return columns[:, tile_index(lag_blocks, shard_len)]


def earlier_relay(piece_in, history_len):

    def earlier_advance(moving, unused):
        arrived = shifted(moving, "seq", 1)
        return (arrived, arrived)

    unused_last, stacked = lax.scan(earlier_advance, piece_in, None, length=history_len)
    return jnp.concatenate([piece_in[None], stacked], axis=0)


def later_relay(piece_in, history_len):

    def later_advance(moving, unused):
        arrived = shifted(moving, "seq", -1)
        return (arrived, arrived)

    unused_last, stacked = lax.scan(later_advance, piece_in, None, length=history_len)
    return jnp.concatenate([piece_in[None], stacked], axis=0)


def lag_window(gated_rows, history, local_groups, group_width, lag_count):
    row_count = gated_rows.shape[0]
    span_len = history.shape[0]
    front_zero = jnp.zeros((row_count, history.shape[1]), history.dtype)
    widened = jnp.concatenate([front_zero, history], axis=0)
    gated_grp = gated_rows.reshape(row_count, local_groups, group_width).transpose(1, 0, 2)
    hist_grp = widened.reshape(span_len + row_count, local_groups, group_width).transpose(1, 0, 2)

    def one_group(pair_in):
        gated_one, hist_one = pair_in
        product = lax.dot_general(
            gated_one, hist_one, (((1,), (1,)), ((), ())), preferred_element_type=jnp.float32
        )
        padded = jnp.pad(product, ((0, 0), (0, row_count)))
        flat_line = jnp.concatenate(
            [padded.reshape(-1), jnp.zeros((row_count,), jnp.float32)], axis=0
        )
        skewed = flat_line.reshape(row_count, span_len + 2 * row_count + 1)
        diag_sums = jnp.sum(skewed, axis=0)
        return jnp.flip(diag_sums[1 : span_len + 1], axis=0)[:lag_count]

    return lax.map(one_group, (gated_grp, hist_grp))


def shards(pre_gate, post_gate, values, cotangent, filters):
    shard_len = pre_gate.shape[1]
    channels = pre_gate.shape[2]
    groups = filters.shape[1]
    group_size = channels // groups
    seq_count = lax.axis_size("seq")
    all_taps = lax.all_gather(filters, ("dp", "seq"), axis=0, tiled=True)
    mixed_in = (pre_gate[0].astype(jnp.float32) * values[0]).astype(jnp.bfloat16)
    gated = (cotangent[0].astype(jnp.float32) * post_gate[0]).astype(jnp.bfloat16)
    history_len = min(-(-K // shard_len), seq_count - 1)
    lag_blocks = history_len + 1
    mixed_ext = earlier_relay(mixed_in, history_len)
    gated_ext = later_relay(gated, history_len)
    mixed_four = mixed_ext.reshape(lag_blocks, shard_len, groups, group_size)
    gated_four = gated_ext.reshape(lag_blocks, shard_len, groups, group_size)
    tiles = build_tiles(all_taps, lag_blocks, shard_len)
    convolved = jnp.einsum(
        "gmij,mjgc->igc", tiles, mixed_four, preferred_element_type=jnp.float32
    ).reshape(shard_len, channels)
    carried = jnp.einsum(
        "gmji,mjgc->igc", tiles, gated_four, preferred_element_type=jnp.float32
    ).reshape(shard_len, channels)
    hist_len = lag_blocks * shard_len
    lag_count = min(K, hist_len)
    history = jnp.flip(mixed_ext, axis=0).reshape(hist_len, channels)
    lag_local = lag_window(gated, history, groups, group_size, lag_count)
    partial_grads = lag_local.T
    output = (post_gate[0].astype(jnp.float32) * convolved).astype(jnp.bfloat16)
    grad_post = (cotangent[0].astype(jnp.float32) * convolved).astype(jnp.bfloat16)
    grad_pre = (carried * values[0]).astype(jnp.bfloat16)
    grad_values = (carried * pre_gate[0]).astype(jnp.bfloat16)
    owned = lax.psum_scatter(partial_grads, ("dp", "seq"), scatter_dimension=0, tiled=True)
    total_tokens = lax.axis_size("dp") * shard_len * seq_count * group_size
    grad_filters = owned / float(total_tokens**0.5)
    return (output[None], grad_pre[None], grad_post[None], grad_values[None], grad_filters)


def solution(mesh):
    return jax.shard_map(
        shards,
        mesh=mesh,
        in_specs=(
            P("dp", "seq", None),
            P("dp", "seq", None),
            P("dp", "seq", None),
            P("dp", "seq", None),
            P(("dp", "seq"), None),
        ),
        out_specs=(
            P("dp", "seq", None),
            P("dp", "seq", None),
            P("dp", "seq", None),
            P("dp", "seq", None),
            P(("dp", "seq"), None),
        ),
        check_vma=False,
    )
```

profile of v0, /device:TPU:0, one launch (start us, length us, event | category | flops | bytes accessed | tf_op | source)
XLA Modules:
  0.0 988.3 jit_solution(10712451121485565493)
XLA Ops:
  9.6 70.6 %all-gather = bf16[32,32,16]{1,2,0:T(8,128)(2,1)S(1)} all-gather(bf16[1,32,16]{1,2,0:T(8,128)(2,1)} %bitcast.78), channel_id=1, replica_groups=mesh['dp'=4,'seq'=8] {'dp','seq'}, dimensions={0}, use_global_device_ids=true | all-gather | bytes 33792 | tf_op jit(solution)/shard_map/all_gather | solution.py:89
  81.6 453.8 %gather_fusion = bf16[131072,16]{1,0:T(8,128)(2,1)} fusion(bf16[16,1152]{0,1:T(8,128)(2,1)S(1)} %pad_bitcast_fusion, s32[131072]{0:T(1024)S(1)} %broadcast_clamp_fusion), kind=kCustom, calls=%fused_computation | custom fusion | bytes 8912896 | tf_op jit(solution)/shard_map/gather | solution.py:36
  535.4 29.0 %copy.40 = bf16[8,128,128,16]{2,1,0,3:T(8,128)(2,1)} copy(bf16[8,128,128,16]{3,2,1,0:T(8,128)(2,1)} %bitcast.62) | data formatting | bytes 8388608 | tf_op jit(solution)/shard_map/gather | solution.py:36
  564.5 112.4 %while.37 = (s32[]{:T(128)}, bf16[128,2048]{1,0:T(8,128)(2,1)S(1)}, bf16[7,128,2048]{1,2,0:T(8,128)(2,1)}, s32[]{:T(128)}) while((s32[]{:T(128)}, bf16[128,2048]{1,0:T(8,128)(2,1)S(1)}, bf16[7,128,2048]{1,2,0:T(8,128)(2,1)}, s32[]{:T(128)}) %tuple.61), condition=%wide.region_3.4_spmd, body=%wide.region_2.3_spmd.sunk | while | flops 2 | bytes 5242985 | solution.py:55
  565.8 12.5 %collective-permute-done.1 = bf16[128,2048]{1,0:T(8,128)(2,1)S(1)} collective-permute-done((bf16[128,2048]{1,0:T(8,128)(2,1)S(1)}, bf16[128,2048]{1,0:T(8,128)(2,1)S(1)}, u32[]{:S(2)}, u32[]{:S(2)}) %collective-permute-start.1) | collective-permute-done | bytes 524320 | tf_op jit(solution)/shard_map/while/body/eval_jaxpr/ppermute | solution.py:13
  580.7 13.5 %collective-permute-done.1 = bf16[128,2048]{1,0:T(8,128)(2,1)S(1)} collective-permute-done((bf16[128,2048]{1,0:T(8,128)(2,1)S(1)}, bf16[128,2048]{1,0:T(8,128)(2,1)S(1)}, u32[]{:S(2)}, u32[]{:S(2)}) %collective-permute-start.1) | collective-permute-done | bytes 524320 | tf_op jit(solution)/shard_map/while/body/eval_jaxpr/ppermute | solution.py:13
  596.8 14.7 %collective-permute-done.1 = bf16[128,2048]{1,0:T(8,128)(2,1)S(1)} collective-permute-done((bf16[128,2048]{1,0:T(8,128)(2,1)S(1)}, bf16[128,2048]{1,0:T(8,128)(2,1)S(1)}, u32[]{:S(2)}, u32[]{:S(2)}) %collective-permute-start.1) | collective-permute-done | bytes 524320 | tf_op jit(solution)/shard_map/while/body/eval_jaxpr/ppermute | solution.py:13
  614.0 14.9 %collective-permute-done.1 = bf16[128,2048]{1,0:T(8,128)(2,1)S(1)} collective-permute-done((bf16[128,2048]{1,0:T(8,128)(2,1)S(1)}, bf16[128,2048]{1,0:T(8,128)(2,1)S(1)}, u32[]{:S(2)}, u32[]{:S(2)}) %collective-permute-start.1) | collective-permute-done | bytes 524320 | tf_op jit(solution)/shard_map/while/body/eval_jaxpr/ppermute | solution.py:13
  631.4 14.6 %collective-permute-done.1 = bf16[128,2048]{1,0:T(8,128)(2,1)S(1)} collective-permute-done((bf16[128,2048]{1,0:T(8,128)(2,1)S(1)}, bf16[128,2048]{1,0:T(8,128)(2,1)S(1)}, u32[]{:S(2)}, u32[]{:S(2)}) %collective-permute-start.1) | collective-permute-done | bytes 524320 | tf_op jit(solution)/shard_map/while/body/eval_jaxpr/ppermute | solution.py:13
  648.5 14.4 %collective-permute-done.1 = bf16[128,2048]{1,0:T(8,128)(2,1)S(1)} collective-permute-done((bf16[128,2048]{1,0:T(8,128)(2,1)S(1)}, bf16[128,2048]{1,0:T(8,128)(2,1)S(1)}, u32[]{:S(2)}, u32[]{:S(2)}) %collective-permute-start.1) | collective-permute-done | bytes 524320 | tf_op jit(solution)/shard_map/while/body/eval_jaxpr/ppermute | solution.py:13
  665.3 10.4 %collective-permute-done.1 = bf16[128,2048]{1,0:T(8,128)(2,1)S(1)} collective-permute-done((bf16[128,2048]{1,0:T(8,128)(2,1)S(1)}, bf16[128,2048]{1,0:T(8,128)(2,1)S(1)}, u32[]{:S(2)}, u32[]{:S(2)}) %collective-permute-start.1) | collective-permute-done | bytes 524320 | tf_op jit(solution)/shard_map/while/body/eval_jaxpr/ppermute | solution.py:13
  684.7 93.8 %while.36 = (s32[]{:T(128)}, bf16[128,2048]{1,0:T(8,128)(2,1)S(1)}, bf16[7,128,2048]{2,1,0:T(8,128)(2,1)}, s32[]{:T(128)}) while((s32[]{:T(128)}, bf16[128,2048]{1,0:T(8,128)(2,1)S(1)}, bf16[7,128,2048]{2,1,0:T(8,128)(2,1)}, s32[]{:T(128)}) %tuple.64), condition=%wide.region_1.2_spmd, body=%wide.region_0.1_spmd.sunk | while | flops 2 | bytes 4194409 | solution.py:45
  689.6 8.6 collective-permute-done
  703.5 7.7 collective-permute-done
  716.5 6.7 collective-permute-done
  728.7 6.6 collective-permute-done
  736.2 7.5 collective-permute-start
  743.7 7.9 collective-permute-done
  757.8 6.9 collective-permute-done
  770.9 6.6 collective-permute-done
  787.5 6.5 copy.53
  798.7 35.5 %while.38 = (s32[]{:T(128)}, f32[16,1024]{1,0:T(8,128)S(1)}, bf16[16,128,128]{2,1,0:T(8,128)(2,1)S(1)}, bf16[16,1152,128]{1,2,0:T(8,128)(2,1)}, s32[]{:T(128)}, /*index=5*/f32[]{:T(128)}, s32[]{:T(128)}) while((s32[]{:T(128)}, f32[16,1024]{1,0:T(8,128)S(1)}, bf16[16,128,128]{2,1,0:T(8,128)(2,1)S(1)}, bf16[16,1152,128]{1,2,0:T(8,128)(2,1)}, ...), condition=%wide.region_6.7_spmd, body=%wide.region_4.6_spmd.sunk | while | flops 37911424 | bytes 6783081 | solution.py:80
  835.5 6.1 copy.37
  847.8 132.2 %reduce-scatter.4.cloned.1.call-done = f32[32,16]{1,0:T(8,128)} async-done(((f32[1024,16]{1,0:T(8,128)}), f32[32,16]{1,0:T(8,128)}) %reduce-scatter.4.cloned.1.call-update) | async-done | bytes 2064
  (225 shorter events, 120.8 us)
Async XLA Ops:
  7.2 972.9 %reduce-scatter.4.cloned.1.call-start = ((), (), s32[]{:S(2)}) async-start(), calls=%async_computation.1 | async-start | bytes 540672
  564.5 13.8 %collective-permute-start.1 = (bf16[128,2048]{1,0:T(8,128)(2,1)S(1)}, bf16[128,2048]{1,0:T(8,128)(2,1)S(1)}, u32[]{:S(2)}, u32[]{:S(2)}) collective-permute-start(bf16[128,2048]{1,0:T(8,128)(2,1)S(1)} %get-tuple-element.196), channel_id=1, source_target_pairs={{1,0},{2,1},{3,2},{4,3},{5,4},{6,5},{7,6},{9,8},{10,9},{11,10},{12... | collective-permute-start | bytes 1572872 | tf_op jit(solution)/shard_map/while/body/eval_jaxpr/ppermute | solution.py:13
  579.4 14.8 %collective-permute-start.1 = (bf16[128,2048]{1,0:T(8,128)(2,1)S(1)}, bf16[128,2048]{1,0:T(8,128)(2,1)S(1)}, u32[]{:S(2)}, u32[]{:S(2)}) collective-permute-start(bf16[128,2048]{1,0:T(8,128)(2,1)S(1)} %get-tuple-element.196), channel_id=1, source_target_pairs={{1,0},{2,1},{3,2},{4,3},{5,4},{6,5},{7,6},{9,8},{10,9},{11,10},{12... | collective-permute-start | bytes 1572872 | tf_op jit(solution)/shard_map/while/body/eval_jaxpr/ppermute | solution.py:13
  595.5 16.0 %collective-permute-start.1 = (bf16[128,2048]{1,0:T(8,128)(2,1)S(1)}, bf16[128,2048]{1,0:T(8,128)(2,1)S(1)}, u32[]{:S(2)}, u32[]{:S(2)}) collective-permute-start(bf16[128,2048]{1,0:T(8,128)(2,1)S(1)} %get-tuple-element.196), channel_id=1, source_target_pairs={{1,0},{2,1},{3,2},{4,3},{5,4},{6,5},{7,6},{9,8},{10,9},{11,10},{12... | collective-permute-start | bytes 1572872 | tf_op jit(solution)/shard_map/while/body/eval_jaxpr/ppermute | solution.py:13
  612.7 16.2 %collective-permute-start.1 = (bf16[128,2048]{1,0:T(8,128)(2,1)S(1)}, bf16[128,2048]{1,0:T(8,128)(2,1)S(1)}, u32[]{:S(2)}, u32[]{:S(2)}) collective-permute-start(bf16[128,2048]{1,0:T(8,128)(2,1)S(1)} %get-tuple-element.196), channel_id=1, source_target_pairs={{1,0},{2,1},{3,2},{4,3},{5,4},{6,5},{7,6},{9,8},{10,9},{11,10},{12... | collective-permute-start | bytes 1572872 | tf_op jit(solution)/shard_map/while/body/eval_jaxpr/ppermute | solution.py:13
  630.1 15.9 %collective-permute-start.1 = (bf16[128,2048]{1,0:T(8,128)(2,1)S(1)}, bf16[128,2048]{1,0:T(8,128)(2,1)S(1)}, u32[]{:S(2)}, u32[]{:S(2)}) collective-permute-start(bf16[128,2048]{1,0:T(8,128)(2,1)S(1)} %get-tuple-element.196), channel_id=1, source_target_pairs={{1,0},{2,1},{3,2},{4,3},{5,4},{6,5},{7,6},{9,8},{10,9},{11,10},{12... | collective-permute-start | bytes 1572872 | tf_op jit(solution)/shard_map/while/body/eval_jaxpr/ppermute | solution.py:13
  647.2 15.7 %collective-permute-start.1 = (bf16[128,2048]{1,0:T(8,128)(2,1)S(1)}, bf16[128,2048]{1,0:T(8,128)(2,1)S(1)}, u32[]{:S(2)}, u32[]{:S(2)}) collective-permute-start(bf16[128,2048]{1,0:T(8,128)(2,1)S(1)} %get-tuple-element.196), channel_id=1, source_target_pairs={{1,0},{2,1},{3,2},{4,3},{5,4},{6,5},{7,6},{9,8},{10,9},{11,10},{12... | collective-permute-start | bytes 1572872 | tf_op jit(solution)/shard_map/while/body/eval_jaxpr/ppermute | solution.py:13
  664.0 11.7 %collective-permute-start.1 = (bf16[128,2048]{1,0:T(8,128)(2,1)S(1)}, bf16[128,2048]{1,0:T(8,128)(2,1)S(1)}, u32[]{:S(2)}, u32[]{:S(2)}) collective-permute-start(bf16[128,2048]{1,0:T(8,128)(2,1)S(1)} %get-tuple-element.196), channel_id=1, source_target_pairs={{1,0},{2,1},{3,2},{4,3},{5,4},{6,5},{7,6},{9,8},{10,9},{11,10},{12... | collective-permute-start | bytes 1572872 | tf_op jit(solution)/shard_map/while/body/eval_jaxpr/ppermute | solution.py:13
  676.9 5.1 copy-start.2
  684.7 13.5 %collective-permute-start = (bf16[128,2048]{1,0:T(8,128)(2,1)S(1)}, bf16[128,2048]{1,0:T(8,128)(2,1)S(1)}, u32[]{:S(2)}, u32[]{:S(2)}) collective-permute-start(bf16[128,2048]{1,0:T(8,128)(2,1)S(1)} %get-tuple-element.208), channel_id=1, source_target_pairs={{0,1},{1,2},{2,3},{3,4},{4,5},{5,6},{6,7},{8,9},{9,10},{10,11},{11... | collective-permute-start | bytes 1572872 | tf_op jit(solution)/shard_map/while/body/eval_jaxpr/ppermute | solution.py:13
  699.1 12.1 %collective-permute-start = (bf16[128,2048]{1,0:T(8,128)(2,1)S(1)}, bf16[128,2048]{1,0:T(8,128)(2,1)S(1)}, u32[]{:S(2)}, u32[]{:S(2)}) collective-permute-start(bf16[128,2048]{1,0:T(8,128)(2,1)S(1)} %get-tuple-element.208), channel_id=1, source_target_pairs={{0,1},{1,2},{2,3},{3,4},{4,5},{5,6},{6,7},{8,9},{9,10},{10,11},{11... | collective-permute-start | bytes 1572872 | tf_op jit(solution)/shard_map/while/body/eval_jaxpr/ppermute | solution.py:13
  712.1 11.1 %collective-permute-start = (bf16[128,2048]{1,0:T(8,128)(2,1)S(1)}, bf16[128,2048]{1,0:T(8,128)(2,1)S(1)}, u32[]{:S(2)}, u32[]{:S(2)}) collective-permute-start(bf16[128,2048]{1,0:T(8,128)(2,1)S(1)} %get-tuple-element.208), channel_id=1, source_target_pairs={{0,1},{1,2},{2,3},{3,4},{4,5},{5,6},{6,7},{8,9},{9,10},{10,11},{11... | collective-permute-start | bytes 1572872 | tf_op jit(solution)/shard_map/while/body/eval_jaxpr/ppermute | solution.py:13
  724.1 11.2 %collective-permute-start = (bf16[128,2048]{1,0:T(8,128)(2,1)S(1)}, bf16[128,2048]{1,0:T(8,128)(2,1)S(1)}, u32[]{:S(2)}, u32[]{:S(2)}) collective-permute-start(bf16[128,2048]{1,0:T(8,128)(2,1)S(1)} %get-tuple-element.208), channel_id=1, source_target_pairs={{0,1},{1,2},{2,3},{3,4},{4,5},{5,6},{6,7},{8,9},{9,10},{10,11},{11... | collective-permute-start | bytes 1572872 | tf_op jit(solution)/shard_map/while/body/eval_jaxpr/ppermute | solution.py:13
  736.2 15.3 %collective-permute-start = (bf16[128,2048]{1,0:T(8,128)(2,1)S(1)}, bf16[128,2048]{1,0:T(8,128)(2,1)S(1)}, u32[]{:S(2)}, u32[]{:S(2)}) collective-permute-start(bf16[128,2048]{1,0:T(8,128)(2,1)S(1)} %get-tuple-element.208), channel_id=1, source_target_pairs={{0,1},{1,2},{2,3},{3,4},{4,5},{5,6},{6,7},{8,9},{9,10},{10,11},{11... | collective-permute-start | bytes 1572872 | tf_op jit(solution)/shard_map/while/body/eval_jaxpr/ppermute | solution.py:13
  752.5 12.2 %collective-permute-start = (bf16[128,2048]{1,0:T(8,128)(2,1)S(1)}, bf16[128,2048]{1,0:T(8,128)(2,1)S(1)}, u32[]{:S(2)}, u32[]{:S(2)}) collective-permute-start(bf16[128,2048]{1,0:T(8,128)(2,1)S(1)} %get-tuple-element.208), channel_id=1, source_target_pairs={{0,1},{1,2},{2,3},{3,4},{4,5},{5,6},{6,7},{8,9},{9,10},{10,11},{11... | collective-permute-start | bytes 1572872 | tf_op jit(solution)/shard_map/while/body/eval_jaxpr/ppermute | solution.py:13
  765.6 12.0 %collective-permute-start = (bf16[128,2048]{1,0:T(8,128)(2,1)S(1)}, bf16[128,2048]{1,0:T(8,128)(2,1)S(1)}, u32[]{:S(2)}, u32[]{:S(2)}) collective-permute-start(bf16[128,2048]{1,0:T(8,128)(2,1)S(1)} %get-tuple-element.208), channel_id=1, source_target_pairs={{0,1},{1,2},{2,3},{3,4},{4,5},{5,6},{6,7},{8,9},{9,10},{10,11},{11... | collective-permute-start | bytes 1572872 | tf_op jit(solution)/shard_map/while/body/eval_jaxpr/ppermute | solution.py:13
  841.6 5.0 copy-start
  841.6 5.0 copy-start.1
Sparse Core Ops, SparseCore 0:
  835.4 144.6 reduce-scatter.3
where the time goes:
time: 991 us; the launch traced here: 988 us
  local copies, waits for them, and re-layouts  538 us (54%)
  waiting for transfers between devices  278 us (28%)
  blocking collectives  70.6 us (7%)
  starting transfers between devices  45.5 us (5%)
  matrix products  28.3 us (3%)
  between operations  14.2 us (1%)
  other arithmetic  11.8 us (1%)
    gather x2, local copies, waits for them, and re-layouts, build_tiles(): return columns[:, tile_index(lag_blocks, shard_len)]  483 us
    ppermute x14, waiting for transfers between devices, shifted(): lax.ppermute(value, axis, [(source, source + steps) for source in range(f...  146 us
    unnamed x2, waiting for transfers between devices  132 us
    all_gather x1, blocking collectives, shards(): all_taps = lax.all_gather(filters, ('dp', 'seq'), axis=0, tiled=True)  70.6 us
    ppermute x14, starting transfers between devices, shifted(): lax.ppermute(value, axis, [(source, source + steps) for source in range(f...  45.5 us
  transfers between devices with their start and end apart: 15, of which 15 were waited for; matrix products, arithmetic and copies ran while one was open for 1% of the time, Pallas kernels for 0%

commit v1 on v0

--- a/solution.py
+++ b/solution.py
@@ -2,6 +2,8 @@
 import jax.numpy as jnp
 import numpy as np
 from jax import lax
+from jax.experimental import pallas as pl
+from jax.experimental.pallas import tpu as pltpu
 from jax.sharding import PartitionSpec as P
 
 K = 1024
@@ -117,9 +119,230 @@
     return (output[None], grad_pre[None], grad_post[None], grad_values[None], grad_filters)
 
 
+BLOCK = 128
+
+
+def swap_fits(pre_gate, post_gate, values, cotangent, filters):
+    seq_count, dp_count = lax.axis_size("seq"), lax.axis_size("dp")
+    channels, groups = pre_gate.shape[2], filters.shape[1]
+    return (
+        groups % seq_count == 0
+        and channels // groups == BLOCK
+        and pre_gate.shape[0] == 1
+        and pre_gate.shape[1] == BLOCK
+        and seq_count % 2 == 0
+        and seq_count & (seq_count - 1) == 0
+        and seq_count * BLOCK == K
+        and filters.shape[0] * seq_count * dp_count == K
+    )
+
+
+def pack_kernel(pre_ref, post_ref, values_ref, cot_ref, out_ref):
+    f32 = jnp.float32
+    out_ref[0, :BLOCK] = (pre_ref[0].astype(f32) * values_ref[0].astype(f32)).astype(jnp.bfloat16)
+    out_ref[0, BLOCK:] = (cot_ref[0].astype(f32) * post_ref[0].astype(f32)).astype(jnp.bfloat16)
+
+
+def gate_and_pack(pre_gate, post_gate, values, cotangent, parts):
+    width = pre_gate.shape[2] // parts
+    spec = pl.BlockSpec((1, BLOCK, width), lambda i: (0, 0, i))
+    return pl.pallas_call(
+        pack_kernel,
+        grid=(parts,),
+        in_specs=[spec] * 4,
+        out_specs=pl.BlockSpec((1, 2 * BLOCK, width), lambda i: (i, 0, 0)),
+        out_shape=jax.ShapeDtypeStruct((parts, 2 * BLOCK, width), jnp.bfloat16),
+        cost_estimate=pl.CostEstimate(flops=4 * pre_gate.size, bytes_accessed=12 * pre_gate.size, transcendentals=0),
+        name="gate_and_pack",
+    )(pre_gate, post_gate, values, cotangent)
+
+
+def toeplitz_kernel(parts, dp_count, rows, index_ref, *refs):
+    pieces, (causal_ref, anti_ref, taps_ref) = refs[:parts], refs[parts:]
+    dp_index, seq_index = index_ref[0], index_ref[1]
+    for q in range(parts):
+        source = lax.rem(seq_index + parts - q, parts)
+        piece = pieces[q][...].astype(jnp.float32)
+        for p in range(dp_count):
+            owner = lax.rem(dp_index + dp_count - p, dp_count)
+            taps_ref[owner * parts + source] = piece[:, p * rows : (p + 1) * rows]
+    local = causal_ref.shape[0]
+    for g in range(local):
+        which = pl.ds(seq_index * local + g, 1)
+        line = jnp.concatenate([taps_ref[o, which, :] for o in range(parts * dp_count)], axis=1)
+        line = jnp.concatenate([line, jnp.zeros((1, 2 * BLOCK), jnp.float32)], axis=1)
+        spread = jnp.broadcast_to(line, (2 * BLOCK, K + 2 * BLOCK))
+        shear = pltpu.roll(spread, 0, 1, stride=1, stride_axis=0)
+        anti_ref[g] = shear[:, :K].astype(jnp.bfloat16)
+        count = K // BLOCK
+        turned = [shear[:BLOCK, m * BLOCK : (m + 1) * BLOCK].T.astype(jnp.bfloat16) for m in range(count)]
+        turned.append(jnp.zeros((BLOCK, BLOCK), jnp.bfloat16))
+        for b in range(count):
+            causal_ref[g, :BLOCK, b * BLOCK : (b + 1) * BLOCK] = turned[count - 2 - b]
+            causal_ref[g, BLOCK:, b * BLOCK : (b + 1) * BLOCK] = turned[count - 1 - b]
+
+
+def toeplitz(filters):
+    parts, dp_count = lax.axis_size("seq"), lax.axis_size("dp")
+    dp_index, seq_index = lax.axis_index("dp"), lax.axis_index("seq")
+    rows, groups = filters.shape
+    local = groups // parts
+    own = filters.T
+    along = [own]
+    for p in range(1, dp_count):
+        along.append(lax.ppermute(own, "dp", [(i, (i + p) % dp_count) for i in range(dp_count)]))
+    own = jnp.concatenate(along, axis=1)
+    pieces = [own]
+    for q in range(1, parts):
+        pieces.append(lax.ppermute(own, "seq", [(i, (i + q) % parts) for i in range(parts)]))
+    band = jax.ShapeDtypeStruct((local, 2 * BLOCK, K), jnp.bfloat16)
+    vmem = pl.BlockSpec(memory_space=pltpu.VMEM)
+    return pl.pallas_call(
+        lambda *refs: toeplitz_kernel(parts, dp_count, rows, *refs),
+        in_specs=[pl.BlockSpec(memory_space=pltpu.SMEM)] + [vmem] * parts,
+        out_specs=[vmem, vmem],
+        out_shape=[band, band],
+        scratch_shapes=[pltpu.VMEM((parts * dp_count, groups, rows), jnp.float32)],
+        cost_estimate=pl.CostEstimate(flops=2_000_000, bytes_accessed=2_000_000, transcendentals=0),
+        name="toeplitz",
+    )(jnp.stack([dp_index, seq_index]).astype(jnp.int32), *pieces)
+
+
+def convolve_kernel(slabs_ref, causal_ref, anti_ref, out_ref):
+    blocks, _, width = slabs_ref.shape
+    length = blocks * BLOCK
+    for g in range(width // BLOCK):
+        lanes = slice(g * BLOCK, (g + 1) * BLOCK)
+        mixed = slabs_ref[:, :BLOCK, lanes].reshape(length, BLOCK)
+        gated = slabs_ref[:, BLOCK:, lanes].reshape(length, BLOCK)
+        for p in range(blocks // 2):
+            reach = (p + 1) * 2 * BLOCK
+            ahead = length - p * 2 * BLOCK
+            convolved = jnp.dot(causal_ref[g, :, K - reach :], mixed[:reach], preferred_element_type=jnp.float32)
+            carried = jnp.dot(anti_ref[g, :, :ahead], gated[length - ahead :], preferred_element_type=jnp.float32)
+            pair = slice(2 * p, 2 * p + 2)
+            out_ref[pair, :BLOCK, lanes] = convolved.reshape(2, BLOCK, BLOCK).astype(jnp.bfloat16)
+            out_ref[pair, BLOCK:, lanes] = carried.reshape(2, BLOCK, BLOCK).astype(jnp.bfloat16)
+
+
+def convolve(slabs, causal, anti):
+    vmem = pl.BlockSpec(memory_space=pltpu.VMEM)
+    return pl.pallas_call(
+        convolve_kernel,
+        in_specs=[vmem] * 3,
+        out_specs=vmem,
+        out_shape=jax.ShapeDtypeStruct(slabs.shape, jnp.bfloat16),
+        cost_estimate=pl.CostEstimate(flops=1_300_000_000, bytes_accessed=4 * slabs.size, transcendentals=0),
+        name="convolve",
+    )(slabs, causal, anti)
+
+
+def lag_kernel(slabs_ref, out_ref):
+    blocks, _, width = slabs_ref.shape
+    length = blocks * BLOCK
+    count = length + BLOCK
+    exchange = (
+        lax.broadcasted_iota(jnp.int32, (BLOCK, BLOCK), 0) + lax.broadcasted_iota(jnp.int32, (BLOCK, BLOCK), 1)
+        == BLOCK - 1
+    ).astype(jnp.bfloat16)
+    turned = [
+        jnp.dot(exchange, slabs_ref[j, :BLOCK, :], preferred_element_type=jnp.float32).astype(jnp.bfloat16)
+        for j in range(blocks)
+    ]
+    for g in range(width // BLOCK):
+        lanes = slice(g * BLOCK, (g + 1) * BLOCK)
+        mixed = jnp.concatenate([block[:, lanes] for block in turned], axis=0)
+        sums = [None] * blocks
+        for i in range(blocks):
+            gated = slabs_ref[i, BLOCK:, lanes]
+            product = lax.dot_general(
+                mixed[: (i + 1) * BLOCK], gated, (((1,), (1,)), ((), ())), preferred_element_type=jnp.float32
+            )
+            for j in range(i + 1):
+                term = product[j * BLOCK : (j + 1) * BLOCK]
+                sums[i - j] = term if sums[i - j] is None else sums[i - j] + term
+        table = jnp.concatenate(sums + [jnp.zeros((BLOCK, BLOCK), jnp.float32)], axis=1)
+        shear = pltpu.roll(table, 0, 1, stride=1, stride_axis=0)
+        line = pltpu.roll(jnp.sum(shear, axis=0, keepdims=True), count - BLOCK + 1, 1)[:, :length]
+        span = length // out_ref.shape[0]
+        for d in range(out_ref.shape[0]):
+            out_ref[d, g : g + 1] = line[:, d * span : (d + 1) * span]
+
+
+def lag_sums(slabs, dp_count):
+    blocks, _, width = slabs.shape
+    vmem = pl.BlockSpec(memory_space=pltpu.VMEM)
+    return pl.pallas_call(
+        lag_kernel,
+        in_specs=[vmem],
+        out_specs=vmem,
+        out_shape=jax.ShapeDtypeStruct((dp_count, width // BLOCK, K // dp_count), jnp.float32),
+        cost_estimate=pl.CostEstimate(flops=600_000_000, bytes_accessed=2 * slabs.size, transcendentals=0),
+        name="lag_sums",
+    )(slabs)
+
+
+def owned_lags(shares):
+    dp_count, local, span = shares.shape
+    parts = lax.axis_size("seq")
+    dp_index, seq_index = lax.axis_index("dp"), lax.axis_index("seq")
+    total = lax.dynamic_index_in_dim(shares, dp_index, 0, keepdims=False)
+    for p in range(1, dp_count):
+        share = lax.dynamic_index_in_dim(shares, lax.rem(dp_index + p, dp_count), 0, keepdims=False)
+        total = total + lax.ppermute(share, "dp", [(i, (i + p) % dp_count) for i in range(dp_count)])
+    step = 1
+    while step < parts:
+        other = lax.ppermute(total, "seq", [(i, i ^ step) for i in range(parts)])
+        upper = (seq_index // step) % 2 == 1
+        total = jnp.where(upper, jnp.concatenate([other, total]), jnp.concatenate([total, other]))
+        step *= 2
+    rows = span // parts
+    return lax.dynamic_slice_in_dim(total, seq_index * rows, rows, 1)
+
+
+def gates_kernel(pre_ref, post_ref, values_ref, cot_ref, back_ref, out_ref, pre_out, post_out, values_out):
+    f32, bf16 = jnp.float32, jnp.bfloat16
+    convolved, carried = back_ref[0, :BLOCK].astype(f32), back_ref[0, BLOCK:].astype(f32)
+    out_ref[0] = (post_ref[0].astype(f32) * convolved).astype(bf16)
+    post_out[0] = (cot_ref[0].astype(f32) * convolved).astype(bf16)
+    pre_out[0] = (carried * values_ref[0].astype(f32)).astype(bf16)
+    values_out[0] = (carried * pre_ref[0].astype(f32)).astype(bf16)
+
+
+def gate_outputs(pre_gate, post_gate, values, cotangent, back):
+    parts, _, width = back.shape
+    spec = pl.BlockSpec((1, BLOCK, width), lambda i: (0, 0, i))
+    shape = jax.ShapeDtypeStruct(pre_gate.shape, jnp.bfloat16)
+    return pl.pallas_call(
+        gates_kernel,
+        grid=(parts,),
+        in_specs=[spec] * 4 + [pl.BlockSpec((1, 2 * BLOCK, width), lambda i: (i, 0, 0))],
+        out_specs=[spec] * 4,
+        out_shape=[shape] * 4,
+        cost_estimate=pl.CostEstimate(flops=4 * pre_gate.size, bytes_accessed=20 * pre_gate.size, transcendentals=0),
+        name="gate_outputs",
+    )(pre_gate, post_gate, values, cotangent, back)
+
+
+def swapped(pre_gate, post_gate, values, cotangent, filters):
+    parts, dp_count = lax.axis_size("seq"), lax.axis_size("dp")
+    packed = gate_and_pack(pre_gate, post_gate, values, cotangent, parts)
+    slabs = lax.all_to_all(packed, "seq", 0, 0, tiled=True)
+    causal, anti = toeplitz(filters)
+    back = lax.all_to_all(convolve(slabs, causal, anti), "seq", 0, 0, tiled=True)
+    output, grad_pre, grad_post, grad_values = gate_outputs(pre_gate, post_gate, values, cotangent, back)
+    total_tokens = dp_count * parts * pre_gate.shape[1] * (pre_gate.shape[2] // filters.shape[1])
+    grad_filters = owned_lags(lag_sums(slabs, dp_count)).T / float(total_tokens**0.5)
+    return output, grad_pre, grad_post, grad_values, grad_filters
+
+
 def solution(mesh):
+    def chosen(*shard):
+        fits = swap_fits(*shard)
+        return (swapped if fits else shards)(*shard)
+
     return jax.shard_map(
-        shards,
+        chosen,
         mesh=mesh,
         in_specs=(
             P("dp", "seq", None),

time: 991 us -> 89.3 us (0.09)
  local copies, waits for them, and re-layouts: 538 us -> 3.82 us
  waiting for transfers between devices: 278 us -> 25.2 us
  blocking collectives: 70.6 us -> 0 us
  matrix products: 28.3 us -> 0 us
  Pallas kernels: 0 us -> 21.4 us
  between operations: 14.2 us -> 0.75 us
  starting transfers between devices: 45.5 us -> 35.2 us
    gather x2 -> x0, local copies, waits for them, and re-layouts: 483 us -> none  [build_tiles(): return columns[:, tile_index(lag_blocks, shard_len)]]
    unnamed x2 -> x0, waiting for transfers between devices: 132 us -> none
    ppermute x14 -> x16, waiting for transfers between devices: 146 us -> 25.2 us  [the longest x7 12.1 us: toeplitz(): lax.ppermute(own, 'seq', [(i, (i + q) % parts) for i in range(parts)])]
    all_gather x1 -> x0, blocking collectives: 70.6 us -> none  [shards(): all_taps = lax.all_gather(filters, ('dp', 'seq'), axis=0, tiled=True)]
    dot_general x18 -> x0, matrix products: 28.3 us -> none  [the longest x16 18.9 us: one_group(): lax.dot_general(gated_one, hist_one, (((1,), (1,)), ((), ())), preferred_...]
    ppermute x14 -> x16, starting transfers between devices: 45.5 us -> 21.4 us  [the longest x7 9.67 us: toeplitz(): lax.ppermute(own, 'seq', [(i, (i + q) % parts) for i in range(parts)])]
    pallas_call x0 -> x5, Pallas kernels: none -> 21.4 us  [the longest x1 5.95 us: gate_outputs(): pl.pallas_call(gates_kernel, grid=(parts,), in_specs=[spec] * 4 + [pl.Blo...]
    reshape x35 -> x0, local copies, waits for them, and re-layouts: 16.9 us -> none  [the longest x16 9.07 us: one_group(): skewed = flat_line.reshape(row_count, span_len + 2 * row_count + 1)]
  transfers between devices with their start and end apart: 15 -> 18, of which waited for: 15 -> 10; matrix products, arithmetic and copies ran while one was open for 1% -> 3% of each run, Pallas kernels for 0% -> 6%
where the time goes in v1:
time: 89.3 us; the launch traced here: 88.5 us
  starting transfers between devices  35.2 us (39%)
  waiting for transfers between devices  25.2 us (28%)
  Pallas kernels  21.4 us (24%)
  local copies, waits for them, and re-layouts  3.82 us (4%)
  other arithmetic  2.12 us (2%)
    ppermute x7, waiting for transfers between devices, toeplitz(): lax.ppermute(own, 'seq', [(i, (i + q) % parts) for i in range(parts)])  12.1 us
    ppermute x7, starting transfers between devices, toeplitz(): lax.ppermute(own, 'seq', [(i, (i + q) % parts) for i in range(parts)])  9.67 us
    ppermute x3, starting transfers between devices, owned_lags(): other = lax.ppermute(total, 'seq', [(i, i ^ step) for i in range(parts)])  8.23 us
    ppermute x3, waiting for transfers between devices, owned_lags(): other = lax.ppermute(total, 'seq', [(i, i ^ step) for i in range(parts)])  7.48 us
    all_to_all x1, starting transfers between devices, swapped(): slabs = lax.all_to_all(packed, 'seq', 0, 0, tiled=True)  7.41 us
    all_to_all x1, starting transfers between devices, swapped(): lax.all_to_all(convolve(slabs, causal, anti), 'seq', 0, 0, tiled=True)  6.34 us
    pallas_call x1, Pallas kernels, gate_outputs(): pl.pallas_call(gates_kernel, grid=(parts,), in_specs=[spec] * 4 + [pl.Blo...  5.95 us
    pallas_call x1, Pallas kernels, gate_and_pack(): pl.pallas_call(pack_kernel, grid=(parts,), in_specs=[spec] * 4, out_specs...  5.45 us
  transfers between devices with their start and end apart: 18, of which 10 were waited for; matrix products, arithmetic and copies ran while one was open for 3% of the time, Pallas kernels for 6%

profile of v1, /device:TPU:0, one launch (start us, length us, event | category | flops | bytes accessed | tf_op | source)
XLA Modules:
  0.0 88.5 jit_solution(14770256669670708946)
XLA Ops:
  0.6 5.4 %gate_and_pack.1 = bf16[8,256,256]{2,1,0:T(8,128)(2,1)} custom-call(bf16[1,128,2048]{2,1,0:T(8,128)(2,1)} %pre_ref.3, bf16[1,128,2048]{2,1,0:T(8,128)(2,1)} %post_ref.3, bf16[1,128,2048]{2,1,0:T(8,128)(2,1)} %values_ref.3, bf16[1,128,2048]{2,1,0:T(8,128)(2,1)} %cot_ref.3), custom_call_target="tpu_custom_call" | custom-call | flops 1048576 | bytes 3145728 | tf_op jit(solution)/shard_map/gate_and_pack/pallas_call | solution.py:149
  6.1 7.4 %all-to-all-start = ((bf16[8,256,256]{2,1,0:T(8,128)(2,1)}), bf16[8,256,256]{2,1,0:T(8,128)(2,1)S(1)}, u32[]{:S(2)}, u32[]{:S(2)}) async-start(bf16[8,256,256]{2,1,0:T(8,128)(2,1)} %gate_and_pack.1), calls=%async_computation | async-start | bytes 2097152 | tf_op jit(solution)/shard_map/all_to_all | solution.py:330
  15.5 2.3 %collective-permute-done.1 = bf16[16,32]{1,0:T(8,128)(2,1)S(1)} collective-permute-done((bf16[16,32]{1,0:T(8,128)(2,1)S(1)}, bf16[16,32]{1,0:T(8,128)(2,1)S(1)}, u32[]{:S(2)}, u32[]{:S(2)}) %collective-permute-start.1) | collective-permute-done | bytes 1056 | tf_op jit(solution)/shard_map/ppermute | solution.py:193
  18.2 2.0 %collective-permute-start.3 = (bf16[16,128]{1,0:T(8,128)(2,1)S(1)}, bf16[16,128]{1,0:T(8,128)(2,1)S(1)}, u32[]{:S(2)}, u32[]{:S(2)}) collective-permute-start(bf16[16,128]{1,0:T(8,128)(2,1)S(1)} %pad_maximum_fusion.refs_1_), channel_id=1, source_target_pairs={{0,1},{1,2},{2,3},{3,4},{4,5},{5,6},{6,7},{7,0},{8,9},{9,10},{10,1... | collective-permute-start | bytes 12296 | tf_op jit(solution)/shard_map/ppermute | solution.py:197
  20.2 1.5 %collective-permute-start.4 = (bf16[16,128]{1,0:T(8,128)(2,1)S(1)}, bf16[16,128]{1,0:T(8,128)(2,1)S(1)}, u32[]{:S(2)}, u32[]{:S(2)}) collective-permute-start(bf16[16,128]{1,0:T(8,128)(2,1)S(1)} %pad_maximum_fusion.refs_1_), channel_id=1, source_target_pairs={{0,2},{1,3},{2,4},{3,5},{4,6},{5,7},{6,0},{7,1},{8,10},{9,11},{10,... | collective-permute-start | bytes 12296 | tf_op jit(solution)/shard_map/ppermute | solution.py:197
  21.7 2.4 %collective-permute-start.5 = (bf16[16,128]{1,0:T(8,128)(2,1)S(1)}, bf16[16,128]{1,0:T(8,128)(2,1)S(1)}, u32[]{:S(2)}, u32[]{:S(2)}) collective-permute-start(bf16[16,128]{1,0:T(8,128)(2,1)S(1)} %pad_maximum_fusion.refs_1_), channel_id=1, source_target_pairs={{0,3},{1,4},{2,5},{3,6},{4,7},{5,0},{6,1},{7,2},{8,11},{9,12},{10,... | collective-permute-start | bytes 12296 | tf_op jit(solution)/shard_map/ppermute | solution.py:197
  24.0 1.5 %collective-permute-start.6 = (bf16[16,128]{1,0:T(8,128)(2,1)S(1)}, bf16[16,128]{1,0:T(8,128)(2,1)S(1)}, u32[]{:S(2)}, u32[]{:S(2)}) collective-permute-start(bf16[16,128]{1,0:T(8,128)(2,1)S(1)} %pad_maximum_fusion.refs_1_), channel_id=1, source_target_pairs={{0,4},{1,5},{2,6},{3,7},{4,0},{5,1},{6,2},{7,3},{8,12},{9,13},{10,... | collective-permute-start | bytes 12296 | tf_op jit(solution)/shard_map/ppermute | solution.py:197
  25.5 2.4 %collective-permute-start.7 = (bf16[16,128]{1,0:T(8,128)(2,1)S(1)}, bf16[16,128]{1,0:T(8,128)(2,1)S(1)}, u32[]{:S(2)}, u32[]{:S(2)}) collective-permute-start(bf16[16,128]{1,0:T(8,128)(2,1)S(1)} %pad_maximum_fusion.refs_1_), channel_id=1, source_target_pairs={{0,5},{1,6},{2,7},{3,0},{4,1},{5,2},{6,3},{7,4},{8,13},{9,14},{10,... | collective-permute-start | bytes 12296 | tf_op jit(solution)/shard_map/ppermute | solution.py:197
  27.8 7.9 %collective-permute-done.3.refs_2_ = bf16[16,128]{1,0:T(8,128)(2,1)S(1)} collective-permute-done((bf16[16,128]{1,0:T(8,128)(2,1)S(1)}, bf16[16,128]{1,0:T(8,128)(2,1)S(1)}, u32[]{:S(2)}, u32[]{:S(2)}) %collective-permute-start.3) | collective-permute-done | bytes 4128 | tf_op jit(solution)/shard_map/ppermute | solution.py:197
  36.5 4.2 %collective-permute-done.5.refs_4_ = bf16[16,128]{1,0:T(8,128)(2,1)S(1)} collective-permute-done((bf16[16,128]{1,0:T(8,128)(2,1)S(1)}, bf16[16,128]{1,0:T(8,128)(2,1)S(1)}, u32[]{:S(2)}, u32[]{:S(2)}) %collective-permute-start.5) | collective-permute-done | bytes 4128 | tf_op jit(solution)/shard_map/ppermute | solution.py:197
  41.9 2.6 %toeplitz.1 = (bf16[2,256,1024]{2,1,0:T(8,128)(2,1)}, bf16[2,256,1024]{2,1,0:T(8,128)(2,1)}) custom-call(s32[2]{0:T(128)} %pad_add_fusion.refs_0_, bf16[16,128]{1,0:T(8,128)(2,1)} %copy-done.2, bf16[16,128]{1,0:T(8,128)(2,1)} %copy-done.4, bf16[16,128]{1,0:T(8,128)(2,1)} %copy-done.5, bf16[16,128]{1,0:T(8,128)(2,1)} %copy-done.6, bf16[16,128]{1,0:T(8,128)(2,1)} %copy-done.7, ...), custom_call_target="tpu_custom_call" | custom-call | flops 2000000 | bytes 2000000 | tf_op jit(solution)/shard_map/toeplitz/pallas_call | solution.py:200
  45.5 4.3 %convolve.1 = bf16[8,256,256]{2,1,0:T(8,128)(2,1)} custom-call(bf16[8,256,256]{2,1,0:T(8,128)(2,1)} %copy-done.1, bf16[2,256,1024]{2,1,0:T(8,128)(2,1)} %get-tuple-element.11.causal_ref, bf16[2,256,1024]{2,1,0:T(8,128)(2,1)} %get-tuple-element.12.anti_ref), custom_call_target="tpu_custom_call" | custom-call | flops 1300000000 | bytes 2097152 | tf_op jit(solution)/shard_map/convolve/pallas_call | solution.py:230
  49.8 6.3 %all-to-all-start.1 = ((bf16[8,256,256]{2,1,0:T(8,128)(2,1)}), bf16[8,256,256]{2,1,0:T(8,128)(2,1)S(1)}, u32[]{:S(2)}, u32[]{:S(2)}) async-start(bf16[8,256,256]{2,1,0:T(8,128)(2,1)} %convolve.1), calls=%async_computation.1 | async-start | bytes 2097152 | tf_op jit(solution)/shard_map/all_to_all | solution.py:332
  56.1 3.1 %lag_sums.1 = f32[4,2,256]{2,1,0:T(2,128)} custom-call(bf16[8,256,256]{2,1,0:T(8,128)(2,1)} %copy-done.1), custom_call_target="tpu_custom_call" | custom-call | flops 600000000 | bytes 1048576 | tf_op jit(solution)/shard_map/lag_sums/pallas_call | solution.py:275
  59.9 1.5 %collective-permute-start.11 = (f32[2,256]{1,0:T(2,128)S(1)}, f32[2,256]{1,0:T(2,128)S(1)}, u32[]{:S(2)}, u32[]{:S(2)}) collective-permute-start(f32[2,256]{1,0:T(2,128)S(1)} %get-tuple-element.19), channel_id=1, source_target_pairs={{0,16},{8,24},{16,0},{24,8},{1,17},{9,25},{17,1},{25,9},{2,18},{10... | collective-permute-start | bytes 6152 | tf_op jit(solution)/shard_map/ppermute | solution.py:292
  61.6 1.9 %collective-permute-done.11 = f32[2,256]{1,0:T(2,128)S(1)} collective-permute-done((f32[2,256]{1,0:T(2,128)S(1)}, f32[2,256]{1,0:T(2,128)S(1)}, u32[]{:S(2)}, u32[]{:S(2)}) %collective-permute-start.11) | collective-permute-done | bytes 2080 | tf_op jit(solution)/shard_map/ppermute | solution.py:292
  65.1 2.0 %collective-permute-start.13 = (f32[2,256]{1,0:T(2,128)S(1)}, f32[2,256]{1,0:T(2,128)S(1)}, u32[]{:S(2)}, u32[]{:S(2)}) collective-permute-start(f32[2,256]{1,0:T(2,128)S(1)} %fusion.6), channel_id=1, source_target_pairs={{0,1},{1,0},{2,3},{3,2},{4,5},{5,4},{6,7},{7,6},{8,9},{9,8},{10,11... | collective-permute-start | bytes 6152 | tf_op jit(solution)/shard_map/ppermute | solution.py:295
  67.1 1.6 %collective-permute-done.13 = f32[2,256]{1,0:T(2,128)S(1)} collective-permute-done((f32[2,256]{1,0:T(2,128)S(1)}, f32[2,256]{1,0:T(2,128)S(1)}, u32[]{:S(2)}, u32[]{:S(2)}) %collective-permute-start.13) | collective-permute-done | bytes 2080 | tf_op jit(solution)/shard_map/ppermute | solution.py:295
  68.7 2.1 %collective-permute-start.14 = (f32[4,256]{1,0:T(4,128)S(1)}, f32[4,256]{1,0:T(4,128)S(1)}, u32[]{:S(2)}, u32[]{:S(2)}) collective-permute-start(f32[4,256]{1,0:T(4,128)S(1)} %maximum_select_fusion.1), channel_id=1, source_target_pairs={{0,2},{1,3},{2,0},{3,1},{4,6},{5,7},{6,4},{7,5},{8,10},{9,11},{10,... | collective-permute-start | bytes 12296 | tf_op jit(solution)/shard_map/ppermute | solution.py:295
  70.8 1.6 %collective-permute-done.14 = f32[4,256]{1,0:T(4,128)S(1)} collective-permute-done((f32[4,256]{1,0:T(4,128)S(1)}, f32[4,256]{1,0:T(4,128)S(1)}, u32[]{:S(2)}, u32[]{:S(2)}) %collective-permute-start.14) | collective-permute-done | bytes 4128 | tf_op jit(solution)/shard_map/ppermute | solution.py:295
  72.4 4.2 %collective-permute-start.15 = (f32[8,256]{1,0:T(8,128)S(1)}, f32[8,256]{1,0:T(8,128)S(1)}, u32[]{:S(2)}, u32[]{:S(2)}) collective-permute-start(f32[8,256]{1,0:T(8,128)S(1)} %maximum_select_fusion), channel_id=1, source_target_pairs={{0,4},{1,5},{2,6},{3,7},{4,0},{5,1},{6,2},{7,3},{8,12},{9,13},{10,... | collective-permute-start | bytes 24584 | tf_op jit(solution)/shard_map/ppermute | solution.py:295
  76.6 4.3 %collective-permute-done.15 = f32[8,256]{1,0:T(8,128)S(1)} collective-permute-done((f32[8,256]{1,0:T(8,128)S(1)}, f32[8,256]{1,0:T(8,128)S(1)}, u32[]{:S(2)}, u32[]{:S(2)}) %collective-permute-start.15) | collective-permute-done | bytes 8224 | tf_op jit(solution)/shard_map/ppermute | solution.py:295
  81.5 1.0 %copy-done = bf16[8,256,256]{2,1,0:T(8,128)(2,1)} copy-done((bf16[8,256,256]{2,1,0:T(8,128)(2,1)}, bf16[8,256,256]{2,1,0:T(8,128)(2,1)S(1)}, u32[]{:S(2)}) %copy-start) | copy-done | bytes 1048600
  82.5 5.9 %gate_outputs.1 = (bf16[1,128,2048]{2,1,0:T(8,128)(2,1)}, bf16[1,128,2048]{2,1,0:T(8,128)(2,1)}, bf16[1,128,2048]{2,1,0:T(8,128)(2,1)}, bf16[1,128,2048]{2,1,0:T(8,128)(2,1)}) custom-call(bf16[1,128,2048]{2,1,0:T(8,128)(2,1)} %pre_ref.3, bf16[1,128,2048]{2,1,0:T(8,128)(2,1)} %post_ref.3, bf16[1,128,2048]{2,1,0:T(8,128)(2,1)} %values_ref.3, ...), custom_call_target="tpu_custom_call" | custom-call | flops 1048576 | bytes 5242880 | tf_op jit(solution)/shard_map/gate_outputs/pallas_call | solution.py:316
  (46 shorter events, 8.6 us)
Async XLA Ops:
  6.1 7.4 %copy-start.3 = (bf16[32,16]{0,1:T(8,128)(2,1)S(1)}, bf16[32,16]{0,1:T(8,128)(2,1)}, u32[]{:S(2)}) copy-start(bf16[32,16]{0,1:T(8,128)(2,1)} %param.9) | copy-start | bytes 3076
  6.1 38.4 %all-to-all-start = ((bf16[8,256,256]{2,1,0:T(8,128)(2,1)}), bf16[8,256,256]{2,1,0:T(8,128)(2,1)S(1)}, u32[]{:S(2)}, u32[]{:S(2)}) async-start(bf16[8,256,256]{2,1,0:T(8,128)(2,1)} %gate_and_pack.1), calls=%async_computation | async-start | bytes 2097152 | tf_op jit(solution)/shard_map/all_to_all | solution.py:330
  13.5 2.0 %collective-permute-start.2 = (bf16[16,32]{1,0:T(8,128)(2,1)S(1)}, bf16[16,32]{1,0:T(8,128)(2,1)S(1)}, u32[]{:S(2)}, u32[]{:S(2)}) collective-permute-start(bf16[16,32]{1,0:T(8,128)(2,1)S(1)} %bitcast.17), channel_id=1, source_target_pairs={{0,24},{8,0},{16,8},{24,16},{1,25},{9,1},{17,9},{25,17},{2,26},{10... | collective-permute-start | bytes 3080 | tf_op jit(solution)/shard_map/ppermute | solution.py:193
  14.2 3.6 %collective-permute-start.1 = (bf16[16,32]{1,0:T(8,128)(2,1)S(1)}, bf16[16,32]{1,0:T(8,128)(2,1)S(1)}, u32[]{:S(2)}, u32[]{:S(2)}) collective-permute-start(bf16[16,32]{1,0:T(8,128)(2,1)S(1)} %bitcast.18), channel_id=1, source_target_pairs={{0,16},{8,24},{16,0},{24,8},{1,17},{9,25},{17,1},{25,9},{2,18},{10... | collective-permute-start | bytes 3080 | tf_op jit(solution)/shard_map/ppermute | solution.py:193
  15.1 3.0 %collective-permute-start = (bf16[16,32]{1,0:T(8,128)(2,1)S(1)}, bf16[16,32]{1,0:T(8,128)(2,1)S(1)}, u32[]{:S(2)}, u32[]{:S(2)}) collective-permute-start(bf16[16,32]{1,0:T(8,128)(2,1)S(1)} %bitcast.19), channel_id=1, source_target_pairs={{0,8},{8,16},{16,24},{24,0},{1,9},{9,17},{17,25},{25,1},{2,10},{10... | collective-permute-start | bytes 3080 | tf_op jit(solution)/shard_map/ppermute | solution.py:193
  18.2 17.5 %copy-start.2 = (bf16[16,128]{1,0:T(8,128)(2,1)}, bf16[16,128]{1,0:T(8,128)(2,1)S(1)}, u32[]{:S(2)}) copy-start(bf16[16,128]{1,0:T(8,128)(2,1)S(1)} %pad_maximum_fusion.refs_1_) | copy-start | bytes 12292
  18.2 17.5 %collective-permute-start.3 = (bf16[16,128]{1,0:T(8,128)(2,1)S(1)}, bf16[16,128]{1,0:T(8,128)(2,1)S(1)}, u32[]{:S(2)}, u32[]{:S(2)}) collective-permute-start(bf16[16,128]{1,0:T(8,128)(2,1)S(1)} %pad_maximum_fusion.refs_1_), channel_id=1, source_target_pairs={{0,1},{1,2},{2,3},{3,4},{4,5},{5,6},{6,7},{7,0},{8,9},{9,10},{10,1... | collective-permute-start | bytes 12296 | tf_op jit(solution)/shard_map/ppermute | solution.py:197
  20.2 15.6 %collective-permute-start.4 = (bf16[16,128]{1,0:T(8,128)(2,1)S(1)}, bf16[16,128]{1,0:T(8,128)(2,1)S(1)}, u32[]{:S(2)}, u32[]{:S(2)}) collective-permute-start(bf16[16,128]{1,0:T(8,128)(2,1)S(1)} %pad_maximum_fusion.refs_1_), channel_id=1, source_target_pairs={{0,2},{1,3},{2,4},{3,5},{4,6},{5,7},{6,0},{7,1},{8,10},{9,11},{10,... | collective-permute-start | bytes 12296 | tf_op jit(solution)/shard_map/ppermute | solution.py:197
  21.7 19.0 %collective-permute-start.5 = (bf16[16,128]{1,0:T(8,128)(2,1)S(1)}, bf16[16,128]{1,0:T(8,128)(2,1)S(1)}, u32[]{:S(2)}, u32[]{:S(2)}) collective-permute-start(bf16[16,128]{1,0:T(8,128)(2,1)S(1)} %pad_maximum_fusion.refs_1_), channel_id=1, source_target_pairs={{0,3},{1,4},{2,5},{3,6},{4,7},{5,0},{6,1},{7,2},{8,11},{9,12},{10,... | collective-permute-start | bytes 12296 | tf_op jit(solution)/shard_map/ppermute | solution.py:197
  24.0 16.7 %collective-permute-start.6 = (bf16[16,128]{1,0:T(8,128)(2,1)S(1)}, bf16[16,128]{1,0:T(8,128)(2,1)S(1)}, u32[]{:S(2)}, u32[]{:S(2)}) collective-permute-start(bf16[16,128]{1,0:T(8,128)(2,1)S(1)} %pad_maximum_fusion.refs_1_), channel_id=1, source_target_pairs={{0,4},{1,5},{2,6},{3,7},{4,0},{5,1},{6,2},{7,3},{8,12},{9,13},{10,... | collective-permute-start | bytes 12296 | tf_op jit(solution)/shard_map/ppermute | solution.py:197
  25.5 15.2 %collective-permute-start.7 = (bf16[16,128]{1,0:T(8,128)(2,1)S(1)}, bf16[16,128]{1,0:T(8,128)(2,1)S(1)}, u32[]{:S(2)}, u32[]{:S(2)}) collective-permute-start(bf16[16,128]{1,0:T(8,128)(2,1)S(1)} %pad_maximum_fusion.refs_1_), channel_id=1, source_target_pairs={{0,5},{1,6},{2,7},{3,0},{4,1},{5,2},{6,3},{7,4},{8,13},{9,14},{10,... | collective-permute-start | bytes 12296 | tf_op jit(solution)/shard_map/ppermute | solution.py:197
  35.8 5.0 %copy-start.4 = (bf16[16,128]{1,0:T(8,128)(2,1)}, bf16[16,128]{1,0:T(8,128)(2,1)S(1)}, u32[]{:S(2)}) copy-start(bf16[16,128]{1,0:T(8,128)(2,1)S(1)} %collective-permute-done.3.refs_2_) | copy-start | bytes 12292
  35.8 5.0 %collective-permute-start.8 = (bf16[16,128]{1,0:T(8,128)(2,1)S(1)}, bf16[16,128]{1,0:T(8,128)(2,1)S(1)}, u32[]{:S(2)}, u32[]{:S(2)}) collective-permute-start(bf16[16,128]{1,0:T(8,128)(2,1)S(1)} %pad_maximum_fusion.refs_1_), channel_id=1, source_target_pairs={{0,6},{1,7},{2,0},{3,1},{4,2},{5,3},{6,4},{7,5},{8,14},{9,15},{10,... | collective-permute-start | bytes 12296 | tf_op jit(solution)/shard_map/ppermute | solution.py:197
  35.8 5.0 %copy-start.5 = (bf16[16,128]{1,0:T(8,128)(2,1)}, bf16[16,128]{1,0:T(8,128)(2,1)S(1)}, u32[]{:S(2)}) copy-start(bf16[16,128]{1,0:T(8,128)(2,1)S(1)} %collective-permute-done.4.refs_3_) | copy-start | bytes 12292
  35.8 4.9 %collective-permute-start.9 = (bf16[16,128]{1,0:T(8,128)(2,1)S(1)}, bf16[16,128]{1,0:T(8,128)(2,1)S(1)}, u32[]{:S(2)}, u32[]{:S(2)}) collective-permute-start(bf16[16,128]{1,0:T(8,128)(2,1)S(1)} %pad_maximum_fusion.refs_1_), channel_id=1, source_target_pairs={{0,7},{1,0},{2,1},{3,2},{4,3},{5,4},{6,5},{7,6},{8,15},{9,8},{10,9... | collective-permute-start | bytes 12296 | tf_op jit(solution)/shard_map/ppermute | solution.py:197
  44.5 1.0 %copy-start.1 = (bf16[8,256,256]{2,1,0:T(8,128)(2,1)}, bf16[8,256,256]{2,1,0:T(8,128)(2,1)S(1)}, u32[]{:S(2)}) copy-start(bf16[8,256,256]{2,1,0:T(8,128)(2,1)S(1)} %all-to-all-done.slabs_ref) | copy-start | bytes 3145732
  49.8 31.7 %all-to-all-start.1 = ((bf16[8,256,256]{2,1,0:T(8,128)(2,1)}), bf16[8,256,256]{2,1,0:T(8,128)(2,1)S(1)}, u32[]{:S(2)}, u32[]{:S(2)}) async-start(bf16[8,256,256]{2,1,0:T(8,128)(2,1)} %convolve.1), calls=%async_computation.1 | async-start | bytes 2097152 | tf_op jit(solution)/shard_map/all_to_all | solution.py:332
  59.9 1.7 %collective-permute-start.12 = (f32[2,256]{1,0:T(2,128)S(1)}, f32[2,256]{1,0:T(2,128)S(1)}, u32[]{:S(2)}, u32[]{:S(2)}) collective-permute-start(f32[2,256]{1,0:T(2,128)S(1)} %get-tuple-element.18), channel_id=1, source_target_pairs={{0,24},{8,0},{16,8},{24,16},{1,25},{9,1},{17,9},{25,17},{2,26},{10... | collective-permute-start | bytes 6152 | tf_op jit(solution)/shard_map/ppermute | solution.py:292
  59.9 3.6 %collective-permute-start.11 = (f32[2,256]{1,0:T(2,128)S(1)}, f32[2,256]{1,0:T(2,128)S(1)}, u32[]{:S(2)}, u32[]{:S(2)}) collective-permute-start(f32[2,256]{1,0:T(2,128)S(1)} %get-tuple-element.19), channel_id=1, source_target_pairs={{0,16},{8,24},{16,0},{24,8},{1,17},{9,25},{17,1},{25,9},{2,18},{10... | collective-permute-start | bytes 6152 | tf_op jit(solution)/shard_map/ppermute | solution.py:292
  61.4 3.0 %collective-permute-start.10 = (f32[2,256]{1,0:T(2,128)S(1)}, f32[2,256]{1,0:T(2,128)S(1)}, u32[]{:S(2)}, u32[]{:S(2)}) collective-permute-start(f32[2,256]{1,0:T(2,128)S(1)} %get-tuple-element.17), channel_id=1, source_target_pairs={{0,8},{8,16},{16,24},{24,0},{1,9},{9,17},{17,25},{25,1},{2,10},{10... | collective-permute-start | bytes 6152 | tf_op jit(solution)/shard_map/ppermute | solution.py:292
  65.1 3.6 %collective-permute-start.13 = (f32[2,256]{1,0:T(2,128)S(1)}, f32[2,256]{1,0:T(2,128)S(1)}, u32[]{:S(2)}, u32[]{:S(2)}) collective-permute-start(f32[2,256]{1,0:T(2,128)S(1)} %fusion.6), channel_id=1, source_target_pairs={{0,1},{1,0},{2,3},{3,2},{4,5},{5,4},{6,7},{7,6},{8,9},{9,8},{10,11... | collective-permute-start | bytes 6152 | tf_op jit(solution)/shard_map/ppermute | solution.py:295
  68.7 3.7 %collective-permute-start.14 = (f32[4,256]{1,0:T(4,128)S(1)}, f32[4,256]{1,0:T(4,128)S(1)}, u32[]{:S(2)}, u32[]{:S(2)}) collective-permute-start(f32[4,256]{1,0:T(4,128)S(1)} %maximum_select_fusion.1), channel_id=1, source_target_pairs={{0,2},{1,3},{2,0},{3,1},{4,6},{5,7},{6,4},{7,5},{8,10},{9,11},{10,... | collective-permute-start | bytes 12296 | tf_op jit(solution)/shard_map/ppermute | solution.py:295
  72.4 8.4 %collective-permute-start.15 = (f32[8,256]{1,0:T(8,128)S(1)}, f32[8,256]{1,0:T(8,128)S(1)}, u32[]{:S(2)}, u32[]{:S(2)}) collective-permute-start(f32[8,256]{1,0:T(8,128)S(1)} %maximum_select_fusion), channel_id=1, source_target_pairs={{0,4},{1,5},{2,6},{3,7},{4,0},{5,1},{6,2},{7,3},{8,12},{9,13},{10,... | collective-permute-start | bytes 24584 | tf_op jit(solution)/shard_map/ppermute | solution.py:295
  81.5 1.0 %copy-start = (bf16[8,256,256]{2,1,0:T(8,128)(2,1)}, bf16[8,256,256]{2,1,0:T(8,128)(2,1)S(1)}, u32[]{:S(2)}) copy-start(bf16[8,256,256]{2,1,0:T(8,128)(2,1)S(1)} %all-to-all-done.1.back_ref) | copy-start | bytes 3145732
  (5 other events, 3.0 us)

commit v2 on v0

--- a/solution.py
+++ b/solution.py
@@ -2,6 +2,8 @@
 import jax.numpy as jnp
 import numpy as np
 from jax import lax
+from jax.experimental import pallas as pl
+from jax.experimental.pallas import tpu as pltpu
 from jax.sharding import PartitionSpec as P
 
 K = 1024
@@ -117,9 +119,387 @@
     return (output[None], grad_pre[None], grad_post[None], grad_values[None], grad_filters)
 
 
+BLOCK = 128
+
+
+def swap_fits(pre_gate, post_gate, values, cotangent, filters):
+    parts, dp_count = lax.axis_size("seq"), lax.axis_size("dp")
+    channels, groups = pre_gate.shape[2], filters.shape[1]
+    return (
+        parts >= 4
+        and parts & (parts - 1) == 0
+        and groups % parts == 0
+        and channels // groups == BLOCK
+        and pre_gate.shape[0] == 1
+        and pre_gate.shape[1] == BLOCK
+        and parts * BLOCK == K
+        and filters.shape[0] * parts * dp_count == K
+    )
+
+
+def swap(chunk, flip):
+    count = lax.axis_size("seq")
+    return lax.ppermute(chunk, "seq", [(i, i ^ flip) for i in range(count)])
+
+
+def vmem_specs(count):
+    return [pl.BlockSpec(memory_space=pltpu.VMEM)] * count
+
+
+def chunk_shapes(count, width, blocks=1):
+    return [jax.ShapeDtypeStruct((blocks * BLOCK, width), jnp.bfloat16)] * count
+
+
+def call(kernel, name, place, operands, out_shape, scratch=(), flops=1000, nbytes=1000, after=()):
+    def body(place_ref, *refs):
+        kernel(place_ref, *refs[: len(operands)], *refs[len(operands) + len(after) :])
+
+    return pl.pallas_call(
+        body,
+        in_specs=[pl.BlockSpec(memory_space=pltpu.SMEM)]
+        + vmem_specs(len(operands))
+        + [pl.BlockSpec(memory_space=pl.ANY)] * len(after),
+        out_specs=vmem_specs(len(out_shape)),
+        out_shape=out_shape,
+        scratch_shapes=list(scratch),
+        compiler_params=pltpu.CompilerParams(vmem_limit_bytes=20 * 1024 * 1024),
+        cost_estimate=pl.CostEstimate(flops=flops, bytes_accessed=nbytes, transcendentals=0),
+        name=name,
+    )(place, *operands, *after)
+
+
+TAIL = 16
+
+
+def pack_kernel(quarters, pieces, place_ref, *refs):
+    f32, bf16 = jnp.float32, jnp.bfloat16
+    taps_in, (a_ref, b_ref), refs = refs[:pieces], refs[pieces : pieces + 2], refs[pieces + 2 :]
+    a_outs, outs, (taps_ref,) = refs[:quarters], refs[quarters : 2 * quarters], refs[2 * quarters :]
+    quarter = place_ref[1]
+    width = a_outs[0].shape[1]
+    local = taps_ref.shape[1]
+    taps = jnp.concatenate([piece[...].astype(f32) for piece in taps_in], axis=1)
+    for i in range(quarters):
+        taps_ref[i] = taps[i * local : (i + 1) * local]
+    for j in range(quarters):
+        columns = pl.ds(pl.multiple_of((quarter ^ j) * width, width), width)
+        a = a_ref[:, columns]
+        a_outs[j][...] = a
+        outs[j][:BLOCK] = a
+        outs[j][BLOCK : 2 * BLOCK] = b_ref[:, columns]
+        outs[j][2 * BLOCK :] = jnp.zeros((TAIL, width), bf16)
+        taps = taps_ref[quarter ^ j]
+        taps = jnp.concatenate([taps, jnp.zeros((TAIL - local, BLOCK), f32)], axis=0)
+        outs[j][2 * BLOCK :, :BLOCK] = taps.astype(bf16)
+
+
+def bands(quarters, dp_count, place_ref, taps_in, taps_ref, causal_ref, anti_ref):
+    half, quarter, dp_index = place_ref[0], place_ref[1], place_ref[2]
+    local, rows = taps_ref.shape[1:]
+    for u in range(2):
+        piece = taps_in[u][...].astype(jnp.float32)
+        for j in range(quarters):
+            for p in range(dp_count):
+                owner = lax.rem(dp_index + dp_count - p, dp_count) * 2 * quarters + (half ^ u) * quarters + (quarter ^ j)
+                start = j * BLOCK + p * rows
+                taps_ref[owner] = piece[:local, start : start + rows]
+    for g in range(local):
+        line = jnp.concatenate([taps_ref[o, g : g + 1] for o in range(taps_ref.shape[0])], axis=1)
+        line = jnp.concatenate([line, jnp.zeros((1, 2 * BLOCK), jnp.float32)], axis=1)
+        spread = jnp.broadcast_to(line, (2 * BLOCK, K + 2 * BLOCK))
+        shear = pltpu.roll(spread, 0, 1, stride=1, stride_axis=0)
+        anti_ref[g] = shear[:, :K].astype(jnp.bfloat16)
+        count = K // BLOCK
+        turned = [shear[:BLOCK, m * BLOCK : (m + 1) * BLOCK].T.astype(jnp.bfloat16) for m in range(count)]
+        turned.append(jnp.zeros((BLOCK, BLOCK), jnp.bfloat16))
+        for b in range(count):
+            causal_ref[g, :BLOCK, b * BLOCK : (b + 1) * BLOCK] = turned[count - 2 - b]
+            causal_ref[g, BLOCK:, b * BLOCK : (b + 1) * BLOCK] = turned[count - 1 - b]
+
+
+def in_order(scratch_ref, quarter, chunks):
+    for j, chunk in enumerate(chunks):
+        scratch_ref[quarter ^ j] = chunk[...]
+
+
+def rows_of(ref, lanes):
+    return ref[:, :, lanes].reshape(ref.shape[0] * BLOCK, BLOCK)
+
+
+def dot(left, right):
+    return jnp.dot(left, right, preferred_element_type=jnp.float32)
+
+
+def causal_part(band, data, p):
+    reach = (p + 1) * 2 * BLOCK
+    return dot(band[:, K - reach :], data[:reach])
+
+
+def anti_part(band, data, p):
+    return dot(band[:, : data.shape[0] - p * 2 * BLOCK], data[p * 2 * BLOCK :])
+
+
+def lag_lines(mixed, gated, first, turn):
+    count = mixed.shape[0] // BLOCK
+    blocks = K // BLOCK
+    turned = jnp.concatenate(
+        [dot(turn, mixed[j * BLOCK : (j + 1) * BLOCK]).astype(jnp.bfloat16) for j in range(count)], axis=0
+    )
+    sums = [None] * blocks
+    for i in range(count):
+        top = min(count, first + i + 1)
+        product = lax.dot_general(
+            turned[: top * BLOCK],
+            gated[i * BLOCK : (i + 1) * BLOCK],
+            (((1,), (1,)), ((), ())),
+            preferred_element_type=jnp.float32,
+        )
+        for j in range(top):
+            term = product[j * BLOCK : (j + 1) * BLOCK]
+            lag = first + i - j
+            sums[lag] = term if sums[lag] is None else sums[lag] + term
+    last = max(m for m in range(blocks) if sums[m] is not None)
+    zero = jnp.zeros((BLOCK, BLOCK), jnp.float32)
+    table = jnp.concatenate([zero if t is None else t for t in sums[: last + 1]] + [zero], axis=1)
+    span = (last + 2) * BLOCK
+    shear = jnp.sum(pltpu.roll(table, 0, 1, stride=1, stride_axis=0), axis=0, keepdims=True)
+    if span < K:
+        shear = jnp.concatenate([shear, jnp.zeros((1, K + BLOCK - span), jnp.float32)], axis=1)
+    return pltpu.roll(shear, K + BLOCK - (BLOCK - 1), 1)[:, :K]
+
+
+def exchange():
+    rows = lax.broadcasted_iota(jnp.int32, (BLOCK, BLOCK), 0)
+    columns = lax.broadcasted_iota(jnp.int32, (BLOCK, BLOCK), 1)
+    return jnp.where(rows + columns == BLOCK - 1, 1.0, 0.0).astype(jnp.bfloat16)
+
+
+def local_kernel(quarters, dp_count, place_ref, *refs):
+    taps_in, refs = refs[:2], refs[2:]
+    ab_in, a_out = refs[:quarters], refs[quarters : 2 * quarters]
+    causal_ref, anti_ref, sums_ref, lines_ref, a_ref, b_ref, done_ref, taps_ref = refs[2 * quarters :]
+    bands(quarters, dp_count, place_ref, taps_in, taps_ref, causal_ref, anti_ref)
+    half, quarter = place_ref[0], place_ref[1]
+    in_order(a_ref, quarter, [ab.at[:BLOCK] for ab in ab_in])
+    in_order(b_ref, quarter, [ab.at[BLOCK : 2 * BLOCK] for ab in ab_in])
+    turn = exchange()
+
+    def work(a_band, a_part, b_band, b_part, a_mixed):
+        for g in range(causal_ref.shape[0]):
+            lanes = slice(g * BLOCK, (g + 1) * BLOCK)
+            a_rows, b_rows = rows_of(a_ref, lanes), rows_of(b_ref, lanes)
+            for p in range(quarters // 2):
+                pair = slice(2 * p, 2 * p + 2)
+                a_sum = a_part(a_band.at[g], a_rows, p).reshape(2, BLOCK, BLOCK)
+                done_ref[pair, :, lanes] = a_sum.astype(jnp.bfloat16)
+                sums_ref[pair, :, lanes] = b_part(b_band.at[g], b_rows, p).reshape(2, BLOCK, BLOCK)
+            mixed, gated = (a_rows, b_rows) if a_mixed else (b_rows, a_rows)
+            lines_ref[g : g + 1] = lag_lines(mixed, gated, 0, turn)
+
+    @pl.when(half == 0)
+    def lower():
+        work(causal_ref, causal_part, anti_ref, anti_part, True)
+
+    @pl.when(half != 0)
+    def upper():
+        work(anti_ref, anti_part, causal_ref, causal_part, False)
+
+    for j in range(quarters):
+        a_out[j][...] = done_ref[quarter ^ j]
+
+
+def lag_kernel(quarters, place_ref, *refs):
+    a_in, r_in = refs[:quarters], refs[quarters : 2 * quarters]
+    lines_ref, out_ref, mixed_ref, gated_ref, total_ref = refs[2 * quarters :]
+    half, quarter = place_ref[0], place_ref[1]
+    width = mixed_ref.shape[2]
+    count = width // BLOCK
+    turn = exchange()
+
+    def gather(mixed, gated, lanes):
+        for j in range(quarters):
+            mixed_ref[quarter ^ j] = mixed[j][:BLOCK, lanes]
+            gated_ref[quarter ^ j] = gated[j][:BLOCK, lanes]
+
+    @pl.when(half == 0)
+    def lower():
+        gather(a_in, r_in, slice(0, width))
+
+    @pl.when(half != 0)
+    def upper():
+        gather(r_in, a_in, slice(width, 2 * width))
+
+    total_ref[...] = lines_ref[...]
+    cross = []
+    for g in range(count):
+        lanes = slice(g * BLOCK, (g + 1) * BLOCK)
+        cross.append(lag_lines(rows_of(mixed_ref, lanes), rows_of(gated_ref, lanes), quarters, turn))
+    cross = jnp.concatenate(cross, axis=0)
+
+    @pl.when(half == 0)
+    def add_lower():
+        total_ref[:count] += cross
+
+    @pl.when(half != 0)
+    def add_upper():
+        total_ref[count:] += cross
+
+    owners, step = out_ref.shape[0], K // out_ref.shape[0]
+    for o in range(owners):
+        start = o * step // BLOCK * BLOCK
+        out_ref[o] = total_ref[:, start : start + BLOCK]
+
+
+def cross_kernel(quarters, place_ref, *refs):
+    ab_in, r_in = refs[:quarters], refs[quarters : 2 * quarters]
+    lines_ref, sums_ref, causal_ref, anti_ref, shares_ref = refs[2 * quarters : 2 * quarters + 5]
+    b_out = refs[2 * quarters + 5 : 3 * quarters + 5]
+    r_ref, done_ref, mixed_ref, gated_ref, total_ref = refs[3 * quarters + 5 :]
+    lag_kernel(quarters, place_ref, *ab_in, *r_in, lines_ref, shares_ref, mixed_ref, gated_ref, total_ref)
+    half, quarter = place_ref[0], place_ref[1]
+    in_order(r_ref, quarter, r_in)
+    length = quarters * BLOCK
+
+    def work(band, first):
+        for g in range(causal_ref.shape[0]):
+            lanes = slice(g * BLOCK, (g + 1) * BLOCK)
+            rows = rows_of(r_ref, lanes)
+            for p in range(quarters // 2):
+                pair = slice(2 * p, 2 * p + 2)
+                start = first(p * 2 * BLOCK)
+                part = dot(band[g, :, start : start + length], rows).reshape(2, BLOCK, BLOCK)
+                done_ref[pair, :, lanes] = (sums_ref[pair, :, lanes] + part).astype(jnp.bfloat16)
+
+    @pl.when(half == 0)
+    def lower():
+        work(anti_ref, lambda row: length - row)
+
+    @pl.when(half != 0)
+    def upper():
+        work(causal_ref, lambda row: K - length - row - 2 * BLOCK)
+
+    for j in range(quarters):
+        b_out[j][...] = done_ref[quarter ^ j]
+
+
+def outputs_kernel(quarters, place_ref, *refs):
+    f32, bf16 = jnp.float32, jnp.bfloat16
+    a_in, b_in, refs = refs[:quarters], refs[quarters : 2 * quarters], refs[2 * quarters :]
+    inputs, outputs, stores, results, (in_sem, out_sem) = refs[:4], refs[4:8], refs[8:12], refs[12:16], refs[16:]
+    half, quarter = place_ref[0], place_ref[1]
+    width = a_in[0].shape[1]
+
+    def copies(j, out):
+        columns = pl.ds(pl.multiple_of((quarter ^ j) * width, width), width)
+        if out:
+            return [
+                pltpu.make_async_copy(store.at[j], target.at[0, :, columns], out_sem.at[j, i])
+                for i, (store, target) in enumerate(zip(results, outputs))
+            ]
+        return [
+            pltpu.make_async_copy(source.at[0, :, columns], store.at[j], in_sem.at[j, i])
+            for i, (source, store) in enumerate(zip(inputs, stores))
+        ]
+
+    for j in range(quarters):
+        for copy in copies(j, False):
+            copy.start()
+    for j in range(quarters):
+        for copy in copies(j, False):
+            copy.wait()
+        pre, post, values, cot = [store[j].astype(f32) for store in stores]
+        a_sum, b_sum = a_in[j][...].astype(f32), b_in[j][...].astype(f32)
+        convolved, carried = jnp.where(half == 0, a_sum, b_sum), jnp.where(half == 0, b_sum, a_sum)
+        for result, value in zip(results, (post * convolved, carried * values, cot * convolved, carried * pre)):
+            result[j] = value.astype(bf16)
+        for copy in copies(j, True):
+            copy.start()
+    for j in range(quarters):
+        for copy in copies(j, True):
+            copy.wait()
+
+
+def swapped(pre_gate, post_gate, values, cotangent, filters):
+    parts, dp_count = lax.axis_size("seq"), lax.axis_size("dp")
+    quarters = parts // 2
+    channels, groups = pre_gate.shape[2], filters.shape[1]
+    width, local = channels // quarters, groups // quarters
+    seq_index = lax.axis_index("seq")
+    place = jnp.stack([seq_index // quarters, seq_index % quarters, lax.axis_index("dp")]).astype(jnp.int32)
+    owners = parts * dp_count
+    rows = filters.shape[0]
+    f32, bf16 = jnp.float32, jnp.bfloat16
+    every = ("dp", "seq")
+
+    taps = filters.T
+    pieces = [taps]
+    for p in range(1, dp_count):
+        pieces.append(lax.ppermute(taps, "dp", [(i, (i + p) % dp_count) for i in range(dp_count)]))
+
+    gates = [pre_gate, post_gate, values, cotangent]
+    lower = seq_index < quarters
+    mixed = (pre_gate[0].astype(f32) * values[0]).astype(bf16)
+    gated = (cotangent[0].astype(f32) * post_gate[0]).astype(bf16)
+    a, b = jnp.where(lower, mixed, gated), jnp.where(lower, gated, mixed)
+    store = pltpu.VMEM((quarters, BLOCK, width), bf16)
+    message = jax.ShapeDtypeStruct((2 * BLOCK + TAIL, width), bf16)
+    chunks = call(
+        lambda *refs: pack_kernel(quarters, dp_count, *refs), "pack", place, pieces + [a, b],
+        chunk_shapes(quarters, width) + [message] * quarters, [pltpu.VMEM((quarters, local, BLOCK), f32)],
+        flops=1000, nbytes=1000,
+    )
+    a_own, ab_own = chunks[:quarters], chunks[quarters:]
+    r_in = [swap(a_own[j], quarters + j) for j in range(quarters)]
+    ab_in = [ab_own[0]] + [swap(ab_own[j], j) for j in range(1, quarters)]
+
+    taps = jnp.concatenate([message[2 * BLOCK :, :BLOCK] for message in ab_in], axis=1)
+    taps = [taps, swap(taps, quarters)]
+    whole = (quarters, BLOCK, width)
+    band = jax.ShapeDtypeStruct((local, 2 * BLOCK, K), bf16)
+    *a_done, causal, anti, sums, lines = call(
+        lambda *refs: local_kernel(quarters, dp_count, *refs), "local", place, taps + ab_in,
+        chunk_shapes(quarters, width)
+        + [band, band, jax.ShapeDtypeStruct(whole, f32), jax.ShapeDtypeStruct((local, K), f32)],
+        [store] * 3 + [pltpu.VMEM((owners, local, rows), f32)], flops=1000, nbytes=1000,
+        after=r_in[2:3],
+    )
+    a_back = [a_done[0]] + [swap(a_done[j], j) for j in range(1, quarters)]
+
+    half_store = pltpu.VMEM((quarters, BLOCK, width // 2), bf16)
+    shares, *b_done = call(
+        lambda *refs: cross_kernel(quarters, *refs), "cross", place, ab_in + r_in + [lines, sums, causal, anti],
+        [jax.ShapeDtypeStruct((owners, local, BLOCK), f32)] + chunk_shapes(quarters, width),
+        [store] * 2 + [half_store] * 2 + [pltpu.VMEM((local, K), f32)], flops=1000, nbytes=1000,
+        after=a_back[1:],
+    )
+    arrived = lax.all_to_all(shares, every, 0, 0, tiled=True)
+    b_back = [b_done[0]] + [swap(b_done[j], j) for j in range(1, quarters)]
+
+    shape = jax.ShapeDtypeStruct(pre_gate.shape, bf16)
+    hbm = [pl.BlockSpec(memory_space=pltpu.HBM)] * 4
+    output, grad_pre, grad_post, grad_values = pl.pallas_call(
+        lambda *refs: outputs_kernel(quarters, *refs),
+        in_specs=[pl.BlockSpec(memory_space=pltpu.SMEM)] + vmem_specs(2 * quarters) + hbm,
+        out_specs=hbm,
+        out_shape=[shape] * 4,
+        scratch_shapes=[store] * 8 + [pltpu.SemaphoreType.DMA((quarters, 4))] * 2,
+        compiler_params=pltpu.CompilerParams(vmem_limit_bytes=20 * 1024 * 1024),
+        cost_estimate=pl.CostEstimate(flops=1000, bytes_accessed=1000, transcendentals=0),
+        name="outputs",
+    )(place, *a_back, *b_back, *gates)
+    total = jnp.sum(arrived.reshape(owners // quarters, groups, BLOCK), axis=0)
+    mine = lax.dynamic_slice_in_dim(total, (lax.axis_index(every) * rows) % BLOCK, rows, 1)
+    total_tokens = dp_count * parts * pre_gate.shape[1] * (channels // groups)
+    return output, grad_pre, grad_post, grad_values, mine.T / float(total_tokens**0.5)
+
+
 def solution(mesh):
+    def chosen(*shard):
+        fits = swap_fits(*shard)
+        return (swapped if fits else shards)(*shard)
+
     return jax.shard_map(
-        shards,
+        chosen,
         mesh=mesh,
         in_specs=(
             P("dp", "seq", None),

time: 991 us -> 69.2 us (0.07)
  local copies, waits for them, and re-layouts: 538 us -> 0.03 us
  waiting for transfers between devices: 278 us -> 26 us
  blocking collectives: 70.6 us -> 0 us
  matrix products: 28.3 us -> 0 us
  starting transfers between devices: 45.5 us -> 28.9 us
  between operations: 14.2 us -> 0.73 us
    gather x2 -> x0, local copies, waits for them, and re-layouts: 483 us -> none  [build_tiles(): return columns[:, tile_index(lag_blocks, shard_len)]]
    unnamed x2 -> x0, waiting for transfers between devices: 132 us -> none
    ppermute x14 -> x17, waiting for transfers between devices: 146 us -> 22.2 us  [the longest x14 21.1 us: swap(): return lax.ppermute(chunk, 'seq', [(i, i ^ flip) for i in range(count)])]
    all_gather x1 -> x0, blocking collectives: 70.6 us -> none  [shards(): all_taps = lax.all_gather(filters, ('dp', 'seq'), axis=0, tiled=True)]
    dot_general x18 -> x0, matrix products: 28.3 us -> none  [the longest x16 18.9 us: one_group(): lax.dot_general(gated_one, hist_one, (((1,), (1,)), ((), ())), preferred_...]
    ppermute x14 -> x17, starting transfers between devices: 45.5 us -> 25.1 us  [the longest x14 21.9 us: swap(): return lax.ppermute(chunk, 'seq', [(i, i ^ flip) for i in range(count)])]
    reshape x35 -> x0, local copies, waits for them, and re-layouts: 16.9 us -> none  [the longest x16 9.07 us: one_group(): skewed = flat_line.reshape(row_count, span_len + 2 * row_count + 1)]
    dynamic_update_slice x37 -> x0, local copies, waits for them, and re-layouts: 14.8 us -> none  [the longest x21 13.7 us: earlier_relay(): lax.scan(earlier_advance, piece_in, None, length=history_len)]
  transfers between devices with their start and end apart: 15 -> 18, of which waited for: 15 -> 11; matrix products, arithmetic and copies ran while one was open for 1% -> 5% of each run, Pallas kernels for 0% -> 5%
where the time goes in v2:
time: 69.2 us; the launch traced here: 69 us
  starting transfers between devices  28.9 us (42%)
  waiting for transfers between devices  26 us (38%)
  Pallas kernels  9.8 us (14%)
  other arithmetic  3.51 us (5%)
  between operations  0.73 us (1%)
    ppermute x14, starting transfers between devices, swap(): return lax.ppermute(chunk, 'seq', [(i, i ^ flip) for i in range(count)])  21.9 us
    ppermute x14, waiting for transfers between devices, swap(): return lax.ppermute(chunk, 'seq', [(i, i ^ flip) for i in range(count)])  21.1 us
    pallas_call x3, Pallas kernels, call(): pl.pallas_call(body, in_specs=[pl.BlockSpec(memory_space=pltpu.SMEM)] + v...  7.29 us
    all_to_all x1, starting transfers between devices, swapped(): arrived = lax.all_to_all(shares, every, 0, 0, tiled=True)  3.8 us
    all_to_all x1, waiting for transfers between devices, swapped(): arrived = lax.all_to_all(shares, every, 0, 0, tiled=True)  3.79 us
    ppermute x3, starting transfers between devices, swapped(): lax.ppermute(taps, 'dp', [(i, (i + p) % dp_count) for i in range(dp_count)])  3.23 us
    pallas_call x1, Pallas kernels, swapped(): pl.pallas_call(lambda *refs: outputs_kernel(quarters, *refs), in_specs=[p...  2.51 us
    select_n x1, other arithmetic, swapped(): a, b = (jnp.where(lower, mixed, gated), jnp.where(lower, gated, mixed))  1.9 us
  transfers between devices with their start and end apart: 18, of which 11 were waited for; matrix products, arithmetic and copies ran while one was open for 5% of the time, Pallas kernels for 5%

profile of v2, /device:TPU:0, one launch (start us, length us, event | category | flops | bytes accessed | tf_op | source)
XLA Modules:
  0.0 69.0 jit_solution(16106803447578106871)
XLA Ops:
  0.6 2.4 %collective-permute-start.2 = (bf16[16,32]{1,0:T(8,128)(2,1)}, bf16[16,32]{1,0:T(8,128)(2,1)S(1)}, u32[]{:S(2)}, u32[]{:S(2)}) collective-permute-start(bf16[16,32]{1,0:T(8,128)(2,1)} %bitcast.13), channel_id=1, source_target_pairs={{0,24},{8,0},{16,8},{24,16},{1,25},{9,1},{17,9},{25,17},{2,26},{10... | collective-permute-start | bytes 3080 | tf_op jit(solution)/shard_map/ppermute | solution.py:437
  3.9 1.9 %select_bitcast_fusion = (bf16[128,2048]{1,0:T(8,128)(2,1)S(1)}, bf16[128,2048]{1,0:T(8,128)(2,1)S(1)}) fusion(pred[]{:T(512)S(6)} %lt.17, bf16[1,128,2048]{2,1,0:T(8,128)(2,1)} %refs_11_.1, bf16[1,128,2048]{2,1,0:T(8,128)(2,1)} %refs_9_.1, bf16[1,128,2048]{2,1,0:T(8,128)(2,1)} %refs_10_.1, bf16[1,128,2048]{2,1,0:T(8,128)(2,1)} %refs_12_.1), kind=kLoop, calls=%fused_computation.2 | loop fusion | flops 2621440 | bytes 3145729 | tf_op jit(solution)/shard_map/jit(_where)/select_n | solution.py:443
  5.9 1.0 %collective-permute-done.1.refs_2_ = bf16[16,32]{1,0:T(8,128)(2,1)S(1)} collective-permute-done((bf16[16,32]{1,0:T(8,128)(2,1)}, bf16[16,32]{1,0:T(8,128)(2,1)S(1)}, u32[]{:S(2)}, u32[]{:S(2)}) %collective-permute-start.1) | collective-permute-done | bytes 1056 | tf_op jit(solution)/shard_map/ppermute | solution.py:437
  7.6 1.6 %collective-permute-start.3 = (bf16[272,512]{1,0:T(8,128)(2,1)S(1)}, bf16[272,512]{1,0:T(8,128)(2,1)S(1)}, u32[]{:S(2)}, u32[]{:S(2)}) collective-permute-start(bf16[272,512]{1,0:T(8,128)(2,1)S(1)} %get-tuple-element.31), channel_id=1, source_target_pairs={{0,1},{1,0},{2,3},{3,2},{4,5},{5,4},{6,7},{7,6},{8,9},{9,8},{10,11... | collective-permute-start | bytes 835592 | tf_op jit(solution)/shard_map/ppermute | solution.py:142
  9.2 1.6 %collective-permute-start.4 = (bf16[272,512]{1,0:T(8,128)(2,1)S(1)}, bf16[272,512]{1,0:T(8,128)(2,1)S(1)}, u32[]{:S(2)}, u32[]{:S(2)}) collective-permute-start(bf16[272,512]{1,0:T(8,128)(2,1)S(1)} %get-tuple-element.32), channel_id=1, source_target_pairs={{0,2},{1,3},{2,0},{3,1},{4,6},{5,7},{6,4},{7,5},{8,10},{9,11},{10,... | collective-permute-start | bytes 835592 | tf_op jit(solution)/shard_map/ppermute | solution.py:142
  11.2 3.6 %collective-permute-start.7 = (bf16[128,512]{1,0:T(8,128)(2,1)S(1)}, bf16[128,512]{1,0:T(8,128)(2,1)S(1)}, u32[]{:S(2)}, u32[]{:S(2)}) collective-permute-start(bf16[128,512]{1,0:T(8,128)(2,1)S(1)} %get-tuple-element.34), channel_id=1, source_target_pairs={{0,6},{1,7},{2,4},{3,5},{4,2},{5,3},{6,0},{7,1},{8,14},{9,15},{10,... | collective-permute-start | bytes 393224 | tf_op jit(solution)/shard_map/ppermute | solution.py:142
  14.8 1.7 %collective-permute-done.3.refs_3_.refs_1_ = bf16[272,512]{1,0:T(8,128)(2,1)S(1)} collective-permute-done((bf16[272,512]{1,0:T(8,128)(2,1)S(1)}, bf16[272,512]{1,0:T(8,128)(2,1)S(1)}, u32[]{:S(2)}, u32[]{:S(2)}) %collective-permute-start.3) | collective-permute-done | bytes 278560 | tf_op jit(solution)/shard_map/ppermute | solution.py:142
  16.5 5.0 %collective-permute-done.4.refs_4_.refs_2_ = bf16[272,512]{1,0:T(8,128)(2,1)S(1)} collective-permute-done((bf16[272,512]{1,0:T(8,128)(2,1)S(1)}, bf16[272,512]{1,0:T(8,128)(2,1)S(1)}, u32[]{:S(2)}, u32[]{:S(2)}) %collective-permute-start.4) | collective-permute-done | bytes 278560 | tf_op jit(solution)/shard_map/ppermute | solution.py:142
  21.5 7.5 %collective-permute-done.5.refs_5_.refs_3_ = bf16[272,512]{1,0:T(8,128)(2,1)S(1)} collective-permute-done((bf16[272,512]{1,0:T(8,128)(2,1)S(1)}, bf16[272,512]{1,0:T(8,128)(2,1)S(1)}, u32[]{:S(2)}, u32[]{:S(2)}) %collective-permute-start.5) | collective-permute-done | bytes 278560 | tf_op jit(solution)/shard_map/ppermute | solution.py:142
  29.1 1.9 %collective-permute-start.6 = (bf16[16,512]{1,0:T(8,128)(2,1)S(1)}, bf16[16,512]{1,0:T(8,128)(2,1)S(1)}, u32[]{:S(2)}, u32[]{:S(2)}) collective-permute-start(bf16[16,512]{1,0:T(8,128)(2,1)S(1)} %pad_maximum_fusion.refs_0_), channel_id=1, source_target_pairs={{0,4},{1,5},{2,6},{3,7},{4,0},{5,1},{6,2},{7,3},{8,12},{9,13},{10,... | collective-permute-start | bytes 49160 | tf_op jit(solution)/shard_map/ppermute | solution.py:142
  31.0 1.9 %collective-permute-start.12 = (bf16[128,512]{1,0:T(8,128)(2,1)S(1)}, bf16[128,512]{1,0:T(8,128)(2,1)S(1)}, u32[]{:S(2)}, u32[]{:S(2)}) collective-permute-start(bf16[128,512]{1,0:T(8,128)(2,1)S(1)} %get-tuple-element.40), channel_id=1, source_target_pairs={{0,5},{1,4},{2,7},{3,6},{4,1},{5,0},{6,3},{7,2},{8,13},{9,12},{10,... | collective-permute-start | bytes 393224 | tf_op jit(solution)/shard_map/ppermute | solution.py:142
  33.0 3.7 %collective-permute-start.13 = (bf16[128,512]{1,0:T(8,128)(2,1)S(1)}, bf16[128,512]{1,0:T(8,128)(2,1)S(1)}, u32[]{:S(2)}, u32[]{:S(2)}) collective-permute-start(bf16[128,512]{1,0:T(8,128)(2,1)S(1)} %get-tuple-element.41), channel_id=1, source_target_pairs={{0,7},{1,6},{2,5},{3,4},{4,3},{5,2},{6,1},{7,0},{8,15},{9,14},{10,... | collective-permute-start | bytes 393224 | tf_op jit(solution)/shard_map/ppermute | solution.py:142
  36.7 3.8 %local.1 = (bf16[128,512]{1,0:T(8,128)(2,1)S(1)}, bf16[128,512]{1,0:T(8,128)(2,1)S(1)}, bf16[128,512]{1,0:T(8,128)(2,1)S(1)}, bf16[128,512]{1,0:T(8,128)(2,1)S(1...) custom-call(s32[3]{0:T(128)S(1)} %pad_add_fusion.place_ref.refs_0_, ...), custom_call_target="tpu_custom_call" | custom-call | flops 1000 | bytes 1000 | tf_op jit(solution)/shard_map/local/pallas_call | solution.py:157
  40.5 1.6 %collective-permute-start.8 = (bf16[128,512]{1,0:T(8,128)(2,1)S(1)}, bf16[128,512]{1,0:T(8,128)(2,1)S(1)}, u32[]{:S(2)}, u32[]{:S(2)}) collective-permute-start(bf16[128,512]{1,0:T(8,128)(2,1)S(1)} %get-tuple-element.36), channel_id=1, source_target_pairs={{0,1},{1,0},{2,3},{3,2},{4,5},{5,4},{6,7},{7,6},{8,9},{9,8},{10,11... | collective-permute-start | bytes 393224 | tf_op jit(solution)/shard_map/ppermute | solution.py:142
  42.1 2.0 %collective-permute-start.10 = (bf16[128,512]{1,0:T(8,128)(2,1)S(1)}, bf16[128,512]{1,0:T(8,128)(2,1)S(1)}, u32[]{:S(2)}, u32[]{:S(2)}) collective-permute-start(bf16[128,512]{1,0:T(8,128)(2,1)S(1)} %get-tuple-element.38), channel_id=1, source_target_pairs={{0,3},{1,2},{2,1},{3,0},{4,7},{5,6},{6,5},{7,4},{8,11},{9,10},{10,... | collective-permute-start | bytes 393224 | tf_op jit(solution)/shard_map/ppermute | solution.py:142
  44.6 2.9 %collective-permute-done.8.refs_12_.refs_2_ = bf16[128,512]{1,0:T(8,128)(2,1)S(1)} collective-permute-done((bf16[128,512]{1,0:T(8,128)(2,1)S(1)}, bf16[128,512]{1,0:T(8,128)(2,1)S(1)}, u32[]{:S(2)}, u32[]{:S(2)}) %collective-permute-start.8) | collective-permute-done | bytes 131104 | tf_op jit(solution)/shard_map/ppermute | solution.py:142
  47.6 1.7 %collective-permute-done.10.refs_14_.refs_4_ = bf16[128,512]{1,0:T(8,128)(2,1)S(1)} collective-permute-done((bf16[128,512]{1,0:T(8,128)(2,1)S(1)}, bf16[128,512]{1,0:T(8,128)(2,1)S(1)}, u32[]{:S(2)}, u32[]{:S(2)}) %collective-permute-start.10) | collective-permute-done | bytes 131104 | tf_op jit(solution)/shard_map/ppermute | solution.py:142
  49.3 2.8 %cross.1 = (f32[32,4,128]{2,1,0:T(4,128)}, bf16[128,512]{1,0:T(8,128)(2,1)S(1)}, bf16[128,512]{1,0:T(8,128)(2,1)S(1)}, bf16[128,512]{1,0:T(8,128)(2,1)S(1)}, bf16[128,512]{1,0:T(8,128)(2,1)S(1)}) custom-call(s32[3]{0:T(128)S(1)} %pad_add_fusion.place_ref.refs_0_, bf16[272,512]{1,0:T(8,128)(2,1)S(1)} %get-tuple-element.30.refs_2_.refs_0_, ...), custom_call_target="tpu_custom_call" | custom-call | flops 1000 | bytes 1000 | tf_op jit(solution)/shard_map/cross/pallas_call | solution.py:157
  52.1 3.8 %all-to-all-start = ((f32[32,4,128]{2,1,0:T(4,128)}), f32[32,4,128]{2,1,0:T(4,128)}, u32[]{:S(2)}, u32[]{:S(2)}) async-start(f32[32,4,128]{2,1,0:T(4,128)} %get-tuple-element.54), calls=%async_computation | async-start | bytes 131072 | tf_op jit(solution)/shard_map/all_to_all | solution.py:475
  55.9 1.8 %collective-permute-start.14 = (bf16[128,512]{1,0:T(8,128)(2,1)S(1)}, bf16[128,512]{1,0:T(8,128)(2,1)S(1)}, u32[]{:S(2)}, u32[]{:S(2)}) collective-permute-start(bf16[128,512]{1,0:T(8,128)(2,1)S(1)} %get-tuple-element.47), channel_id=1, source_target_pairs={{0,1},{1,0},{2,3},{3,2},{4,5},{5,4},{6,7},{7,6},{8,9},{9,8},{10,11... | collective-permute-start | bytes 393224 | tf_op jit(solution)/shard_map/ppermute | solution.py:142
  57.7 1.5 %collective-permute-start.15 = (bf16[128,512]{1,0:T(8,128)(2,1)S(1)}, bf16[128,512]{1,0:T(8,128)(2,1)S(1)}, u32[]{:S(2)}, u32[]{:S(2)}) collective-permute-start(bf16[128,512]{1,0:T(8,128)(2,1)S(1)} %get-tuple-element.48), channel_id=1, source_target_pairs={{0,2},{1,3},{2,0},{3,1},{4,6},{5,7},{6,4},{7,5},{8,10},{9,11},{10,... | collective-permute-start | bytes 393224 | tf_op jit(solution)/shard_map/ppermute | solution.py:142
  59.5 3.8 %all-to-all-done = f32[32,4,128]{2,1,0:T(4,128)} async-done(((f32[32,4,128]{2,1,0:T(4,128)}), f32[32,4,128]{2,1,0:T(4,128)}, u32[]{:S(2)}, u32[]{:S(2)}) %all-to-all-start) | async-done | bytes 65568 | tf_op jit(solution)/shard_map/all_to_all | solution.py:475
  64.8 1.6 %collective-permute-done.16.refs_8_ = bf16[128,512]{1,0:T(8,128)(2,1)S(1)} collective-permute-done((bf16[128,512]{1,0:T(8,128)(2,1)S(1)}, bf16[128,512]{1,0:T(8,128)(2,1)S(1)}, u32[]{:S(2)}, u32[]{:S(2)}) %collective-permute-start.16) | collective-permute-done | bytes 131104 | tf_op jit(solution)/shard_map/ppermute | solution.py:142
  66.5 2.5 %outputs.1 = (bf16[1,128,2048]{2,1,0:T(8,128)(2,1)}, bf16[1,128,2048]{2,1,0:T(8,128)(2,1)}, bf16[1,128,2048]{2,1,0:T(8,128)(2,1)}, bf16[1,128,2048]{2,1,0:T(8,128)(2,1)}) custom-call(s32[3]{0:T(128)S(1)} %pad_add_fusion.place_ref.refs_0_, bf16[128,512]{1,0:T(8,128)(2,1)S(1)} %get-tuple-element.35.refs_1_, ...), custom_call_target="tpu_custom_call" | custom-call | flops 1000 | bytes 1000 | tf_op jit(solution)/shard_map/outputs/pallas_call | solution.py:480
  (35 shorter events, 4.5 us)
Async XLA Ops:
  0.6 6.3 %copy-start.4 = (bf16[32,16]{0,1:T(8,128)(2,1)S(1)}, bf16[32,16]{0,1:T(8,128)(2,1)}, u32[]{:S(2)}) copy-start(bf16[32,16]{0,1:T(8,128)(2,1)} %param.9) | copy-start | bytes 3076
  0.6 5.2 %collective-permute-start.2 = (bf16[16,32]{1,0:T(8,128)(2,1)}, bf16[16,32]{1,0:T(8,128)(2,1)S(1)}, u32[]{:S(2)}, u32[]{:S(2)}) collective-permute-start(bf16[16,32]{1,0:T(8,128)(2,1)} %bitcast.13), channel_id=1, source_target_pairs={{0,24},{8,0},{16,8},{24,16},{1,25},{9,1},{17,9},{25,17},{2,26},{10... | collective-permute-start | bytes 3080 | tf_op jit(solution)/shard_map/ppermute | solution.py:437
  3.1 3.8 %collective-permute-start.1 = (bf16[16,32]{1,0:T(8,128)(2,1)}, bf16[16,32]{1,0:T(8,128)(2,1)S(1)}, u32[]{:S(2)}, u32[]{:S(2)}) collective-permute-start(bf16[16,32]{1,0:T(8,128)(2,1)} %bitcast.14), channel_id=1, source_target_pairs={{0,16},{8,24},{16,0},{24,8},{1,17},{9,25},{17,1},{25,9},{2,18},{10... | collective-permute-start | bytes 3080 | tf_op jit(solution)/shard_map/ppermute | solution.py:437
  3.7 3.2 %collective-permute-start = (bf16[16,32]{1,0:T(8,128)(2,1)}, bf16[16,32]{1,0:T(8,128)(2,1)S(1)}, u32[]{:S(2)}, u32[]{:S(2)}) collective-permute-start(bf16[16,32]{1,0:T(8,128)(2,1)} %bitcast.15), channel_id=1, source_target_pairs={{0,8},{8,16},{16,24},{24,0},{1,9},{9,17},{17,25},{25,1},{2,10},{10... | collective-permute-start | bytes 3080 | tf_op jit(solution)/shard_map/ppermute | solution.py:437
  7.6 8.9 %collective-permute-start.3 = (bf16[272,512]{1,0:T(8,128)(2,1)S(1)}, bf16[272,512]{1,0:T(8,128)(2,1)S(1)}, u32[]{:S(2)}, u32[]{:S(2)}) collective-permute-start(bf16[272,512]{1,0:T(8,128)(2,1)S(1)} %get-tuple-element.31), channel_id=1, source_target_pairs={{0,1},{1,0},{2,3},{3,2},{4,5},{5,4},{6,7},{7,6},{8,9},{9,8},{10,11... | collective-permute-start | bytes 835592 | tf_op jit(solution)/shard_map/ppermute | solution.py:142
  9.2 12.3 %collective-permute-start.4 = (bf16[272,512]{1,0:T(8,128)(2,1)S(1)}, bf16[272,512]{1,0:T(8,128)(2,1)S(1)}, u32[]{:S(2)}, u32[]{:S(2)}) collective-permute-start(bf16[272,512]{1,0:T(8,128)(2,1)S(1)} %get-tuple-element.32), channel_id=1, source_target_pairs={{0,2},{1,3},{2,0},{3,1},{4,6},{5,7},{6,4},{7,5},{8,10},{9,11},{10,... | collective-permute-start | bytes 835592 | tf_op jit(solution)/shard_map/ppermute | solution.py:142
  10.8 18.3 %collective-permute-start.5 = (bf16[272,512]{1,0:T(8,128)(2,1)S(1)}, bf16[272,512]{1,0:T(8,128)(2,1)S(1)}, u32[]{:S(2)}, u32[]{:S(2)}) collective-permute-start(bf16[272,512]{1,0:T(8,128)(2,1)S(1)} %get-tuple-element.33), channel_id=1, source_target_pairs={{0,3},{1,2},{2,1},{3,0},{4,7},{5,6},{6,5},{7,4},{8,11},{9,10},{10,... | collective-permute-start | bytes 835592 | tf_op jit(solution)/shard_map/ppermute | solution.py:142
  11.2 25.6 %collective-permute-start.7 = (bf16[128,512]{1,0:T(8,128)(2,1)S(1)}, bf16[128,512]{1,0:T(8,128)(2,1)S(1)}, u32[]{:S(2)}, u32[]{:S(2)}) collective-permute-start(bf16[128,512]{1,0:T(8,128)(2,1)S(1)} %get-tuple-element.34), channel_id=1, source_target_pairs={{0,6},{1,7},{2,4},{3,5},{4,2},{5,3},{6,0},{7,1},{8,14},{9,15},{10,... | collective-permute-start | bytes 393224 | tf_op jit(solution)/shard_map/ppermute | solution.py:142
  14.8 27.3 %collective-permute-start.11 = (bf16[128,512]{1,0:T(8,128)(2,1)S(1)}, bf16[128,512]{1,0:T(8,128)(2,1)S(1)}, u32[]{:S(2)}, u32[]{:S(2)}) collective-permute-start(bf16[128,512]{1,0:T(8,128)(2,1)S(1)} %get-tuple-element.39), channel_id=1, source_target_pairs={{0,4},{1,5},{2,6},{3,7},{4,0},{5,1},{6,2},{7,3},{8,12},{9,13},{10,... | collective-permute-start | bytes 393224 | tf_op jit(solution)/shard_map/ppermute | solution.py:142
  29.1 7.6 %collective-permute-start.6 = (bf16[16,512]{1,0:T(8,128)(2,1)S(1)}, bf16[16,512]{1,0:T(8,128)(2,1)S(1)}, u32[]{:S(2)}, u32[]{:S(2)}) collective-permute-start(bf16[16,512]{1,0:T(8,128)(2,1)S(1)} %pad_maximum_fusion.refs_0_), channel_id=1, source_target_pairs={{0,4},{1,5},{2,6},{3,7},{4,0},{5,1},{6,2},{7,3},{8,12},{9,13},{10,... | collective-permute-start | bytes 49160 | tf_op jit(solution)/shard_map/ppermute | solution.py:142
  31.0 13.5 %collective-permute-start.12 = (bf16[128,512]{1,0:T(8,128)(2,1)S(1)}, bf16[128,512]{1,0:T(8,128)(2,1)S(1)}, u32[]{:S(2)}, u32[]{:S(2)}) collective-permute-start(bf16[128,512]{1,0:T(8,128)(2,1)S(1)} %get-tuple-element.40), channel_id=1, source_target_pairs={{0,5},{1,4},{2,7},{3,6},{4,1},{5,0},{6,3},{7,2},{8,13},{9,12},{10,... | collective-permute-start | bytes 393224 | tf_op jit(solution)/shard_map/ppermute | solution.py:142
  33.0 11.6 %collective-permute-start.13 = (bf16[128,512]{1,0:T(8,128)(2,1)S(1)}, bf16[128,512]{1,0:T(8,128)(2,1)S(1)}, u32[]{:S(2)}, u32[]{:S(2)}) collective-permute-start(bf16[128,512]{1,0:T(8,128)(2,1)S(1)} %get-tuple-element.41), channel_id=1, source_target_pairs={{0,7},{1,6},{2,5},{3,4},{4,3},{5,2},{6,1},{7,0},{8,15},{9,14},{10,... | collective-permute-start | bytes 393224 | tf_op jit(solution)/shard_map/ppermute | solution.py:142
  40.5 6.9 %collective-permute-start.8 = (bf16[128,512]{1,0:T(8,128)(2,1)S(1)}, bf16[128,512]{1,0:T(8,128)(2,1)S(1)}, u32[]{:S(2)}, u32[]{:S(2)}) collective-permute-start(bf16[128,512]{1,0:T(8,128)(2,1)S(1)} %get-tuple-element.36), channel_id=1, source_target_pairs={{0,1},{1,0},{2,3},{3,2},{4,5},{5,4},{6,7},{7,6},{8,9},{9,8},{10,11... | collective-permute-start | bytes 393224 | tf_op jit(solution)/shard_map/ppermute | solution.py:142
  42.1 5.4 %collective-permute-start.9 = (bf16[128,512]{1,0:T(8,128)(2,1)S(1)}, bf16[128,512]{1,0:T(8,128)(2,1)S(1)}, u32[]{:S(2)}, u32[]{:S(2)}) collective-permute-start(bf16[128,512]{1,0:T(8,128)(2,1)S(1)} %get-tuple-element.37), channel_id=1, source_target_pairs={{0,2},{1,3},{2,0},{3,1},{4,6},{5,7},{6,4},{7,5},{8,10},{9,11},{10,... | collective-permute-start | bytes 393224 | tf_op jit(solution)/shard_map/ppermute | solution.py:142
  42.1 7.1 %collective-permute-start.10 = (bf16[128,512]{1,0:T(8,128)(2,1)S(1)}, bf16[128,512]{1,0:T(8,128)(2,1)S(1)}, u32[]{:S(2)}, u32[]{:S(2)}) collective-permute-start(bf16[128,512]{1,0:T(8,128)(2,1)S(1)} %get-tuple-element.38), channel_id=1, source_target_pairs={{0,3},{1,2},{2,1},{3,0},{4,7},{5,6},{6,5},{7,4},{8,11},{9,10},{10,... | collective-permute-start | bytes 393224 | tf_op jit(solution)/shard_map/ppermute | solution.py:142
  49.2 17.2 %copy-start = (bf16[1,128,2048]{2,1,0:T(8,128)(2,1)S(1)}, bf16[1,128,2048]{2,1,0:T(8,128)(2,1)}, u32[]{:S(2)}) copy-start(bf16[1,128,2048]{2,1,0:T(8,128)(2,1)} %refs_11_.1) | copy-start | bytes 1572868
  49.2 17.2 %copy-start.1 = (bf16[1,128,2048]{2,1,0:T(8,128)(2,1)S(1)}, bf16[1,128,2048]{2,1,0:T(8,128)(2,1)}, u32[]{:S(2)}) copy-start(bf16[1,128,2048]{2,1,0:T(8,128)(2,1)} %refs_9_.1) | copy-start | bytes 1572868
  49.2 17.2 %copy-start.2 = (bf16[1,128,2048]{2,1,0:T(8,128)(2,1)S(1)}, bf16[1,128,2048]{2,1,0:T(8,128)(2,1)}, u32[]{:S(2)}) copy-start(bf16[1,128,2048]{2,1,0:T(8,128)(2,1)} %refs_10_.1) | copy-start | bytes 1572868
  49.2 17.2 %copy-start.3 = (bf16[1,128,2048]{2,1,0:T(8,128)(2,1)S(1)}, bf16[1,128,2048]{2,1,0:T(8,128)(2,1)}, u32[]{:S(2)}) copy-start(bf16[1,128,2048]{2,1,0:T(8,128)(2,1)} %refs_12_.1) | copy-start | bytes 1572868
  52.1 11.2 %all-to-all-start = ((f32[32,4,128]{2,1,0:T(4,128)}), f32[32,4,128]{2,1,0:T(4,128)}, u32[]{:S(2)}, u32[]{:S(2)}) async-start(f32[32,4,128]{2,1,0:T(4,128)} %get-tuple-element.54), calls=%async_computation | async-start | bytes 131072 | tf_op jit(solution)/shard_map/all_to_all | solution.py:475
  55.9 8.9 %collective-permute-start.14 = (bf16[128,512]{1,0:T(8,128)(2,1)S(1)}, bf16[128,512]{1,0:T(8,128)(2,1)S(1)}, u32[]{:S(2)}, u32[]{:S(2)}) collective-permute-start(bf16[128,512]{1,0:T(8,128)(2,1)S(1)} %get-tuple-element.47), channel_id=1, source_target_pairs={{0,1},{1,0},{2,3},{3,2},{4,5},{5,4},{6,7},{7,6},{8,9},{9,8},{10,11... | collective-permute-start | bytes 393224 | tf_op jit(solution)/shard_map/ppermute | solution.py:142
  57.7 7.1 %collective-permute-start.15 = (bf16[128,512]{1,0:T(8,128)(2,1)S(1)}, bf16[128,512]{1,0:T(8,128)(2,1)S(1)}, u32[]{:S(2)}, u32[]{:S(2)}) collective-permute-start(bf16[128,512]{1,0:T(8,128)(2,1)S(1)} %get-tuple-element.48), channel_id=1, source_target_pairs={{0,2},{1,3},{2,0},{3,1},{4,6},{5,7},{6,4},{7,5},{8,10},{9,11},{10,... | collective-permute-start | bytes 393224 | tf_op jit(solution)/shard_map/ppermute | solution.py:142
  59.2 7.3 %collective-permute-start.16 = (bf16[128,512]{1,0:T(8,128)(2,1)S(1)}, bf16[128,512]{1,0:T(8,128)(2,1)S(1)}, u32[]{:S(2)}, u32[]{:S(2)}) collective-permute-start(bf16[128,512]{1,0:T(8,128)(2,1)S(1)} %get-tuple-element.49), channel_id=1, source_target_pairs={{0,3},{1,2},{2,1},{3,0},{4,7},{5,6},{6,5},{7,4},{8,11},{9,10},{10,... | collective-permute-start | bytes 393224 | tf_op jit(solution)/shard_map/ppermute | solution.py:142

commit v3 on v2

--- a/solution.py
+++ b/solution.py
@@ -184,42 +184,42 @@
     for j in range(quarters):
         columns = pl.ds(pl.multiple_of((quarter ^ j) * width, width), width)
         a = a_ref[:, columns]
-        a_outs[j][...] = a
+        taps = taps_ref[quarter ^ j]
+        taps = jnp.concatenate([taps, jnp.zeros((TAIL - local, BLOCK), f32)], axis=0)
+        tail = jnp.concatenate([taps, jnp.zeros((TAIL, width - BLOCK), f32)], axis=1).astype(bf16)
+        a_outs[j][:BLOCK] = a
+        a_outs[j][BLOCK:] = tail
         outs[j][:BLOCK] = a
         outs[j][BLOCK : 2 * BLOCK] = b_ref[:, columns]
-        outs[j][2 * BLOCK :] = jnp.zeros((TAIL, width), bf16)
-        taps = taps_ref[quarter ^ j]
-        taps = jnp.concatenate([taps, jnp.zeros((TAIL - local, BLOCK), f32)], axis=0)
-        outs[j][2 * BLOCK :, :BLOCK] = taps.astype(bf16)
+        outs[j][2 * BLOCK :] = tail
 
 
 def bands(quarters, dp_count, place_ref, taps_in, taps_ref, causal_ref, anti_ref):
     half, quarter, dp_index = place_ref[0], place_ref[1], place_ref[2]
     local, rows = taps_ref.shape[1:]
     for u in range(2):
-        piece = taps_in[u][...].astype(jnp.float32)
         for j in range(quarters):
+            piece = taps_in[u * quarters + j][-TAIL:, :BLOCK].astype(jnp.float32)
             for p in range(dp_count):
                 owner = lax.rem(dp_index + dp_count - p, dp_count) * 2 * quarters + (half ^ u) * quarters + (quarter ^ j)
-                start = j * BLOCK + p * rows
+                start = p * rows
                 taps_ref[owner] = piece[:local, start : start + rows]
     for g in range(local):
         line = jnp.concatenate([taps_ref[o, g : g + 1] for o in range(taps_ref.shape[0])], axis=1)
-        line = jnp.concatenate([line, jnp.zeros((1, 2 * BLOCK), jnp.float32)], axis=1)
-        spread = jnp.broadcast_to(line, (2 * BLOCK, K + 2 * BLOCK))
-        shear = pltpu.roll(spread, 0, 1, stride=1, stride_axis=0)
-        anti_ref[g] = shear[:, :K].astype(jnp.bfloat16)
+        line = jnp.concatenate([line, jnp.zeros((1, BLOCK), jnp.float32)], axis=1)
+        shear = pltpu.roll(jnp.broadcast_to(line, (BLOCK, K + BLOCK)), 0, 1, stride=1, stride_axis=0)
+        zero = jnp.zeros((BLOCK, BLOCK), jnp.bfloat16)
         count = K // BLOCK
-        turned = [shear[:BLOCK, m * BLOCK : (m + 1) * BLOCK].T.astype(jnp.bfloat16) for m in range(count)]
-        turned.append(jnp.zeros((BLOCK, BLOCK), jnp.bfloat16))
+        tiles = [shear[:, m * BLOCK : (m + 1) * BLOCK] for m in range(count)]
         for b in range(count):
-            causal_ref[g, :BLOCK, b * BLOCK : (b + 1) * BLOCK] = turned[count - 2 - b]
-            causal_ref[g, BLOCK:, b * BLOCK : (b + 1) * BLOCK] = turned[count - 1 - b]
-
-
-def in_order(scratch_ref, quarter, chunks):
-    for j, chunk in enumerate(chunks):
-        scratch_ref[quarter ^ j] = chunk[...]
+            columns = slice(b * BLOCK, (b + 1) * BLOCK)
+            anti_ref[g, :BLOCK, columns] = tiles[b].astype(jnp.bfloat16)
+            anti_ref[g, BLOCK:, columns] = tiles[b - 1].astype(jnp.bfloat16) if b else zero
+        turned = [tile.T.astype(jnp.bfloat16) for tile in tiles] + [zero]
+        for b in range(count):
+            columns = slice(b * BLOCK, (b + 1) * BLOCK)
+            causal_ref[g, :BLOCK, columns] = turned[count - 2 - b]
+            causal_ref[g, BLOCK:, columns] = turned[count - 1 - b]
 
 
 def rows_of(ref, lanes):
@@ -239,15 +239,16 @@
     return dot(band[:, : data.shape[0] - p * 2 * BLOCK], data[p * 2 * BLOCK :])
 
 
-def lag_lines(mixed, gated, first, turn):
+def lag_lines(mixed, mixed_first, gated, gated_first, turn):
     count = mixed.shape[0] // BLOCK
     blocks = K // BLOCK
     turned = jnp.concatenate(
         [dot(turn, mixed[j * BLOCK : (j + 1) * BLOCK]).astype(jnp.bfloat16) for j in range(count)], axis=0
     )
     sums = [None] * blocks
-    for i in range(count):
-        top = min(count, first + i + 1)
+    for i in range(gated.shape[0] // BLOCK):
+        first = gated_first + i - mixed_first
+        top = min(count, first + 1)
         product = lax.dot_general(
             turned[: top * BLOCK],
             gated[i * BLOCK : (i + 1) * BLOCK],
@@ -256,11 +257,9 @@
         )
         for j in range(top):
             term = product[j * BLOCK : (j + 1) * BLOCK]
-            lag = first + i - j
-            sums[lag] = term if sums[lag] is None else sums[lag] + term
+            sums[first - j] = term if sums[first - j] is None else sums[first - j] + term
     last = max(m for m in range(blocks) if sums[m] is not None)
-    zero = jnp.zeros((BLOCK, BLOCK), jnp.float32)
-    table = jnp.concatenate([zero if t is None else t for t in sums[: last + 1]] + [zero], axis=1)
+    table = jnp.concatenate(sums[: last + 1] + [jnp.zeros((BLOCK, BLOCK), jnp.float32)], axis=1)
     span = (last + 2) * BLOCK
     shear = jnp.sum(pltpu.roll(table, 0, 1, stride=1, stride_axis=0), axis=0, keepdims=True)
     if span < K:
@@ -274,148 +273,120 @@
     return jnp.where(rows + columns == BLOCK - 1, 1.0, 0.0).astype(jnp.bfloat16)
 
 
-def local_kernel(quarters, dp_count, place_ref, *refs):
-    taps_in, refs = refs[:2], refs[2:]
-    ab_in, a_out = refs[:quarters], refs[quarters : 2 * quarters]
-    causal_ref, anti_ref, sums_ref, lines_ref, a_ref, b_ref, done_ref, taps_ref = refs[2 * quarters :]
-    bands(quarters, dp_count, place_ref, taps_in, taps_ref, causal_ref, anti_ref)
+def gather(quarters, place_ref, ab_in, r_in, a_ref, data_ref):
     half, quarter = place_ref[0], place_ref[1]
-    in_order(a_ref, quarter, [ab.at[:BLOCK] for ab in ab_in])
-    in_order(b_ref, quarter, [ab.at[BLOCK : 2 * BLOCK] for ab in ab_in])
+    for j in range(quarters):
+        a_ref[quarter ^ j] = ab_in[j][:BLOCK]
+        data_ref[half * quarters + (quarter ^ j)] = ab_in[j][BLOCK : 2 * BLOCK]
+        data_ref[(1 - half) * quarters + (quarter ^ j)] = r_in[j][:BLOCK]
+
+
+def lags_kernel(quarters, place_ref, *refs):
+    ab_in, r_in, refs = refs[:quarters], refs[quarters : 2 * quarters], refs[2 * quarters :]
+    shares_ref, a_ref, data_ref, lines_ref = refs
+    gather(quarters, place_ref, ab_in, r_in, a_ref, data_ref)
+    half = place_ref[0]
     turn = exchange()
-
-    def work(a_band, a_part, b_band, b_part, a_mixed):
+    local = lines_ref.shape[0]
+    length = quarters * BLOCK
+
+    @pl.when(half == 0)
+    def lower():
+        for g in range(local):
+            lanes = slice(g * BLOCK, (g + 1) * BLOCK)
+            mixed, gated = rows_of(a_ref, lanes), rows_of(data_ref, lanes)
+            lines_ref[g : g + 1] = lag_lines(mixed, 0, gated if g < local // 2 else gated[:length], 0, turn)
+
+    @pl.when(half != 0)
+    def upper():
+        for g in range(local):
+            lanes = slice(g * BLOCK, (g + 1) * BLOCK)
+            gated, mixed = rows_of(a_ref, lanes), rows_of(data_ref, lanes)
+            first = quarters if g < local // 2 else 0
+            lines_ref[g : g + 1] = lag_lines(mixed[first * BLOCK :], first, gated, quarters, turn)
+
+    step = BLOCK // local
+    lane = lax.broadcasted_iota(jnp.int32, (1, K), 1) % BLOCK // step
+    for u in range(local):
+        row = jnp.zeros((1, K), jnp.float32)
+        for g in range(local):
+            row = jnp.where(lane == g, pltpu.roll(lines_ref[g : g + 1], (g - u) * step % K, 1), row)
+        for block in range(K // BLOCK):
+            shares_ref[block * local + u : block * local + u + 1] = row[:, block * BLOCK : (block + 1) * BLOCK]
+
+
+def sums_kernel(quarters, dp_count, place_ref, *refs):
+    ab_in, r_in, outs, refs = refs[:quarters], refs[quarters : 2 * quarters], refs[2 * quarters : 3 * quarters], refs[3 * quarters :]
+    causal_ref, anti_ref, a_ref, data_ref, a_sum_ref, b_sum_ref, taps_ref = refs
+    gather(quarters, place_ref, ab_in, r_in, a_ref, data_ref)
+    bands(quarters, dp_count, place_ref, ab_in + r_in, taps_ref, causal_ref, anti_ref)
+    half, quarter = place_ref[0], place_ref[1]
+
+    def work(a_part, a_band, b_part, b_band, first):
         for g in range(causal_ref.shape[0]):
             lanes = slice(g * BLOCK, (g + 1) * BLOCK)
-            a_rows, b_rows = rows_of(a_ref, lanes), rows_of(b_ref, lanes)
+            a_rows, data = rows_of(a_ref, lanes), rows_of(data_ref, lanes)
             for p in range(quarters // 2):
                 pair = slice(2 * p, 2 * p + 2)
-                a_sum = a_part(a_band.at[g], a_rows, p).reshape(2, BLOCK, BLOCK)
-                done_ref[pair, :, lanes] = a_sum.astype(jnp.bfloat16)
-                sums_ref[pair, :, lanes] = b_part(b_band.at[g], b_rows, p).reshape(2, BLOCK, BLOCK)
-            mixed, gated = (a_rows, b_rows) if a_mixed else (b_rows, a_rows)
-            lines_ref[g : g + 1] = lag_lines(mixed, gated, 0, turn)
+                a_sum = a_part(a_band.at[g], a_rows, p)
+                a_sum_ref[pair, :, lanes] = a_sum.reshape(2, BLOCK, BLOCK).astype(jnp.bfloat16)
+                b_sum = b_part(b_band.at[g], data, first + p)
+                b_sum_ref[pair, :, lanes] = b_sum.reshape(2, BLOCK, BLOCK).astype(jnp.bfloat16)
 
     @pl.when(half == 0)
     def lower():
-        work(causal_ref, causal_part, anti_ref, anti_part, True)
+        work(causal_part, causal_ref, anti_part, anti_ref, 0)
 
     @pl.when(half != 0)
     def upper():
-        work(anti_ref, anti_part, causal_ref, causal_part, False)
+        work(anti_part, anti_ref, causal_part, causal_ref, quarters // 2)
 
     for j in range(quarters):
-        a_out[j][...] = done_ref[quarter ^ j]
-
-
-def lag_kernel(quarters, place_ref, *refs):
-    a_in, r_in = refs[:quarters], refs[quarters : 2 * quarters]
-    lines_ref, out_ref, mixed_ref, gated_ref, total_ref = refs[2 * quarters :]
-    half, quarter = place_ref[0], place_ref[1]
-    width = mixed_ref.shape[2]
-    count = width // BLOCK
-    turn = exchange()
-
-    def gather(mixed, gated, lanes):
-        for j in range(quarters):
-            mixed_ref[quarter ^ j] = mixed[j][:BLOCK, lanes]
-            gated_ref[quarter ^ j] = gated[j][:BLOCK, lanes]
-
-    @pl.when(half == 0)
-    def lower():
-        gather(a_in, r_in, slice(0, width))
-
-    @pl.when(half != 0)
-    def upper():
-        gather(r_in, a_in, slice(width, 2 * width))
-
-    total_ref[...] = lines_ref[...]
-    cross = []
-    for g in range(count):
-        lanes = slice(g * BLOCK, (g + 1) * BLOCK)
-        cross.append(lag_lines(rows_of(mixed_ref, lanes), rows_of(gated_ref, lanes), quarters, turn))
-    cross = jnp.concatenate(cross, axis=0)
-
-    @pl.when(half == 0)
-    def add_lower():
-        total_ref[:count] += cross
-
-    @pl.when(half != 0)
-    def add_upper():
-        total_ref[count:] += cross
-
-    owners, step = out_ref.shape[0], K // out_ref.shape[0]
-    for o in range(owners):
-        start = o * step // BLOCK * BLOCK
-        out_ref[o] = total_ref[:, start : start + BLOCK]
-
-
-def cross_kernel(quarters, place_ref, *refs):
-    ab_in, r_in = refs[:quarters], refs[quarters : 2 * quarters]
-    lines_ref, sums_ref, causal_ref, anti_ref, shares_ref = refs[2 * quarters : 2 * quarters + 5]
-    b_out = refs[2 * quarters + 5 : 3 * quarters + 5]
-    r_ref, done_ref, mixed_ref, gated_ref, total_ref = refs[3 * quarters + 5 :]
-    lag_kernel(quarters, place_ref, *ab_in, *r_in, lines_ref, shares_ref, mixed_ref, gated_ref, total_ref)
-    half, quarter = place_ref[0], place_ref[1]
-    in_order(r_ref, quarter, r_in)
-    length = quarters * BLOCK
-
-    def work(band, first):
-        for g in range(causal_ref.shape[0]):
-            lanes = slice(g * BLOCK, (g + 1) * BLOCK)
-            rows = rows_of(r_ref, lanes)
-            for p in range(quarters // 2):
-                pair = slice(2 * p, 2 * p + 2)
-                start = first(p * 2 * BLOCK)
-                part = dot(band[g, :, start : start + length], rows).reshape(2, BLOCK, BLOCK)
-                done_ref[pair, :, lanes] = (sums_ref[pair, :, lanes] + part).astype(jnp.bfloat16)
-
-    @pl.when(half == 0)
-    def lower():
-        work(anti_ref, lambda row: length - row)
-
-    @pl.when(half != 0)
-    def upper():
-        work(causal_ref, lambda row: K - length - row - 2 * BLOCK)
-
-    for j in range(quarters):
-        b_out[j][...] = done_ref[quarter ^ j]
+        outs[j][:BLOCK] = a_sum_ref[quarter ^ j]
+        outs[j][BLOCK:] = b_sum_ref[quarter ^ j]
+
+
+def owned_kernel(scale, place_ref, arrived_ref, out_ref):
+    groups, rows = out_ref.shape
+    local = BLOCK // rows
+    quarters = groups // local
+    total = arrived_ref[:quarters]
+    for i in range(1, arrived_ref.shape[0] // quarters):
+        total = total + arrived_ref[i * quarters : (i + 1) * quarters]
+    total = total * scale
+    for g in range(local):
+        part = (total if g == 0 else pltpu.roll(total, BLOCK - g * rows, 1))[:, :rows]
+        for q in range(quarters):
+            out_ref[q * local + g : q * local + g + 1] = part[q : q + 1]
 
 
 def outputs_kernel(quarters, place_ref, *refs):
     f32, bf16 = jnp.float32, jnp.bfloat16
-    a_in, b_in, refs = refs[:quarters], refs[quarters : 2 * quarters], refs[2 * quarters :]
-    inputs, outputs, stores, results, (in_sem, out_sem) = refs[:4], refs[4:8], refs[8:12], refs[12:16], refs[16:]
+    back, inputs, refs = refs[:quarters], refs[quarters : quarters + 4], refs[quarters + 4 :]
+    outputs, results, sem = refs[:4], refs[4:8], refs[8]
     half, quarter = place_ref[0], place_ref[1]
-    width = a_in[0].shape[1]
-
-    def copies(j, out):
-        columns = pl.ds(pl.multiple_of((quarter ^ j) * width, width), width)
-        if out:
-            return [
-                pltpu.make_async_copy(store.at[j], target.at[0, :, columns], out_sem.at[j, i])
-                for i, (store, target) in enumerate(zip(results, outputs))
-            ]
+    width = back[0].shape[1]
+
+    def copies(j, columns):
         return [
-            pltpu.make_async_copy(source.at[0, :, columns], store.at[j], in_sem.at[j, i])
-            for i, (source, store) in enumerate(zip(inputs, stores))
+            pltpu.make_async_copy(store.at[j], target.at[0, :, columns], sem.at[j, i])
+            for i, (store, target) in enumerate(zip(results, outputs))
         ]
 
+    def place(j):
+        return pl.ds(pl.multiple_of((quarter ^ j) * width, width), width)
+
     for j in range(quarters):
-        for copy in copies(j, False):
-            copy.start()
-    for j in range(quarters):
-        for copy in copies(j, False):
-            copy.wait()
-        pre, post, values, cot = [store[j].astype(f32) for store in stores]
-        a_sum, b_sum = a_in[j][...].astype(f32), b_in[j][...].astype(f32)
+        columns = place(j)
+        pre, post, values, cot = [source[0, :, columns].astype(f32) for source in inputs]
+        a_sum, b_sum = back[j][:BLOCK].astype(f32), back[j][BLOCK:].astype(f32)
         convolved, carried = jnp.where(half == 0, a_sum, b_sum), jnp.where(half == 0, b_sum, a_sum)
         for result, value in zip(results, (post * convolved, carried * values, cot * convolved, carried * pre)):
             result[j] = value.astype(bf16)
-        for copy in copies(j, True):
+        for copy in copies(j, columns):
             copy.start()
     for j in range(quarters):
-        for copy in copies(j, True):
+        for copy in copies(j, place(j)):
             copy.wait()
 
 
@@ -442,55 +413,51 @@
     gated = (cotangent[0].astype(f32) * post_gate[0]).astype(bf16)
     a, b = jnp.where(lower, mixed, gated), jnp.where(lower, gated, mixed)
     store = pltpu.VMEM((quarters, BLOCK, width), bf16)
+    short = jax.ShapeDtypeStruct((BLOCK + TAIL, width), bf16)
     message = jax.ShapeDtypeStruct((2 * BLOCK + TAIL, width), bf16)
     chunks = call(
         lambda *refs: pack_kernel(quarters, dp_count, *refs), "pack", place, pieces + [a, b],
-        chunk_shapes(quarters, width) + [message] * quarters, [pltpu.VMEM((quarters, local, BLOCK), f32)],
+        [short] * quarters + [message] * quarters, [pltpu.VMEM((quarters, local, BLOCK), f32)],
         flops=1000, nbytes=1000,
     )
     a_own, ab_own = chunks[:quarters], chunks[quarters:]
     r_in = [swap(a_own[j], quarters + j) for j in range(quarters)]
     ab_in = [ab_own[0]] + [swap(ab_own[j], j) for j in range(1, quarters)]
 
-    taps = jnp.concatenate([message[2 * BLOCK :, :BLOCK] for message in ab_in], axis=1)
-    taps = [taps, swap(taps, quarters)]
-    whole = (quarters, BLOCK, width)
-    band = jax.ShapeDtypeStruct((local, 2 * BLOCK, K), bf16)
-    *a_done, causal, anti, sums, lines = call(
-        lambda *refs: local_kernel(quarters, dp_count, *refs), "local", place, taps + ab_in,
-        chunk_shapes(quarters, width)
-        + [band, band, jax.ShapeDtypeStruct(whole, f32), jax.ShapeDtypeStruct((local, K), f32)],
-        [store] * 3 + [pltpu.VMEM((owners, local, rows), f32)], flops=1000, nbytes=1000,
-        after=r_in[2:3],
-    )
-    a_back = [a_done[0]] + [swap(a_done[j], j) for j in range(1, quarters)]
-
-    half_store = pltpu.VMEM((quarters, BLOCK, width // 2), bf16)
-    shares, *b_done = call(
-        lambda *refs: cross_kernel(quarters, *refs), "cross", place, ab_in + r_in + [lines, sums, causal, anti],
-        [jax.ShapeDtypeStruct((owners, local, BLOCK), f32)] + chunk_shapes(quarters, width),
-        [store] * 2 + [half_store] * 2 + [pltpu.VMEM((local, K), f32)], flops=1000, nbytes=1000,
-        after=a_back[1:],
+    band = pltpu.VMEM((local, 2 * BLOCK, K), bf16)
+    store = pltpu.VMEM((quarters, BLOCK, width), bf16)
+    whole = pltpu.VMEM((parts, BLOCK, width), bf16)
+    done = call(
+        lambda *refs: sums_kernel(quarters, dp_count, *refs), "sums", place, ab_in + r_in, chunk_shapes(quarters, width, 2),
+        [band, band, store, whole, store, store, pltpu.VMEM((owners, local, rows), f32)], flops=1000, nbytes=1000,
+    )
+    back = [done[0]] + [swap(done[j], j) for j in range(1, quarters)]
+    token = lax.ppermute(done[0], "dp", [(i, i ^ 1) for i in range(dp_count)])
+    (shares,) = call(
+        lambda *refs: lags_kernel(quarters, *refs), "lags", place, ab_in + r_in,
+        [jax.ShapeDtypeStruct((owners, BLOCK), f32)], [store, whole, pltpu.VMEM((local, K), f32)],
+        flops=1000, nbytes=1000, after=[token],
     )
     arrived = lax.all_to_all(shares, every, 0, 0, tiled=True)
-    b_back = [b_done[0]] + [swap(b_done[j], j) for j in range(1, quarters)]
 
     shape = jax.ShapeDtypeStruct(pre_gate.shape, bf16)
     hbm = [pl.BlockSpec(memory_space=pltpu.HBM)] * 4
     output, grad_pre, grad_post, grad_values = pl.pallas_call(
         lambda *refs: outputs_kernel(quarters, *refs),
-        in_specs=[pl.BlockSpec(memory_space=pltpu.SMEM)] + vmem_specs(2 * quarters) + hbm,
+        in_specs=[pl.BlockSpec(memory_space=pltpu.SMEM)] + vmem_specs(quarters + 4),
         out_specs=hbm,
         out_shape=[shape] * 4,
-        scratch_shapes=[store] * 8 + [pltpu.SemaphoreType.DMA((quarters, 4))] * 2,
+        scratch_shapes=[store] * 4 + [pltpu.SemaphoreType.DMA((quarters, 4))],
         compiler_params=pltpu.CompilerParams(vmem_limit_bytes=20 * 1024 * 1024),
         cost_estimate=pl.CostEstimate(flops=1000, bytes_accessed=1000, transcendentals=0),
         name="outputs",
-    )(place, *a_back, *b_back, *gates)
-    total = jnp.sum(arrived.reshape(owners // quarters, groups, BLOCK), axis=0)
-    mine = lax.dynamic_slice_in_dim(total, (lax.axis_index(every) * rows) % BLOCK, rows, 1)
+    )(place, *back, *gates)
     total_tokens = dp_count * parts * pre_gate.shape[1] * (channels // groups)
-    return output, grad_pre, grad_post, grad_values, mine.T / float(total_tokens**0.5)
+    (mine,) = call(
+        lambda *refs: owned_kernel(1.0 / float(total_tokens**0.5), *refs), "owned", place, [arrived],
+        [jax.ShapeDtypeStruct((groups, rows), f32)], flops=1000, nbytes=1000,
+    )
+    return output, grad_pre, grad_post, grad_values, mine.T
 
 
 def solution(mesh):

time: 69.2 us -> 63.5 us (0.918)
  starting transfers between devices: 28.9 us -> 26 us
  waiting for transfers between devices: 26 us -> 23.8 us
  other arithmetic: 3.51 us -> 1.98 us
  Pallas kernels: 9.8 us -> 10.9 us
    ppermute x14 -> x10, starting transfers between devices: 21.9 us -> 17.7 us  [swap(): return lax.ppermute(chunk, 'seq', [(i, i ^ flip) for i in range(count)])]
    all_to_all x1, waiting for transfers between devices: 3.79 us -> 0.93 us  [swapped(): arrived = lax.all_to_all(shares, every, 0, 0, tiled=True)]
    pallas_call x3 -> x4, Pallas kernels: 7.29 us -> 8.81 us  [call(): pl.pallas_call(body, in_specs=[pl.BlockSpec(memory_space=pltpu.SMEM)] + v...]
    all_to_all x1, starting transfers between devices: 3.8 us -> 5.08 us  [swapped(): arrived = lax.all_to_all(shares, every, 0, 0, tiled=True)]
    reduce_sum x1 -> x0, other arithmetic: 0.85 us -> none  [swapped(): total = jnp.sum(arrived.reshape(owners // quarters, groups, BLOCK), axis=0)]
    ppermute x14 -> x10, waiting for transfers between devices: 21.1 us -> 21.8 us  [swap(): return lax.ppermute(chunk, 'seq', [(i, i ^ flip) for i in range(count)])]
  transfers between devices with their start and end apart: 18 -> 15, of which waited for: 11 -> 8; matrix products, arithmetic and copies ran while one was open for 5% -> 3% of each run, Pallas kernels for 5% -> 8%
where the time goes in v3:
time: 63.5 us; the launch traced here: 63.4 us
  starting transfers between devices  26 us (41%)
  waiting for transfers between devices  23.8 us (37%)
  Pallas kernels  10.9 us (17%)
  other arithmetic  1.98 us (3%)
  between operations  0.72 us (1%)
    ppermute x10, waiting for transfers between devices, swap(): return lax.ppermute(chunk, 'seq', [(i, i ^ flip) for i in range(count)])  21.8 us
    ppermute x10, starting transfers between devices, swap(): return lax.ppermute(chunk, 'seq', [(i, i ^ flip) for i in range(count)])  17.7 us
    pallas_call x4, Pallas kernels, call(): pl.pallas_call(body, in_specs=[pl.BlockSpec(memory_space=pltpu.SMEM)] + v...  8.81 us
    all_to_all x1, starting transfers between devices, swapped(): arrived = lax.all_to_all(shares, every, 0, 0, tiled=True)  5.08 us
    ppermute x3, starting transfers between devices, swapped(): lax.ppermute(taps, 'dp', [(i, (i + p) % dp_count) for i in range(dp_count)])  3.23 us
    pallas_call x1, Pallas kernels, swapped(): pl.pallas_call(lambda *refs: outputs_kernel(quarters, *refs), in_specs=[p...  2.04 us
    select_n x1, other arithmetic, swapped(): a, b = (jnp.where(lower, mixed, gated), jnp.where(lower, gated, mixed))  1.9 us
  transfers between devices with their start and end apart: 15, of which 8 were waited for; matrix products, arithmetic and copies ran while one was open for 3% of the time, Pallas kernels for 8%

profile of v3, /device:TPU:0, one launch (start us, length us, event | category | flops | bytes accessed | tf_op | source)
XLA Modules:
  0.0 63.4 jit_solution(7436051373188036385)
XLA Ops:
  0.6 2.4 %collective-permute-start.2 = (bf16[16,32]{1,0:T(8,128)(2,1)}, bf16[16,32]{1,0:T(8,128)(2,1)S(1)}, u32[]{:S(2)}, u32[]{:S(2)}) collective-permute-start(bf16[16,32]{1,0:T(8,128)(2,1)} %bitcast.14), channel_id=1, source_target_pairs={{0,24},{8,0},{16,8},{24,16},{1,25},{9,1},{17,9},{25,17},{2,26},{10... | collective-permute-start | bytes 3080 | tf_op jit(solution)/shard_map/ppermute | solution.py:408
  3.9 1.9 %select_bitcast_fusion = (bf16[128,2048]{1,0:T(8,128)(2,1)S(1)}, bf16[128,2048]{1,0:T(8,128)(2,1)S(1)}) fusion(pred[]{:T(512)S(6)} %lt.10, bf16[1,128,2048]{2,1,0:T(8,128)(2,1)} %refs_7_.1, bf16[1,128,2048]{2,1,0:T(8,128)(2,1)} %refs_5_.1, bf16[1,128,2048]{2,1,0:T(8,128)(2,1)} %refs_6_.1, bf16[1,128,2048]{2,1,0:T(8,128)(2,1)} %refs_8_.1), kind=kLoop, calls=%fused_computation.2 | loop fusion | flops 2621440 | bytes 3145729 | tf_op jit(solution)/shard_map/jit(_where)/select_n | solution.py:414
  5.9 1.0 %collective-permute-done.1.refs_2_ = bf16[16,32]{1,0:T(8,128)(2,1)S(1)} collective-permute-done((bf16[16,32]{1,0:T(8,128)(2,1)}, bf16[16,32]{1,0:T(8,128)(2,1)S(1)}, u32[]{:S(2)}, u32[]{:S(2)}) %collective-permute-start.1) | collective-permute-done | bytes 1056 | tf_op jit(solution)/shard_map/ppermute | solution.py:408
  6.9 0.7 %pack.1 = (bf16[144,512]{1,0:T(8,128)(2,1)S(1)}, bf16[144,512]{1,0:T(8,128)(2,1)S(1)}, bf16[144,512]{1,0:T(8,128)(2,1)S(1)}, bf16[144,512]{1,0:T(8,128)(2,1)S(1)...) custom-call(s32[3]{0:T(128)S(1)} %pad_add_fusion.place_ref.refs_0_, ...), custom_call_target="tpu_custom_call" | custom-call | flops 1000 | bytes 1000 | tf_op jit(solution)/shard_map/pack/pallas_call | solution.py:157
  7.6 2.7 %collective-permute-start.6 = (bf16[144,512]{1,0:T(8,128)(2,1)S(1)}, bf16[144,512]{1,0:T(8,128)(2,1)S(1)}, u32[]{:S(2)}, u32[]{:S(2)}) collective-permute-start(bf16[144,512]{1,0:T(8,128)(2,1)S(1)} %get-tuple-element.25), channel_id=1, source_target_pairs={{0,4},{1,5},{2,6},{3,7},{4,0},{5,1},{6,2},{7,3},{8,12},{9,13},{10,... | collective-permute-start | bytes 442376 | tf_op jit(solution)/shard_map/ppermute | solution.py:142
  10.3 1.3 %collective-permute-start.7 = (bf16[144,512]{1,0:T(8,128)(2,1)S(1)}, bf16[144,512]{1,0:T(8,128)(2,1)S(1)}, u32[]{:S(2)}, u32[]{:S(2)}) collective-permute-start(bf16[144,512]{1,0:T(8,128)(2,1)S(1)} %get-tuple-element.26), channel_id=1, source_target_pairs={{0,5},{1,4},{2,7},{3,6},{4,1},{5,0},{6,3},{7,2},{8,13},{9,12},{10,... | collective-permute-start | bytes 442376 | tf_op jit(solution)/shard_map/ppermute | solution.py:142
  12.1 1.6 %collective-permute-start.4 = (bf16[272,512]{1,0:T(8,128)(2,1)S(1)}, bf16[272,512]{1,0:T(8,128)(2,1)S(1)}, u32[]{:S(2)}, u32[]{:S(2)}) collective-permute-start(bf16[272,512]{1,0:T(8,128)(2,1)S(1)} %get-tuple-element.23), channel_id=1, source_target_pairs={{0,2},{1,3},{2,0},{3,1},{4,6},{5,7},{6,4},{7,5},{8,10},{9,11},{10,... | collective-permute-start | bytes 835592 | tf_op jit(solution)/shard_map/ppermute | solution.py:142
  13.6 1.4 %collective-permute-start.5 = (bf16[272,512]{1,0:T(8,128)(2,1)S(1)}, bf16[272,512]{1,0:T(8,128)(2,1)S(1)}, u32[]{:S(2)}, u32[]{:S(2)}) collective-permute-start(bf16[272,512]{1,0:T(8,128)(2,1)S(1)} %get-tuple-element.24), channel_id=1, source_target_pairs={{0,3},{1,2},{2,1},{3,0},{4,7},{5,6},{6,5},{7,4},{8,11},{9,10},{10,... | collective-permute-start | bytes 835592 | tf_op jit(solution)/shard_map/ppermute | solution.py:142
  15.1 6.7 %collective-permute-done.6.refs_4_ = bf16[144,512]{1,0:T(8,128)(2,1)S(1)} collective-permute-done((bf16[144,512]{1,0:T(8,128)(2,1)S(1)}, bf16[144,512]{1,0:T(8,128)(2,1)S(1)}, u32[]{:S(2)}, u32[]{:S(2)}) %collective-permute-start.6) | collective-permute-done | bytes 147488 | tf_op jit(solution)/shard_map/ppermute | solution.py:142
  21.7 3.4 %collective-permute-start.8 = (bf16[144,512]{1,0:T(8,128)(2,1)S(1)}, bf16[144,512]{1,0:T(8,128)(2,1)S(1)}, u32[]{:S(2)}, u32[]{:S(2)}) collective-permute-start(bf16[144,512]{1,0:T(8,128)(2,1)S(1)} %get-tuple-element.27), channel_id=1, source_target_pairs={{0,6},{1,7},{2,4},{3,5},{4,2},{5,3},{6,0},{7,1},{8,14},{9,15},{10,... | collective-permute-start | bytes 442376 | tf_op jit(solution)/shard_map/ppermute | solution.py:142
  25.1 0.7 %collective-permute-done.7.refs_5_ = bf16[144,512]{1,0:T(8,128)(2,1)S(1)} collective-permute-done((bf16[144,512]{1,0:T(8,128)(2,1)S(1)}, bf16[144,512]{1,0:T(8,128)(2,1)S(1)}, u32[]{:S(2)}, u32[]{:S(2)}) %collective-permute-start.7) | collective-permute-done | bytes 147488 | tf_op jit(solution)/shard_map/ppermute | solution.py:142
  25.8 3.4 %collective-permute-start.9 = (bf16[144,512]{1,0:T(8,128)(2,1)S(1)}, bf16[144,512]{1,0:T(8,128)(2,1)S(1)}, u32[]{:S(2)}, u32[]{:S(2)}) collective-permute-start(bf16[144,512]{1,0:T(8,128)(2,1)S(1)} %get-tuple-element.28), channel_id=1, source_target_pairs={{0,7},{1,6},{2,5},{3,4},{4,3},{5,2},{6,1},{7,0},{8,15},{9,14},{10,... | collective-permute-start | bytes 442376 | tf_op jit(solution)/shard_map/ppermute | solution.py:142
  29.2 6.0 %collective-permute-done.8.refs_6_ = bf16[144,512]{1,0:T(8,128)(2,1)S(1)} collective-permute-done((bf16[144,512]{1,0:T(8,128)(2,1)S(1)}, bf16[144,512]{1,0:T(8,128)(2,1)S(1)}, u32[]{:S(2)}, u32[]{:S(2)}) %collective-permute-start.8) | collective-permute-done | bytes 147488 | tf_op jit(solution)/shard_map/ppermute | solution.py:142
  35.2 4.0 %collective-permute-done.9.refs_7_ = bf16[144,512]{1,0:T(8,128)(2,1)S(1)} collective-permute-done((bf16[144,512]{1,0:T(8,128)(2,1)S(1)}, bf16[144,512]{1,0:T(8,128)(2,1)S(1)}, u32[]{:S(2)}, u32[]{:S(2)}) %collective-permute-start.9) | collective-permute-done | bytes 147488 | tf_op jit(solution)/shard_map/ppermute | solution.py:142
  39.2 4.2 %sums.1 = (bf16[256,512]{1,0:T(8,128)(2,1)S(1)}, bf16[256,512]{1,0:T(8,128)(2,1)}, bf16[256,512]{1,0:T(8,128)(2,1)}, bf16[256,512]{1,0:T(8,128)(2,1)S(1)}) custom-call(s32[3]{0:T(128)S(1)} %pad_add_fusion.place_ref.refs_0_, bf16[272,512]{1,0:T(8,128)(2,1)S(1)} %get-tuple-element.21.refs_0_, bf16[272,512]{1,0:T(8,128)(2,1)S(1)} %collective-permute-done.3.refs_1_, ...), custom_call_target="tpu_custom_call" | custom-call | flops 1000 | bytes 1000 | tf_op jit(solution)/shard_map/sums/pallas_call | solution.py:157
  43.4 0.8 %collective-permute-start.10 = (bf16[256,512]{1,0:T(8,128)(2,1)}, bf16[256,512]{1,0:T(8,128)(2,1)S(1)}, u32[]{:S(2)}, u32[]{:S(2)}) collective-permute-start(bf16[256,512]{1,0:T(8,128)(2,1)} %get-tuple-element.30), channel_id=1, source_target_pairs={{0,1},{1,0},{2,3},{3,2},{4,5},{5,4},{6,7},{7,6},{8,9},{9,8},{10,11... | collective-permute-start | bytes 786440 | tf_op jit(solution)/shard_map/ppermute | solution.py:142
  44.2 0.9 %collective-permute-start.11 = (bf16[256,512]{1,0:T(8,128)(2,1)}, bf16[256,512]{1,0:T(8,128)(2,1)S(1)}, u32[]{:S(2)}, u32[]{:S(2)}) collective-permute-start(bf16[256,512]{1,0:T(8,128)(2,1)} %get-tuple-element.31), channel_id=1, source_target_pairs={{0,2},{1,3},{2,0},{3,1},{4,6},{5,7},{6,4},{7,5},{8,10},{9,11},{10,... | collective-permute-start | bytes 786440 | tf_op jit(solution)/shard_map/ppermute | solution.py:142
  45.1 1.7 %collective-permute-start.12 = (bf16[256,512]{1,0:T(8,128)(2,1)S(1)}, bf16[256,512]{1,0:T(8,128)(2,1)S(1)}, u32[]{:S(2)}, u32[]{:S(2)}) collective-permute-start(bf16[256,512]{1,0:T(8,128)(2,1)S(1)} %get-tuple-element.32), channel_id=1, source_target_pairs={{0,3},{1,2},{2,1},{3,0},{4,7},{5,6},{6,5},{7,4},{8,11},{9,10},{10,... | collective-permute-start | bytes 786440 | tf_op jit(solution)/shard_map/ppermute | solution.py:142
  46.9 2.7 %lags.1 = f32[32,128]{1,0:T(8,128)} custom-call(s32[3]{0:T(128)S(1)} %pad_add_fusion.place_ref.refs_0_, bf16[272,512]{1,0:T(8,128)(2,1)S(1)} %get-tuple-element.21.refs_0_, bf16[272,512]{1,0:T(8,128)(2,1)S(1)} %collective-permute-done.3.refs_1_, bf16[272,512]{1,0:T(8,128)(2,1)S(1)} %collective-permute-done.4.refs_2_, ...), custom_call_target="tpu_custom_call" | custom-call | flops 1000 | bytes 1000 | tf_op jit(solution)/shard_map/lags/pallas_call | solution.py:157
  49.6 5.1 %all-to-all-start = ((f32[32,1,128]{2,1,0:T(1,128)}), f32[32,1,128]{2,1,0:T(1,128)S(1)}, u32[]{:S(2)}, u32[]{:S(2)}) async-start(f32[32,1,128]{2,1,0:T(1,128)} %bitcast.7), calls=%async_computation | async-start | bytes 32768 | tf_op jit(solution)/shard_map/all_to_all | solution.py:441
  54.7 4.4 %collective-permute-done.12.refs_4_ = bf16[256,512]{1,0:T(8,128)(2,1)S(1)} collective-permute-done((bf16[256,512]{1,0:T(8,128)(2,1)S(1)}, bf16[256,512]{1,0:T(8,128)(2,1)S(1)}, u32[]{:S(2)}, u32[]{:S(2)}) %collective-permute-start.12) | collective-permute-done | bytes 262176 | tf_op jit(solution)/shard_map/ppermute | solution.py:142
  59.2 2.0 %outputs.1 = (bf16[1,128,2048]{2,1,0:T(8,128)(2,1)}, bf16[1,128,2048]{2,1,0:T(8,128)(2,1)}, bf16[1,128,2048]{2,1,0:T(8,128)(2,1)}, bf16[1,128,2048]{2,1,0:T(8,128)(2,1)}) custom-call(s32[3]{0:T(128)S(1)} %pad_add_fusion.place_ref.refs_0_, bf16[256,512]{1,0:T(8,128)(2,1)S(1)} %get-tuple-element.29.refs_1_, ...), custom_call_target="tpu_custom_call" | custom-call | flops 1000 | bytes 1000 | tf_op jit(solution)/shard_map/outputs/pallas_call | solution.py:445
  61.2 0.9 %all-to-all-done = f32[32,1,128]{2,1,0:T(1,128)S(1)} async-done(((f32[32,1,128]{2,1,0:T(1,128)}), f32[32,1,128]{2,1,0:T(1,128)S(1)}, u32[]{:S(2)}, u32[]{:S(2)}) %all-to-all-start) | async-done | bytes 16416 | tf_op jit(solution)/shard_map/all_to_all | solution.py:441
  62.1 1.2 %owned.1 = f32[16,32]{1,0:T(8,128)} custom-call(s32[3]{0:T(128)S(1)} %pad_add_fusion.place_ref.refs_0_, f32[32,128]{1,0:T(8,128)S(1)} %bitcast.13), custom_call_target="tpu_custom_call" | custom-call | flops 1000 | bytes 1000 | tf_op jit(solution)/shard_map/owned/pallas_call | solution.py:157
  (23 shorter events, 1.5 us)
Async XLA Ops:
  0.6 5.2 %collective-permute-start.2 = (bf16[16,32]{1,0:T(8,128)(2,1)}, bf16[16,32]{1,0:T(8,128)(2,1)S(1)}, u32[]{:S(2)}, u32[]{:S(2)}) collective-permute-start(bf16[16,32]{1,0:T(8,128)(2,1)} %bitcast.14), channel_id=1, source_target_pairs={{0,24},{8,0},{16,8},{24,16},{1,25},{9,1},{17,9},{25,17},{2,26},{10... | collective-permute-start | bytes 3080 | tf_op jit(solution)/shard_map/ppermute | solution.py:408
  3.1 3.8 %collective-permute-start.1 = (bf16[16,32]{1,0:T(8,128)(2,1)}, bf16[16,32]{1,0:T(8,128)(2,1)S(1)}, u32[]{:S(2)}, u32[]{:S(2)}) collective-permute-start(bf16[16,32]{1,0:T(8,128)(2,1)} %bitcast.15), channel_id=1, source_target_pairs={{0,16},{8,24},{16,0},{24,8},{1,17},{9,25},{17,1},{25,9},{2,18},{10... | collective-permute-start | bytes 3080 | tf_op jit(solution)/shard_map/ppermute | solution.py:408
  3.7 3.2 %collective-permute-start = (bf16[16,32]{1,0:T(8,128)(2,1)}, bf16[16,32]{1,0:T(8,128)(2,1)S(1)}, u32[]{:S(2)}, u32[]{:S(2)}) collective-permute-start(bf16[16,32]{1,0:T(8,128)(2,1)} %bitcast.16), channel_id=1, source_target_pairs={{0,8},{8,16},{16,24},{24,0},{1,9},{9,17},{17,25},{25,1},{2,10},{10... | collective-permute-start | bytes 3080 | tf_op jit(solution)/shard_map/ppermute | solution.py:408
  5.8 1.2 %copy-start.4 = (bf16[32,16]{0,1:T(8,128)(2,1)S(1)}, bf16[32,16]{0,1:T(8,128)(2,1)}, u32[]{:S(2)}) copy-start(bf16[32,16]{0,1:T(8,128)(2,1)} %param.9) | copy-start | bytes 3076
  7.6 14.1 %collective-permute-start.6 = (bf16[144,512]{1,0:T(8,128)(2,1)S(1)}, bf16[144,512]{1,0:T(8,128)(2,1)S(1)}, u32[]{:S(2)}, u32[]{:S(2)}) collective-permute-start(bf16[144,512]{1,0:T(8,128)(2,1)S(1)} %get-tuple-element.25), channel_id=1, source_target_pairs={{0,4},{1,5},{2,6},{3,7},{4,0},{5,1},{6,2},{7,3},{8,12},{9,13},{10,... | collective-permute-start | bytes 442376 | tf_op jit(solution)/shard_map/ppermute | solution.py:142
  10.3 15.5 %collective-permute-start.7 = (bf16[144,512]{1,0:T(8,128)(2,1)S(1)}, bf16[144,512]{1,0:T(8,128)(2,1)S(1)}, u32[]{:S(2)}, u32[]{:S(2)}) collective-permute-start(bf16[144,512]{1,0:T(8,128)(2,1)S(1)} %get-tuple-element.26), channel_id=1, source_target_pairs={{0,5},{1,4},{2,7},{3,6},{4,1},{5,0},{6,3},{7,2},{8,13},{9,12},{10,... | collective-permute-start | bytes 442376 | tf_op jit(solution)/shard_map/ppermute | solution.py:142
  11.6 27.6 %collective-permute-start.3 = (bf16[272,512]{1,0:T(8,128)(2,1)S(1)}, bf16[272,512]{1,0:T(8,128)(2,1)S(1)}, u32[]{:S(2)}, u32[]{:S(2)}) collective-permute-start(bf16[272,512]{1,0:T(8,128)(2,1)S(1)} %get-tuple-element.22), channel_id=1, source_target_pairs={{0,1},{1,0},{2,3},{3,2},{4,5},{5,4},{6,7},{7,6},{8,9},{9,8},{10,11... | collective-permute-start | bytes 835592 | tf_op jit(solution)/shard_map/ppermute | solution.py:142
  12.1 27.1 %collective-permute-start.4 = (bf16[272,512]{1,0:T(8,128)(2,1)S(1)}, bf16[272,512]{1,0:T(8,128)(2,1)S(1)}, u32[]{:S(2)}, u32[]{:S(2)}) collective-permute-start(bf16[272,512]{1,0:T(8,128)(2,1)S(1)} %get-tuple-element.23), channel_id=1, source_target_pairs={{0,2},{1,3},{2,0},{3,1},{4,6},{5,7},{6,4},{7,5},{8,10},{9,11},{10,... | collective-permute-start | bytes 835592 | tf_op jit(solution)/shard_map/ppermute | solution.py:142
  13.6 25.5 %collective-permute-start.5 = (bf16[272,512]{1,0:T(8,128)(2,1)S(1)}, bf16[272,512]{1,0:T(8,128)(2,1)S(1)}, u32[]{:S(2)}, u32[]{:S(2)}) collective-permute-start(bf16[272,512]{1,0:T(8,128)(2,1)S(1)} %get-tuple-element.24), channel_id=1, source_target_pairs={{0,3},{1,2},{2,1},{3,0},{4,7},{5,6},{6,5},{7,4},{8,11},{9,10},{10,... | collective-permute-start | bytes 835592 | tf_op jit(solution)/shard_map/ppermute | solution.py:142
  21.7 13.4 %collective-permute-start.8 = (bf16[144,512]{1,0:T(8,128)(2,1)S(1)}, bf16[144,512]{1,0:T(8,128)(2,1)S(1)}, u32[]{:S(2)}, u32[]{:S(2)}) collective-permute-start(bf16[144,512]{1,0:T(8,128)(2,1)S(1)} %get-tuple-element.27), channel_id=1, source_target_pairs={{0,6},{1,7},{2,4},{3,5},{4,2},{5,3},{6,0},{7,1},{8,14},{9,15},{10,... | collective-permute-start | bytes 442376 | tf_op jit(solution)/shard_map/ppermute | solution.py:142
  25.8 13.3 %collective-permute-start.9 = (bf16[144,512]{1,0:T(8,128)(2,1)S(1)}, bf16[144,512]{1,0:T(8,128)(2,1)S(1)}, u32[]{:S(2)}, u32[]{:S(2)}) collective-permute-start(bf16[144,512]{1,0:T(8,128)(2,1)S(1)} %get-tuple-element.28), channel_id=1, source_target_pairs={{0,7},{1,6},{2,5},{3,4},{4,3},{5,2},{6,1},{7,0},{8,15},{9,14},{10,... | collective-permute-start | bytes 442376 | tf_op jit(solution)/shard_map/ppermute | solution.py:142
  39.1 20.0 %copy-start.3 = (bf16[1,128,2048]{2,1,0:T(8,128)(2,1)S(1)}, bf16[1,128,2048]{2,1,0:T(8,128)(2,1)}, u32[]{:S(2)}) copy-start(bf16[1,128,2048]{2,1,0:T(8,128)(2,1)} %refs_8_.1) | copy-start | bytes 1572868
  43.3 3.5 %collective-permute-start.13 = (bf16[256,512]{1,0:T(8,128)(2,1)S(1)}, bf16[256,512]{1,0:T(8,128)(2,1)S(1)}, u32[]{:S(2)}, u32[]{:S(2)}) collective-permute-start(bf16[256,512]{1,0:T(8,128)(2,1)S(1)} %get-tuple-element.29.refs_1_), channel_id=1, source_target_pairs={{0,8},{8,0},{16,24},{24,16},{1,9},{9,1},{17,25},{25,17},{2,10},{10... | collective-permute-start | bytes 786440 | tf_op jit(solution)/shard_map/ppermute | solution.py:435
  43.4 11.3 %collective-permute-start.10 = (bf16[256,512]{1,0:T(8,128)(2,1)}, bf16[256,512]{1,0:T(8,128)(2,1)S(1)}, u32[]{:S(2)}, u32[]{:S(2)}) collective-permute-start(bf16[256,512]{1,0:T(8,128)(2,1)} %get-tuple-element.30), channel_id=1, source_target_pairs={{0,1},{1,0},{2,3},{3,2},{4,5},{5,4},{6,7},{7,6},{8,9},{9,8},{10,11... | collective-permute-start | bytes 786440 | tf_op jit(solution)/shard_map/ppermute | solution.py:142
  44.2 10.5 %collective-permute-start.11 = (bf16[256,512]{1,0:T(8,128)(2,1)}, bf16[256,512]{1,0:T(8,128)(2,1)S(1)}, u32[]{:S(2)}, u32[]{:S(2)}) collective-permute-start(bf16[256,512]{1,0:T(8,128)(2,1)} %get-tuple-element.31), channel_id=1, source_target_pairs={{0,2},{1,3},{2,0},{3,1},{4,6},{5,7},{6,4},{7,5},{8,10},{9,11},{10,... | collective-permute-start | bytes 786440 | tf_op jit(solution)/shard_map/ppermute | solution.py:142
  45.1 14.0 %copy-start = (bf16[1,128,2048]{2,1,0:T(8,128)(2,1)S(1)}, bf16[1,128,2048]{2,1,0:T(8,128)(2,1)}, u32[]{:S(2)}) copy-start(bf16[1,128,2048]{2,1,0:T(8,128)(2,1)} %refs_7_.1) | copy-start | bytes 1572868
  45.1 14.0 %copy-start.1 = (bf16[1,128,2048]{2,1,0:T(8,128)(2,1)S(1)}, bf16[1,128,2048]{2,1,0:T(8,128)(2,1)}, u32[]{:S(2)}) copy-start(bf16[1,128,2048]{2,1,0:T(8,128)(2,1)} %refs_5_.1) | copy-start | bytes 1572868
  45.1 14.0 %copy-start.2 = (bf16[1,128,2048]{2,1,0:T(8,128)(2,1)S(1)}, bf16[1,128,2048]{2,1,0:T(8,128)(2,1)}, u32[]{:S(2)}) copy-start(bf16[1,128,2048]{2,1,0:T(8,128)(2,1)} %refs_6_.1) | copy-start | bytes 1572868
  45.1 14.0 %collective-permute-start.12 = (bf16[256,512]{1,0:T(8,128)(2,1)S(1)}, bf16[256,512]{1,0:T(8,128)(2,1)S(1)}, u32[]{:S(2)}, u32[]{:S(2)}) collective-permute-start(bf16[256,512]{1,0:T(8,128)(2,1)S(1)} %get-tuple-element.32), channel_id=1, source_target_pairs={{0,3},{1,2},{2,1},{3,0},{4,7},{5,6},{6,5},{7,4},{8,11},{9,10},{10,... | collective-permute-start | bytes 786440 | tf_op jit(solution)/shard_map/ppermute | solution.py:142
  49.6 12.6 %all-to-all-start = ((f32[32,1,128]{2,1,0:T(1,128)}), f32[32,1,128]{2,1,0:T(1,128)S(1)}, u32[]{:S(2)}, u32[]{:S(2)}) async-start(f32[32,1,128]{2,1,0:T(1,128)} %bitcast.7), calls=%async_computation | async-start | bytes 32768 | tf_op jit(solution)/shard_map/all_to_all | solution.py:441

commit v4 on v3

--- a/solution.py
+++ b/solution.py
@@ -176,30 +176,31 @@
     taps_in, (a_ref, b_ref), refs = refs[:pieces], refs[pieces : pieces + 2], refs[pieces + 2 :]
     a_outs, outs, (taps_ref,) = refs[:quarters], refs[quarters : 2 * quarters], refs[2 * quarters :]
     quarter = place_ref[1]
-    width = a_outs[0].shape[1]
     local = taps_ref.shape[1]
     taps = jnp.concatenate([piece[...].astype(f32) for piece in taps_in], axis=1)
     for i in range(quarters):
         taps_ref[i] = taps[i * local : (i + 1) * local]
     for j in range(quarters):
-        columns = pl.ds(pl.multiple_of((quarter ^ j) * width, width), width)
-        a = a_ref[:, columns]
-        taps = taps_ref[quarter ^ j]
-        taps = jnp.concatenate([taps, jnp.zeros((TAIL - local, BLOCK), f32)], axis=0)
-        tail = jnp.concatenate([taps, jnp.zeros((TAIL, width - BLOCK), f32)], axis=1).astype(bf16)
-        a_outs[j][:BLOCK] = a
-        a_outs[j][BLOCK:] = tail
-        outs[j][:BLOCK] = a
-        outs[j][BLOCK : 2 * BLOCK] = b_ref[:, columns]
-        outs[j][2 * BLOCK :] = tail
-
-
-def bands(quarters, dp_count, place_ref, taps_in, taps_ref, causal_ref, anti_ref):
+        for g in range(local):
+            columns = pl.ds(pl.multiple_of(((quarter ^ j) * local + g) * BLOCK, BLOCK), BLOCK)
+            a = a_ref[:, columns]
+            a_outs[j][g * BLOCK : (g + 1) * BLOCK] = a
+            if j < quarters - 1:
+                outs[j][g * BLOCK : (g + 1) * BLOCK] = a
+                outs[j][(local + g) * BLOCK : (local + g + 1) * BLOCK] = b_ref[:, columns]
+            else:
+                outs[j][g * BLOCK : (g + 1) * BLOCK] = b_ref[:, columns]
+        tail = jnp.concatenate([taps_ref[quarter ^ j], jnp.zeros((TAIL - local, BLOCK), f32)], axis=0).astype(bf16)
+        a_outs[j][local * BLOCK :] = tail
+        outs[j][-TAIL:] = tail
+
+
+def bands(quarters, dp_count, place_ref, taps_in, taps_ref, causal_ref, anti_ref, causal_from, anti_to):
     half, quarter, dp_index = place_ref[0], place_ref[1], place_ref[2]
     local, rows = taps_ref.shape[1:]
     for u in range(2):
         for j in range(quarters):
-            piece = taps_in[u * quarters + j][-TAIL:, :BLOCK].astype(jnp.float32)
+            piece = taps_in[u * quarters + j][-TAIL:].astype(jnp.float32)
             for p in range(dp_count):
                 owner = lax.rem(dp_index + dp_count - p, dp_count) * 2 * quarters + (half ^ u) * quarters + (quarter ^ j)
                 start = p * rows
@@ -211,14 +212,15 @@
         zero = jnp.zeros((BLOCK, BLOCK), jnp.bfloat16)
         count = K // BLOCK
         tiles = [shear[:, m * BLOCK : (m + 1) * BLOCK] for m in range(count)]
-        for b in range(count):
+        for b in range(anti_to // BLOCK):
             columns = slice(b * BLOCK, (b + 1) * BLOCK)
             anti_ref[g, :BLOCK, columns] = tiles[b].astype(jnp.bfloat16)
             anti_ref[g, BLOCK:, columns] = tiles[b - 1].astype(jnp.bfloat16) if b else zero
-        turned = [tile.T.astype(jnp.bfloat16) for tile in tiles] + [zero]
-        for b in range(count):
+        wanted = count - causal_from // BLOCK
+        turned = [tile.T.astype(jnp.bfloat16) for tile in tiles[:wanted]] + [zero]
+        for b in range(count - wanted, count):
             columns = slice(b * BLOCK, (b + 1) * BLOCK)
-            causal_ref[g, :BLOCK, columns] = turned[count - 2 - b]
+            causal_ref[g, :BLOCK, columns] = turned[count - 2 - b] if b < count - 1 else zero
             causal_ref[g, BLOCK:, columns] = turned[count - 1 - b]
 
 
@@ -275,14 +277,19 @@
 
 def gather(quarters, place_ref, ab_in, r_in, a_ref, data_ref):
     half, quarter = place_ref[0], place_ref[1]
+    local = a_ref.shape[2] // BLOCK
     for j in range(quarters):
-        a_ref[quarter ^ j] = ab_in[j][:BLOCK]
-        data_ref[half * quarters + (quarter ^ j)] = ab_in[j][BLOCK : 2 * BLOCK]
-        data_ref[(1 - half) * quarters + (quarter ^ j)] = r_in[j][:BLOCK]
+        b_in, b_row = (ab_in[j], local) if j < quarters - 1 else (ab_in[j + 1], 0)
+        for g in range(local):
+            lanes = slice(g * BLOCK, (g + 1) * BLOCK)
+            a_ref[quarter ^ j, :, lanes] = ab_in[j][g * BLOCK : (g + 1) * BLOCK]
+            b_rows = slice((b_row + g) * BLOCK, (b_row + g + 1) * BLOCK)
+            data_ref[half * quarters + (quarter ^ j), :, lanes] = b_in[b_rows]
+            data_ref[(1 - half) * quarters + (quarter ^ j), :, lanes] = r_in[j][g * BLOCK : (g + 1) * BLOCK]
 
 
 def lags_kernel(quarters, place_ref, *refs):
-    ab_in, r_in, refs = refs[:quarters], refs[quarters : 2 * quarters], refs[2 * quarters :]
+    ab_in, r_in, refs = refs[: quarters + 1], refs[quarters + 1 : 2 * quarters + 1], refs[2 * quarters + 1 :]
     shares_ref, a_ref, data_ref, lines_ref = refs
     gather(quarters, place_ref, ab_in, r_in, a_ref, data_ref)
     half = place_ref[0]
@@ -316,10 +323,11 @@
 
 
 def sums_kernel(quarters, dp_count, place_ref, *refs):
-    ab_in, r_in, outs, refs = refs[:quarters], refs[quarters : 2 * quarters], refs[2 * quarters : 3 * quarters], refs[3 * quarters :]
+    ab_in, r_in, refs = refs[: quarters + 1], refs[quarters + 1 : 2 * quarters + 1], refs[2 * quarters + 1 :]
+    outs, refs = refs[:quarters], refs[quarters:]
     causal_ref, anti_ref, a_ref, data_ref, a_sum_ref, b_sum_ref, taps_ref = refs
     gather(quarters, place_ref, ab_in, r_in, a_ref, data_ref)
-    bands(quarters, dp_count, place_ref, ab_in + r_in, taps_ref, causal_ref, anti_ref)
+    tails = ab_in[:quarters] + r_in
     half, quarter = place_ref[0], place_ref[1]
 
     def work(a_part, a_band, b_part, b_band, first):
@@ -335,10 +343,12 @@
 
     @pl.when(half == 0)
     def lower():
+        bands(quarters, dp_count, place_ref, tails, taps_ref, causal_ref, anti_ref, K // 2, K)
         work(causal_part, causal_ref, anti_part, anti_ref, 0)
 
     @pl.when(half != 0)
     def upper():
+        bands(quarters, dp_count, place_ref, tails, taps_ref, causal_ref, anti_ref, 0, K // 2)
         work(anti_part, anti_ref, causal_part, causal_ref, quarters // 2)
 
     for j in range(quarters):
@@ -360,34 +370,51 @@
             out_ref[q * local + g : q * local + g + 1] = part[q : q + 1]
 
 
-def outputs_kernel(quarters, place_ref, *refs):
+def outputs_kernel(js, place_ref, *refs):
     f32, bf16 = jnp.float32, jnp.bfloat16
-    back, inputs, refs = refs[:quarters], refs[quarters : quarters + 4], refs[quarters + 4 :]
-    outputs, results, sem = refs[:4], refs[4:8], refs[8]
+    count = len(js)
+    back, inputs = refs[:count], refs[count : count + 4]
+    outputs, results, sem = refs[-9:-5], refs[-5:-1], refs[-1]
     half, quarter = place_ref[0], place_ref[1]
     width = back[0].shape[1]
 
-    def copies(j, columns):
-        return [
-            pltpu.make_async_copy(store.at[j], target.at[0, :, columns], sem.at[j, i])
-            for i, (store, target) in enumerate(zip(results, outputs))
-        ]
-
     def place(j):
         return pl.ds(pl.multiple_of((quarter ^ j) * width, width), width)
 
-    for j in range(quarters):
-        columns = place(j)
+    def copies(i):
+        return [
+            pltpu.make_async_copy(store.at[i], target.at[0, :, place(js[i])], sem.at[i, k])
+            for k, (store, target) in enumerate(zip(results, outputs))
+        ]
+
+    for i in range(count):
+        columns = place(js[i])
         pre, post, values, cot = [source[0, :, columns].astype(f32) for source in inputs]
-        a_sum, b_sum = back[j][:BLOCK].astype(f32), back[j][BLOCK:].astype(f32)
+        a_sum, b_sum = back[i][:BLOCK].astype(f32), back[i][BLOCK:].astype(f32)
         convolved, carried = jnp.where(half == 0, a_sum, b_sum), jnp.where(half == 0, b_sum, a_sum)
         for result, value in zip(results, (post * convolved, carried * values, cot * convolved, carried * pre)):
-            result[j] = value.astype(bf16)
-        for copy in copies(j, columns):
+            result[i] = value.astype(bf16)
+        for copy in copies(i):
             copy.start()
-    for j in range(quarters):
-        for copy in copies(j, place(j)):
+    for i in range(count):
+        for copy in copies(i):
             copy.wait()
+
+
+def gate_outputs(js, place, back, gates, earlier=()):
+    hbm = [pl.BlockSpec(memory_space=pltpu.HBM)] * 4
+    store = pltpu.VMEM((len(js), BLOCK, back[0].shape[1]), jnp.bfloat16)
+    return pl.pallas_call(
+        lambda *refs: outputs_kernel(js, *refs),
+        in_specs=[pl.BlockSpec(memory_space=pltpu.SMEM)] + vmem_specs(len(js) + 4) + hbm[: len(earlier)],
+        out_specs=hbm,
+        out_shape=[jax.ShapeDtypeStruct(gates[0].shape, jnp.bfloat16)] * 4,
+        input_output_aliases={1 + len(js) + 4 + k: k for k in range(len(earlier))},
+        scratch_shapes=[store] * 4 + [pltpu.SemaphoreType.DMA((len(js), 4))],
+        compiler_params=pltpu.CompilerParams(vmem_limit_bytes=20 * 1024 * 1024),
+        cost_estimate=pl.CostEstimate(flops=1000, bytes_accessed=1000, transcendentals=0),
+        name="outputs",
+    )(place, *[back[j] for j in js], *gates, *earlier)
 
 
 def swapped(pre_gate, post_gate, values, cotangent, filters):
@@ -413,16 +440,17 @@
     gated = (cotangent[0].astype(f32) * post_gate[0]).astype(bf16)
     a, b = jnp.where(lower, mixed, gated), jnp.where(lower, gated, mixed)
     store = pltpu.VMEM((quarters, BLOCK, width), bf16)
-    short = jax.ShapeDtypeStruct((BLOCK + TAIL, width), bf16)
-    message = jax.ShapeDtypeStruct((2 * BLOCK + TAIL, width), bf16)
+    short = jax.ShapeDtypeStruct((local * BLOCK + TAIL, BLOCK), bf16)
+    message = jax.ShapeDtypeStruct((2 * local * BLOCK + TAIL, BLOCK), bf16)
     chunks = call(
         lambda *refs: pack_kernel(quarters, dp_count, *refs), "pack", place, pieces + [a, b],
-        [short] * quarters + [message] * quarters, [pltpu.VMEM((quarters, local, BLOCK), f32)],
+        [short] * quarters + [message] * (quarters - 1) + [short], [pltpu.VMEM((quarters, local, BLOCK), f32)],
         flops=1000, nbytes=1000,
     )
     a_own, ab_own = chunks[:quarters], chunks[quarters:]
     r_in = [swap(a_own[j], quarters + j) for j in range(quarters)]
-    ab_in = [ab_own[0]] + [swap(ab_own[j], j) for j in range(1, quarters)]
+    ab_in = [ab_own[0]] + [swap(ab_own[j], j) for j in range(1, quarters - 1)]
+    ab_in += [swap(a_own[-1], quarters - 1), swap(ab_own[-1], quarters - 1)]
 
     band = pltpu.VMEM((local, 2 * BLOCK, K), bf16)
     store = pltpu.VMEM((quarters, BLOCK, width), bf16)
@@ -440,18 +468,9 @@
     )
     arrived = lax.all_to_all(shares, every, 0, 0, tiled=True)
 
-    shape = jax.ShapeDtypeStruct(pre_gate.shape, bf16)
-    hbm = [pl.BlockSpec(memory_space=pltpu.HBM)] * 4
-    output, grad_pre, grad_post, grad_values = pl.pallas_call(
-        lambda *refs: outputs_kernel(quarters, *refs),
-        in_specs=[pl.BlockSpec(memory_space=pltpu.SMEM)] + vmem_specs(quarters + 4),
-        out_specs=hbm,
-        out_shape=[shape] * 4,
-        scratch_shapes=[store] * 4 + [pltpu.SemaphoreType.DMA((quarters, 4))],
-        compiler_params=pltpu.CompilerParams(vmem_limit_bytes=20 * 1024 * 1024),
-        cost_estimate=pl.CostEstimate(flops=1000, bytes_accessed=1000, transcendentals=0),
-        name="outputs",
-    )(place, *back, *gates)
+    early, last = list(range(quarters - 1)), [quarters - 1]
+    outputs = gate_outputs(early, place, back, gates)
+    output, grad_pre, grad_post, grad_values = gate_outputs(last, place, back, gates, outputs)
     total_tokens = dp_count * parts * pre_gate.shape[1] * (channels // groups)
     (mine,) = call(
         lambda *refs: owned_kernel(1.0 / float(total_tokens**0.5), *refs), "owned", place, [arrived],

time: 63.5 us -> 61.9 us (0.975)
  starting transfers between devices: 26 us -> 24 us
  Pallas kernels: 10.9 us -> 12.1 us
  waiting for transfers between devices: 23.8 us -> 22.8 us
    ppermute x10 -> x11, starting transfers between devices: 17.7 us -> 16.3 us  [swap(): return lax.ppermute(chunk, 'seq', [(i, i ^ flip) for i in range(count)])]
    pallas_call x1 -> x2, Pallas kernels: 2.04 us -> 3.26 us  [gate_outputs(): pl.pallas_call(lambda *refs: outputs_kernel(js, *refs), in_specs=[pl.Bloc...]
    ppermute x10 -> x11, waiting for transfers between devices: 21.8 us -> 20.6 us  [swap(): return lax.ppermute(chunk, 'seq', [(i, i ^ flip) for i in range(count)])]
  transfers between devices with their start and end apart: 15 -> 16, of which waited for: 8 -> 10; matrix products, arithmetic and copies ran while one was open for 3% -> 3% of each run, Pallas kernels for 8% -> 10%
where the time goes in v4:
time: 61.9 us; the launch traced here: 61.7 us
  starting transfers between devices  24 us (39%)
  waiting for transfers between devices  22.8 us (37%)
  Pallas kernels  12.1 us (20%)
  other arithmetic  1.98 us (3%)
  between operations  0.75 us (1%)
    ppermute x11, waiting for transfers between devices, swap(): return lax.ppermute(chunk, 'seq', [(i, i ^ flip) for i in range(count)])  20.6 us
    ppermute x11, starting transfers between devices, swap(): return lax.ppermute(chunk, 'seq', [(i, i ^ flip) for i in range(count)])  16.3 us
    pallas_call x4, Pallas kernels, call(): pl.pallas_call(body, in_specs=[pl.BlockSpec(memory_space=pltpu.SMEM)] + v...  8.86 us
    all_to_all x1, starting transfers between devices, swapped(): arrived = lax.all_to_all(shares, every, 0, 0, tiled=True)  4.53 us
    pallas_call x2, Pallas kernels, gate_outputs(): pl.pallas_call(lambda *refs: outputs_kernel(js, *refs), in_specs=[pl.Bloc...  3.26 us
    ppermute x3, starting transfers between devices, swapped(): lax.ppermute(taps, 'dp', [(i, (i + p) % dp_count) for i in range(dp_count)])  3.23 us
    select_n x1, other arithmetic, swapped(): a, b = (jnp.where(lower, mixed, gated), jnp.where(lower, gated, mixed))  1.9 us
  transfers between devices with their start and end apart: 16, of which 10 were waited for; matrix products, arithmetic and copies ran while one was open for 3% of the time, Pallas kernels for 10%

profile of v4, /device:TPU:0, one launch (start us, length us, event | category | flops | bytes accessed | tf_op | source)
XLA Modules:
  0.0 61.7 jit_solution(16922721201433417566)
XLA Ops:
  0.6 2.4 %collective-permute-start.2 = (bf16[16,32]{1,0:T(8,128)(2,1)}, bf16[16,32]{1,0:T(8,128)(2,1)S(1)}, u32[]{:S(2)}, u32[]{:S(2)}) collective-permute-start(bf16[16,32]{1,0:T(8,128)(2,1)} %bitcast.14), channel_id=1, source_target_pairs={{0,24},{8,0},{16,8},{24,16},{1,25},{9,1},{17,9},{25,17},{2,26},{10... | collective-permute-start | bytes 3080 | tf_op jit(solution)/shard_map/ppermute | solution.py:435
  3.9 1.9 %select_bitcast_fusion = (bf16[128,2048]{1,0:T(8,128)(2,1)S(1)}, bf16[128,2048]{1,0:T(8,128)(2,1)S(1)}) fusion(pred[]{:T(512)S(6)} %lt.10, bf16[1,128,2048]{2,1,0:T(8,128)(2,1)} %refs_4_.3, bf16[1,128,2048]{2,1,0:T(8,128)(2,1)} %refs_2_.1, bf16[1,128,2048]{2,1,0:T(8,128)(2,1)} %refs_3_.1, bf16[1,128,2048]{2,1,0:T(8,128)(2,1)} %refs_5_.3), kind=kLoop, calls=%fused_computation.2 | loop fusion | flops 2621440 | bytes 3145729 | tf_op jit(solution)/shard_map/jit(_where)/select_n | solution.py:441
  5.9 1.0 %collective-permute-done.1.refs_2_ = bf16[16,32]{1,0:T(8,128)(2,1)S(1)} collective-permute-done((bf16[16,32]{1,0:T(8,128)(2,1)}, bf16[16,32]{1,0:T(8,128)(2,1)S(1)}, u32[]{:S(2)}, u32[]{:S(2)}) %collective-permute-start.1) | collective-permute-done | bytes 1056 | tf_op jit(solution)/shard_map/ppermute | solution.py:435
  6.9 0.8 %pack.1 = (bf16[528,128]{1,0:T(8,128)(2,1)S(1)}, bf16[528,128]{1,0:T(8,128)(2,1)S(1)}, bf16[528,128]{1,0:T(8,128)(2,1)S(1)}, bf16[528,128]{1,0:T(8,128)(2,1)S(1)...) custom-call(s32[3]{0:T(128)S(1)} %pad_add_fusion.place_ref.refs_0_, ...), custom_call_target="tpu_custom_call" | custom-call | flops 1000 | bytes 1000 | tf_op jit(solution)/shard_map/pack/pallas_call | solution.py:157
  7.8 2.6 %collective-permute-start.6 = (bf16[528,128]{1,0:T(8,128)(2,1)S(1)}, bf16[528,128]{1,0:T(8,128)(2,1)S(1)}, u32[]{:S(2)}, u32[]{:S(2)}) collective-permute-start(bf16[528,128]{1,0:T(8,128)(2,1)S(1)} %get-tuple-element.29), channel_id=1, source_target_pairs={{0,3},{1,2},{2,1},{3,0},{4,7},{5,6},{6,5},{7,4},{8,11},{9,10},{10,... | collective-permute-start | bytes 405512 | tf_op jit(solution)/shard_map/ppermute | solution.py:142
  10.4 2.6 %collective-permute-start.7 = (bf16[528,128]{1,0:T(8,128)(2,1)S(1)}, bf16[528,128]{1,0:T(8,128)(2,1)S(1)}, u32[]{:S(2)}, u32[]{:S(2)}) collective-permute-start(bf16[528,128]{1,0:T(8,128)(2,1)S(1)} %get-tuple-element.30), channel_id=1, source_target_pairs={{0,4},{1,5},{2,6},{3,7},{4,0},{5,1},{6,2},{7,3},{8,12},{9,13},{10,... | collective-permute-start | bytes 405512 | tf_op jit(solution)/shard_map/ppermute | solution.py:142
  13.2 1.5 %collective-permute-start.3 = (bf16[1040,128]{1,0:T(8,128)(2,1)S(1)}, bf16[1040,128]{1,0:T(8,128)(2,1)S(1)}, u32[]{:S(2)}, u32[]{:S(2)}) collective-permute-start(bf16[1040,128]{1,0:T(8,128)(2,1)S(1)} %get-tuple-element.26), channel_id=1, source_target_pairs={{0,1},{1,0},{2,3},{3,2},{4,5},{5,4},{6,7},{7,6},{8,9},{9,8},{10,11... | collective-permute-start | bytes 798728 | tf_op jit(solution)/shard_map/ppermute | solution.py:142
  15.2 2.8 %collective-permute-done.6.refs_4_ = bf16[528,128]{1,0:T(8,128)(2,1)S(1)} collective-permute-done((bf16[528,128]{1,0:T(8,128)(2,1)S(1)}, bf16[528,128]{1,0:T(8,128)(2,1)S(1)}, u32[]{:S(2)}, u32[]{:S(2)}) %collective-permute-start.6) | collective-permute-done | bytes 135200 | tf_op jit(solution)/shard_map/ppermute | solution.py:142
  18.0 2.5 %collective-permute-start.9 = (bf16[528,128]{1,0:T(8,128)(2,1)S(1)}, bf16[528,128]{1,0:T(8,128)(2,1)S(1)}, u32[]{:S(2)}, u32[]{:S(2)}) collective-permute-start(bf16[528,128]{1,0:T(8,128)(2,1)S(1)} %get-tuple-element.32), channel_id=1, source_target_pairs={{0,6},{1,7},{2,4},{3,5},{4,2},{5,3},{6,0},{7,1},{8,14},{9,15},{10,... | collective-permute-start | bytes 405512 | tf_op jit(solution)/shard_map/ppermute | solution.py:142
  20.5 3.1 %collective-permute-done.7.refs_5_ = bf16[528,128]{1,0:T(8,128)(2,1)S(1)} collective-permute-done((bf16[528,128]{1,0:T(8,128)(2,1)S(1)}, bf16[528,128]{1,0:T(8,128)(2,1)S(1)}, u32[]{:S(2)}, u32[]{:S(2)}) %collective-permute-start.7) | collective-permute-done | bytes 135200 | tf_op jit(solution)/shard_map/ppermute | solution.py:142
  23.6 2.4 %collective-permute-start.10 = (bf16[528,128]{1,0:T(8,128)(2,1)S(1)}, bf16[528,128]{1,0:T(8,128)(2,1)S(1)}, u32[]{:S(2)}, u32[]{:S(2)}) collective-permute-start(bf16[528,128]{1,0:T(8,128)(2,1)S(1)} %get-tuple-element.28), channel_id=1, source_target_pairs={{0,7},{1,6},{2,5},{3,4},{4,3},{5,2},{6,1},{7,0},{8,15},{9,14},{10,... | collective-permute-start | bytes 405512 | tf_op jit(solution)/shard_map/ppermute | solution.py:142
  26.1 5.8 %collective-permute-done.9.refs_7_ = bf16[528,128]{1,0:T(8,128)(2,1)S(1)} collective-permute-done((bf16[528,128]{1,0:T(8,128)(2,1)S(1)}, bf16[528,128]{1,0:T(8,128)(2,1)S(1)}, u32[]{:S(2)}, u32[]{:S(2)}) %collective-permute-start.9) | collective-permute-done | bytes 135200 | tf_op jit(solution)/shard_map/ppermute | solution.py:142
  32.0 2.7 %collective-permute-done.10.refs_8_ = bf16[528,128]{1,0:T(8,128)(2,1)S(1)} collective-permute-done((bf16[528,128]{1,0:T(8,128)(2,1)S(1)}, bf16[528,128]{1,0:T(8,128)(2,1)S(1)}, u32[]{:S(2)}, u32[]{:S(2)}) %collective-permute-start.10) | collective-permute-done | bytes 135200 | tf_op jit(solution)/shard_map/ppermute | solution.py:142
  34.7 2.8 %collective-permute-done.5.refs_3_ = bf16[528,128]{1,0:T(8,128)(2,1)S(1)} collective-permute-done((bf16[528,128]{1,0:T(8,128)(2,1)S(1)}, bf16[528,128]{1,0:T(8,128)(2,1)S(1)}, u32[]{:S(2)}, u32[]{:S(2)}) %collective-permute-start.5) | collective-permute-done | bytes 135200 | tf_op jit(solution)/shard_map/ppermute | solution.py:142
  37.5 3.9 %sums.1 = (bf16[256,512]{1,0:T(8,128)(2,1)S(1)}, bf16[256,512]{1,0:T(8,128)(2,1)}, bf16[256,512]{1,0:T(8,128)(2,1)}, bf16[256,512]{1,0:T(8,128)(2,1)S(1)}) custom-call(s32[3]{0:T(128)S(1)} %pad_add_fusion.place_ref.refs_0_, bf16[1040,128]{1,0:T(8,128)(2,1)S(1)} %get-tuple-element.25.refs_0_, bf16[1040,128]{1,0:T(8,128)(2,1)S(1)} %collective-permute-done.3.refs_1_, ...), custom_call_target="tpu_custom_call" | custom-call | flops 1000 | bytes 1000 | tf_op jit(solution)/shard_map/sums/pallas_call | solution.py:157
  41.5 1.5 %collective-permute-start.12 = (bf16[256,512]{1,0:T(8,128)(2,1)}, bf16[256,512]{1,0:T(8,128)(2,1)S(1)}, u32[]{:S(2)}, u32[]{:S(2)}) collective-permute-start(bf16[256,512]{1,0:T(8,128)(2,1)} %get-tuple-element.35), channel_id=1, source_target_pairs={{0,1},{1,0},{2,3},{3,2},{4,5},{5,4},{6,7},{7,6},{8,9},{9,8},{10,11... | collective-permute-start | bytes 786440 | tf_op jit(solution)/shard_map/ppermute | solution.py:142
  43.0 2.3 %collective-permute-start.13 = (bf16[256,512]{1,0:T(8,128)(2,1)}, bf16[256,512]{1,0:T(8,128)(2,1)S(1)}, u32[]{:S(2)}, u32[]{:S(2)}) collective-permute-start(bf16[256,512]{1,0:T(8,128)(2,1)} %get-tuple-element.36), channel_id=1, source_target_pairs={{0,2},{1,3},{2,0},{3,1},{4,6},{5,7},{6,4},{7,5},{8,10},{9,11},{10,... | collective-permute-start | bytes 786440 | tf_op jit(solution)/shard_map/ppermute | solution.py:142
  45.4 2.9 %lags.1 = f32[32,128]{1,0:T(8,128)} custom-call(s32[3]{0:T(128)S(1)} %pad_add_fusion.place_ref.refs_0_, bf16[1040,128]{1,0:T(8,128)(2,1)S(1)} %get-tuple-element.25.refs_0_, bf16[1040,128]{1,0:T(8,128)(2,1)S(1)} %collective-permute-done.3.refs_1_, bf16[1040,128]{1,0:T(8,128)(2,1)S(1)} %collective-permute-done.4.refs_2_, ...), custom_call_target="tpu_custom_call" | custom-call | flops 1000 | bytes 1000 | tf_op jit(solution)/shard_map/lags/pallas_call | solution.py:157
  48.3 4.5 %all-to-all-start = ((f32[32,1,128]{2,1,0:T(1,128)}), f32[32,1,128]{2,1,0:T(1,128)S(1)}, u32[]{:S(2)}, u32[]{:S(2)}) async-start(f32[32,1,128]{2,1,0:T(1,128)} %bitcast.7), calls=%async_computation | async-start | bytes 32768 | tf_op jit(solution)/shard_map/all_to_all | solution.py:469
  52.9 1.8 %outputs.2 = (bf16[1,128,2048]{2,1,0:T(8,128)(2,1)}, bf16[1,128,2048]{2,1,0:T(8,128)(2,1)}, bf16[1,128,2048]{2,1,0:T(8,128)(2,1)}, bf16[1,128,2048]{2,1,0:T(8,128)(2,1)}) custom-call(s32[3]{0:T(128)S(1)} %pad_add_fusion.place_ref.refs_0_, bf16[256,512]{1,0:T(8,128)(2,1)S(1)} %get-tuple-element.34.refs_1_, ...), custom_call_target="tpu_custom_call" | custom-call | flops 1000 | bytes 1000 | tf_op jit(solution)/shard_map/outputs/pallas_call | solution.py:407
  54.7 3.2 %collective-permute-done.11.refs_1_ = bf16[256,512]{1,0:T(8,128)(2,1)S(1)} collective-permute-done((bf16[256,512]{1,0:T(8,128)(2,1)S(1)}, bf16[256,512]{1,0:T(8,128)(2,1)S(1)}, u32[]{:S(2)}, u32[]{:S(2)}) %collective-permute-start.11) | collective-permute-done | bytes 262176 | tf_op jit(solution)/shard_map/ppermute | solution.py:142
  57.9 1.4 %outputs.3 = (bf16[1,128,2048]{2,1,0:T(8,128)(2,1)}, bf16[1,128,2048]{2,1,0:T(8,128)(2,1)}, bf16[1,128,2048]{2,1,0:T(8,128)(2,1)}, bf16[1,128,2048]{2,1,0:T(8,128)(2,1)}) custom-call(s32[3]{0:T(128)S(1)} %pad_add_fusion.place_ref.refs_0_, ...), custom_call_target="tpu_custom_call", output_to_operand_aliasing={{0}: (6, {}), {1}: (7, {}), {2}: (8, {}), {3}: (9, {})} | custom-call | flops 1000 | bytes 1000 | tf_op jit(solution)/shard_map/outputs/pallas_call | solution.py:407
  59.3 1.1 %all-to-all-done = f32[32,1,128]{2,1,0:T(1,128)S(1)} async-done(((f32[32,1,128]{2,1,0:T(1,128)}), f32[32,1,128]{2,1,0:T(1,128)S(1)}, u32[]{:S(2)}, u32[]{:S(2)}) %all-to-all-start) | async-done | bytes 16416 | tf_op jit(solution)/shard_map/all_to_all | solution.py:469
  60.5 1.2 %owned.1 = f32[16,32]{1,0:T(8,128)} custom-call(s32[3]{0:T(128)S(1)} %pad_add_fusion.place_ref.refs_0_, f32[32,128]{1,0:T(8,128)S(1)} %bitcast.13), custom_call_target="tpu_custom_call" | custom-call | flops 1000 | bytes 1000 | tf_op jit(solution)/shard_map/owned/pallas_call | solution.py:157
  (26 shorter events, 2.0 us)
Async XLA Ops:
  0.6 5.2 %collective-permute-start.2 = (bf16[16,32]{1,0:T(8,128)(2,1)}, bf16[16,32]{1,0:T(8,128)(2,1)S(1)}, u32[]{:S(2)}, u32[]{:S(2)}) collective-permute-start(bf16[16,32]{1,0:T(8,128)(2,1)} %bitcast.14), channel_id=1, source_target_pairs={{0,24},{8,0},{16,8},{24,16},{1,25},{9,1},{17,9},{25,17},{2,26},{10... | collective-permute-start | bytes 3080 | tf_op jit(solution)/shard_map/ppermute | solution.py:435
  3.1 3.8 %collective-permute-start.1 = (bf16[16,32]{1,0:T(8,128)(2,1)}, bf16[16,32]{1,0:T(8,128)(2,1)S(1)}, u32[]{:S(2)}, u32[]{:S(2)}) collective-permute-start(bf16[16,32]{1,0:T(8,128)(2,1)} %bitcast.15), channel_id=1, source_target_pairs={{0,16},{8,24},{16,0},{24,8},{1,17},{9,25},{17,1},{25,9},{2,18},{10... | collective-permute-start | bytes 3080 | tf_op jit(solution)/shard_map/ppermute | solution.py:435
  3.7 3.2 %collective-permute-start = (bf16[16,32]{1,0:T(8,128)(2,1)}, bf16[16,32]{1,0:T(8,128)(2,1)S(1)}, u32[]{:S(2)}, u32[]{:S(2)}) collective-permute-start(bf16[16,32]{1,0:T(8,128)(2,1)} %bitcast.16), channel_id=1, source_target_pairs={{0,8},{8,16},{16,24},{24,0},{1,9},{9,17},{17,25},{25,1},{2,10},{10... | collective-permute-start | bytes 3080 | tf_op jit(solution)/shard_map/ppermute | solution.py:435
  5.8 1.2 %copy-start.4 = (bf16[32,16]{0,1:T(8,128)(2,1)S(1)}, bf16[32,16]{0,1:T(8,128)(2,1)}, u32[]{:S(2)}) copy-start(bf16[32,16]{0,1:T(8,128)(2,1)} %param.9) | copy-start | bytes 3076
  7.8 10.2 %collective-permute-start.6 = (bf16[528,128]{1,0:T(8,128)(2,1)S(1)}, bf16[528,128]{1,0:T(8,128)(2,1)S(1)}, u32[]{:S(2)}, u32[]{:S(2)}) collective-permute-start(bf16[528,128]{1,0:T(8,128)(2,1)S(1)} %get-tuple-element.29), channel_id=1, source_target_pairs={{0,3},{1,2},{2,1},{3,0},{4,7},{5,6},{6,5},{7,4},{8,11},{9,10},{10,... | collective-permute-start | bytes 405512 | tf_op jit(solution)/shard_map/ppermute | solution.py:142
  10.4 13.2 %collective-permute-start.7 = (bf16[528,128]{1,0:T(8,128)(2,1)S(1)}, bf16[528,128]{1,0:T(8,128)(2,1)S(1)}, u32[]{:S(2)}, u32[]{:S(2)}) collective-permute-start(bf16[528,128]{1,0:T(8,128)(2,1)S(1)} %get-tuple-element.30), channel_id=1, source_target_pairs={{0,4},{1,5},{2,6},{3,7},{4,0},{5,1},{6,2},{7,3},{8,12},{9,13},{10,... | collective-permute-start | bytes 405512 | tf_op jit(solution)/shard_map/ppermute | solution.py:142
  13.0 13.2 %collective-permute-start.8 = (bf16[528,128]{1,0:T(8,128)(2,1)S(1)}, bf16[528,128]{1,0:T(8,128)(2,1)S(1)}, u32[]{:S(2)}, u32[]{:S(2)}) collective-permute-start(bf16[528,128]{1,0:T(8,128)(2,1)S(1)} %get-tuple-element.31), channel_id=1, source_target_pairs={{0,5},{1,4},{2,7},{3,6},{4,1},{5,0},{6,3},{7,2},{8,13},{9,12},{10,... | collective-permute-start | bytes 405512 | tf_op jit(solution)/shard_map/ppermute | solution.py:142
  13.2 24.3 %collective-permute-start.3 = (bf16[1040,128]{1,0:T(8,128)(2,1)S(1)}, bf16[1040,128]{1,0:T(8,128)(2,1)S(1)}, u32[]{:S(2)}, u32[]{:S(2)}) collective-permute-start(bf16[1040,128]{1,0:T(8,128)(2,1)S(1)} %get-tuple-element.26), channel_id=1, source_target_pairs={{0,1},{1,0},{2,3},{3,2},{4,5},{5,4},{6,7},{7,6},{8,9},{9,8},{10,11... | collective-permute-start | bytes 798728 | tf_op jit(solution)/shard_map/ppermute | solution.py:142
  14.8 22.7 %collective-permute-start.4 = (bf16[1040,128]{1,0:T(8,128)(2,1)S(1)}, bf16[1040,128]{1,0:T(8,128)(2,1)S(1)}, u32[]{:S(2)}, u32[]{:S(2)}) collective-permute-start(bf16[1040,128]{1,0:T(8,128)(2,1)S(1)} %get-tuple-element.27), channel_id=1, source_target_pairs={{0,2},{1,3},{2,0},{3,1},{4,6},{5,7},{6,4},{7,5},{8,10},{9,11},{10,... | collective-permute-start | bytes 798728 | tf_op jit(solution)/shard_map/ppermute | solution.py:142
  18.0 14.0 %collective-permute-start.9 = (bf16[528,128]{1,0:T(8,128)(2,1)S(1)}, bf16[528,128]{1,0:T(8,128)(2,1)S(1)}, u32[]{:S(2)}, u32[]{:S(2)}) collective-permute-start(bf16[528,128]{1,0:T(8,128)(2,1)S(1)} %get-tuple-element.32), channel_id=1, source_target_pairs={{0,6},{1,7},{2,4},{3,5},{4,2},{5,3},{6,0},{7,1},{8,14},{9,15},{10,... | collective-permute-start | bytes 405512 | tf_op jit(solution)/shard_map/ppermute | solution.py:142
  23.6 11.1 %collective-permute-start.10 = (bf16[528,128]{1,0:T(8,128)(2,1)S(1)}, bf16[528,128]{1,0:T(8,128)(2,1)S(1)}, u32[]{:S(2)}, u32[]{:S(2)}) collective-permute-start(bf16[528,128]{1,0:T(8,128)(2,1)S(1)} %get-tuple-element.28), channel_id=1, source_target_pairs={{0,7},{1,6},{2,5},{3,4},{4,3},{5,2},{6,1},{7,0},{8,15},{9,14},{10,... | collective-permute-start | bytes 405512 | tf_op jit(solution)/shard_map/ppermute | solution.py:142
  26.1 11.4 %collective-permute-start.5 = (bf16[528,128]{1,0:T(8,128)(2,1)S(1)}, bf16[528,128]{1,0:T(8,128)(2,1)S(1)}, u32[]{:S(2)}, u32[]{:S(2)}) collective-permute-start(bf16[528,128]{1,0:T(8,128)(2,1)S(1)} %get-tuple-element.28), channel_id=1, source_target_pairs={{0,3},{1,2},{2,1},{3,0},{4,7},{5,6},{6,5},{7,4},{8,11},{9,10},{10,... | collective-permute-start | bytes 405512 | tf_op jit(solution)/shard_map/ppermute | solution.py:142
  37.5 15.3 %copy-start.3 = (bf16[1,128,2048]{2,1,0:T(8,128)(2,1)S(1)}, bf16[1,128,2048]{2,1,0:T(8,128)(2,1)}, u32[]{:S(2)}) copy-start(bf16[1,128,2048]{2,1,0:T(8,128)(2,1)} %refs_5_.3) | copy-start | bytes 1572868
  41.4 4.0 %collective-permute-start.14 = (bf16[256,512]{1,0:T(8,128)(2,1)S(1)}, bf16[256,512]{1,0:T(8,128)(2,1)S(1)}, u32[]{:S(2)}, u32[]{:S(2)}) collective-permute-start(bf16[256,512]{1,0:T(8,128)(2,1)S(1)} %get-tuple-element.34.refs_1_), channel_id=1, source_target_pairs={{0,8},{8,0},{16,24},{24,16},{1,9},{9,1},{17,25},{25,17},{2,10},{10... | collective-permute-start | bytes 786440 | tf_op jit(solution)/shard_map/ppermute | solution.py:463
  41.5 11.4 %collective-permute-start.12 = (bf16[256,512]{1,0:T(8,128)(2,1)}, bf16[256,512]{1,0:T(8,128)(2,1)S(1)}, u32[]{:S(2)}, u32[]{:S(2)}) collective-permute-start(bf16[256,512]{1,0:T(8,128)(2,1)} %get-tuple-element.35), channel_id=1, source_target_pairs={{0,1},{1,0},{2,3},{3,2},{4,5},{5,4},{6,7},{7,6},{8,9},{9,8},{10,11... | collective-permute-start | bytes 786440 | tf_op jit(solution)/shard_map/ppermute | solution.py:142
  43.0 9.9 %collective-permute-start.13 = (bf16[256,512]{1,0:T(8,128)(2,1)}, bf16[256,512]{1,0:T(8,128)(2,1)S(1)}, u32[]{:S(2)}, u32[]{:S(2)}) collective-permute-start(bf16[256,512]{1,0:T(8,128)(2,1)} %get-tuple-element.36), channel_id=1, source_target_pairs={{0,2},{1,3},{2,0},{3,1},{4,6},{5,7},{6,4},{7,5},{8,10},{9,11},{10,... | collective-permute-start | bytes 786440 | tf_op jit(solution)/shard_map/ppermute | solution.py:142
  45.3 7.6 %copy-start = (bf16[1,128,2048]{2,1,0:T(8,128)(2,1)S(1)}, bf16[1,128,2048]{2,1,0:T(8,128)(2,1)}, u32[]{:S(2)}) copy-start(bf16[1,128,2048]{2,1,0:T(8,128)(2,1)} %refs_4_.3) | copy-start | bytes 1572868
  45.3 7.6 %copy-start.1 = (bf16[1,128,2048]{2,1,0:T(8,128)(2,1)S(1)}, bf16[1,128,2048]{2,1,0:T(8,128)(2,1)}, u32[]{:S(2)}) copy-start(bf16[1,128,2048]{2,1,0:T(8,128)(2,1)} %refs_2_.1) | copy-start | bytes 1572868
  45.3 7.6 %copy-start.2 = (bf16[1,128,2048]{2,1,0:T(8,128)(2,1)S(1)}, bf16[1,128,2048]{2,1,0:T(8,128)(2,1)}, u32[]{:S(2)}) copy-start(bf16[1,128,2048]{2,1,0:T(8,128)(2,1)} %refs_3_.1) | copy-start | bytes 1572868
  45.3 12.6 %collective-permute-start.11 = (bf16[256,512]{1,0:T(8,128)(2,1)S(1)}, bf16[256,512]{1,0:T(8,128)(2,1)S(1)}, u32[]{:S(2)}, u32[]{:S(2)}) collective-permute-start(bf16[256,512]{1,0:T(8,128)(2,1)S(1)} %get-tuple-element.33), channel_id=1, source_target_pairs={{0,3},{1,2},{2,1},{3,0},{4,7},{5,6},{6,5},{7,4},{8,11},{9,10},{10,... | collective-permute-start | bytes 786440 | tf_op jit(solution)/shard_map/ppermute | solution.py:142
  48.3 12.2 %all-to-all-start = ((f32[32,1,128]{2,1,0:T(1,128)}), f32[32,1,128]{2,1,0:T(1,128)S(1)}, u32[]{:S(2)}, u32[]{:S(2)}) async-start(f32[32,1,128]{2,1,0:T(1,128)} %bitcast.7), calls=%async_computation | async-start | bytes 32768 | tf_op jit(solution)/shard_map/all_to_all | solution.py:469

commit v5 on v4

--- a/solution.py
+++ b/solution.py
@@ -134,6 +134,7 @@
         and pre_gate.shape[1] == BLOCK
         and parts * BLOCK == K
         and filters.shape[0] * parts * dp_count == K
+        and dp_count == parts // 2 == groups // (parts // 2)
     )
 
 
@@ -197,17 +198,24 @@
 
 def bands(quarters, dp_count, place_ref, taps_in, taps_ref, causal_ref, anti_ref, causal_from, anti_to):
     half, quarter, dp_index = place_ref[0], place_ref[1], place_ref[2]
-    local, rows = taps_ref.shape[1:]
     for u in range(2):
         for j in range(quarters):
-            piece = taps_in[u * quarters + j][-TAIL:].astype(jnp.float32)
-            for p in range(dp_count):
-                owner = lax.rem(dp_index + dp_count - p, dp_count) * 2 * quarters + (half ^ u) * quarters + (quarter ^ j)
-                start = p * rows
-                taps_ref[owner] = piece[:local, start : start + rows]
-    for g in range(local):
-        line = jnp.concatenate([taps_ref[o, g : g + 1] for o in range(taps_ref.shape[0])], axis=1)
-        line = jnp.concatenate([line, jnp.zeros((1, BLOCK), jnp.float32)], axis=1)
+            tail = taps_in[u * quarters + j][-TAIL:].astype(jnp.float32)
+            taps_ref[(half ^ u) * quarters + (quarter ^ j)] = tail[: taps_ref.shape[1]]
+    rows = BLOCK // dp_count
+    part = lax.broadcasted_iota(jnp.int32, (1, BLOCK), 1) // rows
+    blocks = []
+    for d in range(dp_count):
+        way = lax.rem(dp_index + dp_count - d, dp_count)
+        for h in range(2):
+            block = None
+            for q in range(quarters):
+                shift = lax.rem(q + dp_count - way, dp_count) * rows
+                moved = pltpu.roll(taps_ref[h * quarters + q], shift, 1)
+                block = moved if block is None else jnp.where(part == q, moved, block)
+            blocks.append(block)
+    for g in range(causal_ref.shape[0]):
+        line = jnp.concatenate([block[g : g + 1] for block in blocks] + [jnp.zeros((1, BLOCK), jnp.float32)], axis=1)
         shear = pltpu.roll(jnp.broadcast_to(line, (BLOCK, K + BLOCK)), 0, 1, stride=1, stride_axis=0)
         zero = jnp.zeros((BLOCK, BLOCK), jnp.bfloat16)
         count = K // BLOCK
@@ -232,47 +240,54 @@
     return jnp.dot(left, right, preferred_element_type=jnp.float32)
 
 
-def causal_part(band, data, p):
-    reach = (p + 1) * 2 * BLOCK
-    return dot(band[:, K - reach :], data[:reach])
-
-
-def anti_part(band, data, p):
-    return dot(band[:, : data.shape[0] - p * 2 * BLOCK], data[p * 2 * BLOCK :])
-
-
-def lag_lines(mixed, mixed_first, gated, gated_first, turn):
+WIDE = 2 * BLOCK
+
+
+def side_by_side(data):
+    return jnp.concatenate([data[:-WIDE], data[WIDE:]], axis=1)
+
+
+def causal_part(band, data):
+    length = data.shape[0]
+    both = dot(band[:, K - length + WIDE :], side_by_side(data))
+    return both[:, :BLOCK], both[:, BLOCK:] + dot(band[:, K - length : K - length + WIDE], data[:WIDE])
+
+
+def anti_part(band, data):
+    length = data.shape[0]
+    both = dot(band[:, : length - WIDE], side_by_side(data))
+    return both[:, :BLOCK] + dot(band[:, length - WIDE : length], data[-WIDE:]), both[:, BLOCK:]
+
+
+def lag_lines(mixed, mixed_first, gated, gated_first):
     count = mixed.shape[0] // BLOCK
     blocks = K // BLOCK
-    turned = jnp.concatenate(
-        [dot(turn, mixed[j * BLOCK : (j + 1) * BLOCK]).astype(jnp.bfloat16) for j in range(count)], axis=0
-    )
+    still = [mixed[j * BLOCK : (j + 1) * BLOCK] for j in range(count)]
+    ready = [gated[i * BLOCK : (i + 1) * BLOCK] for i in range(gated.shape[0] // BLOCK)]
     sums = [None] * blocks
-    for i in range(gated.shape[0] // BLOCK):
-        first = gated_first + i - mixed_first
-        top = min(count, first + 1)
-        product = lax.dot_general(
-            turned[: top * BLOCK],
-            gated[i * BLOCK : (i + 1) * BLOCK],
-            (((1,), (1,)), ((), ())),
-            preferred_element_type=jnp.float32,
-        )
-        for j in range(top):
-            term = product[j * BLOCK : (j + 1) * BLOCK]
-            sums[first - j] = term if sums[first - j] is None else sums[first - j] + term
+    for lag in range(blocks):
+        pairs = [(j, j + lag + mixed_first - gated_first) for j in range(count)]
+        pairs = [(j, i) for j, i in pairs if 0 <= i < len(ready)]
+        if pairs:
+            left = jnp.concatenate([still[j] for j, _ in pairs], axis=1)
+            right = jnp.concatenate([ready[i] for _, i in pairs], axis=1)
+            sums[lag] = lax.dot_general(left, right, (((1,), (1,)), ((), ())), preferred_element_type=jnp.float32)
     last = max(m for m in range(blocks) if sums[m] is not None)
-    table = jnp.concatenate(sums[: last + 1] + [jnp.zeros((BLOCK, BLOCK), jnp.float32)], axis=1)
+    zero = jnp.zeros((BLOCK, BLOCK), jnp.float32)
+    table = jnp.concatenate([zero if term is None else term for term in sums[: last + 1]] + [zero], axis=1)
     span = (last + 2) * BLOCK
-    shear = jnp.sum(pltpu.roll(table, 0, 1, stride=1, stride_axis=0), axis=0, keepdims=True)
-    if span < K:
-        shear = jnp.concatenate([shear, jnp.zeros((1, K + BLOCK - span), jnp.float32)], axis=1)
-    return pltpu.roll(shear, K + BLOCK - (BLOCK - 1), 1)[:, :K]
-
-
-def exchange():
-    rows = lax.broadcasted_iota(jnp.int32, (BLOCK, BLOCK), 0)
-    columns = lax.broadcasted_iota(jnp.int32, (BLOCK, BLOCK), 1)
-    return jnp.where(rows + columns == BLOCK - 1, 1.0, 0.0).astype(jnp.bfloat16)
+    parts, step = [table[row : row + 8] for row in range(0, BLOCK, 8)], 8
+    while len(parts) > 1:
+        parts = [near + pltpu.roll(far, span - step, 1) for near, far in zip(parts[::2], parts[1::2])]
+        step *= 2
+    total = parts[0]
+    row = lax.broadcasted_iota(jnp.int32, (8, span), 0)
+    for step in (1, 2, 4):
+        total = jnp.where((row & step) != 0, pltpu.roll(total, span - step, 1), total)
+    line = jnp.sum(total, axis=0, keepdims=True)[:, : span - BLOCK]
+    if span - BLOCK < K:
+        line = jnp.concatenate([line, jnp.zeros((1, K + BLOCK - span), jnp.float32)], axis=1)
+    return line
 
 
 def gather(quarters, place_ref, ab_in, r_in, a_ref, data_ref):
@@ -293,7 +308,6 @@
     shares_ref, a_ref, data_ref, lines_ref = refs
     gather(quarters, place_ref, ab_in, r_in, a_ref, data_ref)
     half = place_ref[0]
-    turn = exchange()
     local = lines_ref.shape[0]
     length = quarters * BLOCK
 
@@ -302,7 +316,7 @@
         for g in range(local):
             lanes = slice(g * BLOCK, (g + 1) * BLOCK)
             mixed, gated = rows_of(a_ref, lanes), rows_of(data_ref, lanes)
-            lines_ref[g : g + 1] = lag_lines(mixed, 0, gated if g < local // 2 else gated[:length], 0, turn)
+            lines_ref[g : g + 1] = lag_lines(mixed, 0, gated if g < local // 2 else gated[:length], 0)
 
     @pl.when(half != 0)
     def upper():
@@ -310,14 +324,16 @@
             lanes = slice(g * BLOCK, (g + 1) * BLOCK)
             gated, mixed = rows_of(a_ref, lanes), rows_of(data_ref, lanes)
             first = quarters if g < local // 2 else 0
-            lines_ref[g : g + 1] = lag_lines(mixed[first * BLOCK :], first, gated, quarters, turn)
+            lines_ref[g : g + 1] = lag_lines(mixed[first * BLOCK :], first, gated, quarters)
 
     step = BLOCK // local
     lane = lax.broadcasted_iota(jnp.int32, (1, K), 1) % BLOCK // step
+    lines = lines_ref[...]
+    moved = {d: pltpu.roll(lines, d * step % K, 1) if d else lines for d in range(1 - local, local)}
     for u in range(local):
-        row = jnp.zeros((1, K), jnp.float32)
-        for g in range(local):
-            row = jnp.where(lane == g, pltpu.roll(lines_ref[g : g + 1], (g - u) * step % K, 1), row)
+        row = moved[-u][:1]
+        for g in range(1, local):
+            row = jnp.where(lane == g, moved[g - u][g : g + 1], row)
         for block in range(K // BLOCK):
             shares_ref[block * local + u : block * local + u + 1] = row[:, block * BLOCK : (block + 1) * BLOCK]
 
@@ -325,35 +341,34 @@
 def sums_kernel(quarters, dp_count, place_ref, *refs):
     ab_in, r_in, refs = refs[: quarters + 1], refs[quarters + 1 : 2 * quarters + 1], refs[2 * quarters + 1 :]
     outs, refs = refs[:quarters], refs[quarters:]
-    causal_ref, anti_ref, a_ref, data_ref, a_sum_ref, b_sum_ref, taps_ref = refs
+    causal_ref, anti_ref, a_ref, data_ref, done_ref, taps_ref = refs
     gather(quarters, place_ref, ab_in, r_in, a_ref, data_ref)
     tails = ab_in[:quarters] + r_in
     half, quarter = place_ref[0], place_ref[1]
-
-    def work(a_part, a_band, b_part, b_band, first):
-        for g in range(causal_ref.shape[0]):
+    local = causal_ref.shape[0]
+
+    def work(a_part, a_band, b_part, b_band):
+        for g in range(local):
             lanes = slice(g * BLOCK, (g + 1) * BLOCK)
-            a_rows, data = rows_of(a_ref, lanes), rows_of(data_ref, lanes)
-            for p in range(quarters // 2):
-                pair = slice(2 * p, 2 * p + 2)
-                a_sum = a_part(a_band.at[g], a_rows, p)
-                a_sum_ref[pair, :, lanes] = a_sum.reshape(2, BLOCK, BLOCK).astype(jnp.bfloat16)
-                b_sum = b_part(b_band.at[g], data, first + p)
-                b_sum_ref[pair, :, lanes] = b_sum.reshape(2, BLOCK, BLOCK).astype(jnp.bfloat16)
+            for rows, sums in (
+                (slice(0, BLOCK), a_part(a_band.at[g], rows_of(a_ref, lanes))),
+                (slice(BLOCK, WIDE), b_part(b_band.at[g], rows_of(data_ref, lanes))),
+            ):
+                for p in range(2):
+                    done_ref[2 * p : 2 * p + 2, g, rows] = sums[p].reshape(2, BLOCK, BLOCK).astype(jnp.bfloat16)
 
     @pl.when(half == 0)
     def lower():
         bands(quarters, dp_count, place_ref, tails, taps_ref, causal_ref, anti_ref, K // 2, K)
-        work(causal_part, causal_ref, anti_part, anti_ref, 0)
+        work(causal_part, causal_ref, anti_part, anti_ref)
 
     @pl.when(half != 0)
     def upper():
         bands(quarters, dp_count, place_ref, tails, taps_ref, causal_ref, anti_ref, 0, K // 2)
-        work(anti_part, anti_ref, causal_part, causal_ref, quarters // 2)
+        work(anti_part, anti_ref, causal_part, causal_ref)
 
     for j in range(quarters):
-        outs[j][:BLOCK] = a_sum_ref[quarter ^ j]
-        outs[j][BLOCK:] = b_sum_ref[quarter ^ j]
+        outs[j][...] = done_ref[quarter ^ j].reshape(local * WIDE, BLOCK)
 
 
 def owned_kernel(scale, place_ref, arrived_ref, out_ref):
@@ -376,24 +391,25 @@
     back, inputs = refs[:count], refs[count : count + 4]
     outputs, results, sem = refs[-9:-5], refs[-5:-1], refs[-1]
     half, quarter = place_ref[0], place_ref[1]
-    width = back[0].shape[1]
-
-    def place(j):
-        return pl.ds(pl.multiple_of((quarter ^ j) * width, width), width)
+    width = results[0].shape[2]
 
     def copies(i):
+        columns = pl.ds(pl.multiple_of((quarter ^ js[i]) * width, width), width)
         return [
-            pltpu.make_async_copy(store.at[i], target.at[0, :, place(js[i])], sem.at[i, k])
+            pltpu.make_async_copy(store.at[i], target.at[0, :, columns], sem.at[i, k])
             for k, (store, target) in enumerate(zip(results, outputs))
         ]
 
     for i in range(count):
-        columns = place(js[i])
-        pre, post, values, cot = [source[0, :, columns].astype(f32) for source in inputs]
-        a_sum, b_sum = back[i][:BLOCK].astype(f32), back[i][BLOCK:].astype(f32)
-        convolved, carried = jnp.where(half == 0, a_sum, b_sum), jnp.where(half == 0, b_sum, a_sum)
-        for result, value in zip(results, (post * convolved, carried * values, cot * convolved, carried * pre)):
-            result[i] = value.astype(bf16)
+        for g in range(width // BLOCK):
+            lanes = slice(g * BLOCK, (g + 1) * BLOCK)
+            columns = pl.ds(pl.multiple_of((quarter ^ js[i]) * width + g * BLOCK, BLOCK), BLOCK)
+            pre, post, values, cot = [source[0, :, columns].astype(f32) for source in inputs]
+            sums = back[i][g * WIDE : (g + 1) * WIDE].astype(f32)
+            a_sum, b_sum = sums[:BLOCK], sums[BLOCK:]
+            convolved, carried = jnp.where(half == 0, a_sum, b_sum), jnp.where(half == 0, b_sum, a_sum)
+            for result, value in zip(results, (post * convolved, carried * values, cot * convolved, carried * pre)):
+                result[i, :, lanes] = value.astype(bf16)
         for copy in copies(i):
             copy.start()
     for i in range(count):
@@ -403,7 +419,7 @@
 
 def gate_outputs(js, place, back, gates, earlier=()):
     hbm = [pl.BlockSpec(memory_space=pltpu.HBM)] * 4
-    store = pltpu.VMEM((len(js), BLOCK, back[0].shape[1]), jnp.bfloat16)
+    store = pltpu.VMEM((len(js), BLOCK, back[0].shape[0] // 2), jnp.bfloat16)
     return pl.pallas_call(
         lambda *refs: outputs_kernel(js, *refs),
         in_specs=[pl.BlockSpec(memory_space=pltpu.SMEM)] + vmem_specs(len(js) + 4) + hbm[: len(earlier)],
@@ -455,10 +471,19 @@
     band = pltpu.VMEM((local, 2 * BLOCK, K), bf16)
     store = pltpu.VMEM((quarters, BLOCK, width), bf16)
     whole = pltpu.VMEM((parts, BLOCK, width), bf16)
-    done = call(
-        lambda *refs: sums_kernel(quarters, dp_count, *refs), "sums", place, ab_in + r_in, chunk_shapes(quarters, width, 2),
-        [band, band, store, whole, store, store, pltpu.VMEM((owners, local, rows), f32)], flops=1000, nbytes=1000,
-    )
+    done = pl.pallas_call(
+        lambda *refs: sums_kernel(quarters, dp_count, *refs),
+        in_specs=[pl.BlockSpec(memory_space=pltpu.SMEM)] + vmem_specs(2 * quarters + 1),
+        out_specs=vmem_specs(quarters),
+        out_shape=[jax.ShapeDtypeStruct((2 * local * BLOCK, BLOCK), bf16)] * quarters,
+        scratch_shapes=[
+            band, band, store, whole, pltpu.VMEM((quarters, local, WIDE, BLOCK), bf16),
+            pltpu.VMEM((parts, 8, BLOCK), f32),
+        ],
+        compiler_params=pltpu.CompilerParams(vmem_limit_bytes=20 * 1024 * 1024),
+        cost_estimate=pl.CostEstimate(flops=1000, bytes_accessed=1000, transcendentals=0),
+        name="sums",
+    )(place, *ab_in, *r_in)
     back = [done[0]] + [swap(done[j], j) for j in range(1, quarters)]
     token = lax.ppermute(done[0], "dp", [(i, i ^ 1) for i in range(dp_count)])
     (shares,) = call(
@@ -468,7 +493,7 @@
     )
     arrived = lax.all_to_all(shares, every, 0, 0, tiled=True)
 
-    early, last = list(range(quarters - 1)), [quarters - 1]
+    early, last = [0, quarters - 1], list(range(1, quarters - 1))
     outputs = gate_outputs(early, place, back, gates)
     output, grad_pre, grad_post, grad_values = gate_outputs(last, place, back, gates, outputs)
     total_tokens = dp_count * parts * pre_gate.shape[1] * (channels // groups)

time: 61.9 us -> 60.6 us (0.979)
    pallas_call x4 -> x3, Pallas kernels: 8.86 us -> 4.96 us  [call(): pl.pallas_call(body, in_specs=[pl.BlockSpec(memory_space=pltpu.SMEM)] + v...]
    pallas_call x0 -> x1, Pallas kernels: none -> 3.13 us  [swapped(): pl.pallas_call(lambda *refs: sums_kernel(quarters, dp_count, *refs), in_s...]
where the time goes in v5:
time: 60.6 us; the launch traced here: 60.5 us
  starting transfers between devices  23.8 us (39%)
  waiting for transfers between devices  22.5 us (37%)
  Pallas kernels  11.5 us (19%)
  other arithmetic  1.98 us (3%)
  between operations  0.75 us (1%)
    ppermute x11, waiting for transfers between devices, swap(): return lax.ppermute(chunk, 'seq', [(i, i ^ flip) for i in range(count)])  20.6 us
    ppermute x11, starting transfers between devices, swap(): return lax.ppermute(chunk, 'seq', [(i, i ^ flip) for i in range(count)])  16.2 us
    pallas_call x3, Pallas kernels, call(): pl.pallas_call(body, in_specs=[pl.BlockSpec(memory_space=pltpu.SMEM)] + v...  4.96 us
    all_to_all x1, starting transfers between devices, swapped(): arrived = lax.all_to_all(shares, every, 0, 0, tiled=True)  4.32 us
    pallas_call x2, Pallas kernels, gate_outputs(): pl.pallas_call(lambda *refs: outputs_kernel(js, *refs), in_specs=[pl.Bloc...  3.36 us
    ppermute x3, starting transfers between devices, swapped(): lax.ppermute(taps, 'dp', [(i, (i + p) % dp_count) for i in range(dp_count)])  3.23 us
    pallas_call x1, Pallas kernels, swapped(): pl.pallas_call(lambda *refs: sums_kernel(quarters, dp_count, *refs), in_s...  3.13 us
    select_n x1, other arithmetic, swapped(): a, b = (jnp.where(lower, mixed, gated), jnp.where(lower, gated, mixed))  1.9 us
  transfers between devices with their start and end apart: 16, of which 10 were waited for; matrix products, arithmetic and copies ran while one was open for 3% of the time, Pallas kernels for 10%

profile of v5, /device:TPU:0, one launch (start us, length us, event | category | flops | bytes accessed | tf_op | source)
XLA Modules:
  0.0 60.5 jit_solution(7511313276741937082)
XLA Ops:
  0.6 2.4 %collective-permute-start.2 = (bf16[16,32]{1,0:T(8,128)(2,1)}, bf16[16,32]{1,0:T(8,128)(2,1)S(1)}, u32[]{:S(2)}, u32[]{:S(2)}) collective-permute-start(bf16[16,32]{1,0:T(8,128)(2,1)} %bitcast.14), channel_id=1, source_target_pairs={{0,24},{8,0},{16,8},{24,16},{1,25},{9,1},{17,9},{25,17},{2,26},{10... | collective-permute-start | bytes 3080 | tf_op jit(solution)/shard_map/ppermute | solution.py:451
  3.1 0.6 %collective-permute-start.1 = (bf16[16,32]{1,0:T(8,128)(2,1)}, bf16[16,32]{1,0:T(8,128)(2,1)S(1)}, u32[]{:S(2)}, u32[]{:S(2)}) collective-permute-start(bf16[16,32]{1,0:T(8,128)(2,1)} %bitcast.15), channel_id=1, source_target_pairs={{0,16},{8,24},{16,0},{24,8},{1,17},{9,25},{17,1},{25,9},{2,18},{10... | collective-permute-start | bytes 3080 | tf_op jit(solution)/shard_map/ppermute | solution.py:451
  3.9 1.9 %select_bitcast_fusion = (bf16[128,2048]{1,0:T(8,128)(2,1)S(1)}, bf16[128,2048]{1,0:T(8,128)(2,1)S(1)}) fusion(pred[]{:T(512)S(6)} %lt.10, bf16[1,128,2048]{2,1,0:T(8,128)(2,1)} %refs_5_.3, bf16[1,128,2048]{2,1,0:T(8,128)(2,1)} %refs_3_.3, bf16[1,128,2048]{2,1,0:T(8,128)(2,1)} %refs_4_.3, bf16[1,128,2048]{2,1,0:T(8,128)(2,1)} %refs_6_.3), kind=kLoop, calls=%fused_computation.2 | loop fusion | flops 2621440 | bytes 3145729 | tf_op jit(solution)/shard_map/jit(_where)/select_n | solution.py:457
  5.9 1.0 %collective-permute-done.1.refs_2_ = bf16[16,32]{1,0:T(8,128)(2,1)S(1)} collective-permute-done((bf16[16,32]{1,0:T(8,128)(2,1)}, bf16[16,32]{1,0:T(8,128)(2,1)S(1)}, u32[]{:S(2)}, u32[]{:S(2)}) %collective-permute-start.1) | collective-permute-done | bytes 1056 | tf_op jit(solution)/shard_map/ppermute | solution.py:451
  6.9 0.8 %pack.1 = (bf16[528,128]{1,0:T(8,128)(2,1)S(1)}, bf16[528,128]{1,0:T(8,128)(2,1)S(1)}, bf16[528,128]{1,0:T(8,128)(2,1)S(1)}, bf16[528,128]{1,0:T(8,128)(2,1)S(1)...) custom-call(s32[3]{0:T(128)S(1)} %pad_add_fusion.place_ref.refs_0_, ...), custom_call_target="tpu_custom_call" | custom-call | flops 1000 | bytes 1000 | tf_op jit(solution)/shard_map/pack/pallas_call | solution.py:158
  7.8 2.6 %collective-permute-start.6 = (bf16[528,128]{1,0:T(8,128)(2,1)S(1)}, bf16[528,128]{1,0:T(8,128)(2,1)S(1)}, u32[]{:S(2)}, u32[]{:S(2)}) collective-permute-start(bf16[528,128]{1,0:T(8,128)(2,1)S(1)} %get-tuple-element.29), channel_id=1, source_target_pairs={{0,3},{1,2},{2,1},{3,0},{4,7},{5,6},{6,5},{7,4},{8,11},{9,10},{10,... | collective-permute-start | bytes 405512 | tf_op jit(solution)/shard_map/ppermute | solution.py:143
  10.4 2.6 %collective-permute-start.7 = (bf16[528,128]{1,0:T(8,128)(2,1)S(1)}, bf16[528,128]{1,0:T(8,128)(2,1)S(1)}, u32[]{:S(2)}, u32[]{:S(2)}) collective-permute-start(bf16[528,128]{1,0:T(8,128)(2,1)S(1)} %get-tuple-element.30), channel_id=1, source_target_pairs={{0,4},{1,5},{2,6},{3,7},{4,0},{5,1},{6,2},{7,3},{8,12},{9,13},{10,... | collective-permute-start | bytes 405512 | tf_op jit(solution)/shard_map/ppermute | solution.py:143
  13.2 1.5 %collective-permute-start.3 = (bf16[1040,128]{1,0:T(8,128)(2,1)S(1)}, bf16[1040,128]{1,0:T(8,128)(2,1)S(1)}, u32[]{:S(2)}, u32[]{:S(2)}) collective-permute-start(bf16[1040,128]{1,0:T(8,128)(2,1)S(1)} %get-tuple-element.26), channel_id=1, source_target_pairs={{0,1},{1,0},{2,3},{3,2},{4,5},{5,4},{6,7},{7,6},{8,9},{9,8},{10,11... | collective-permute-start | bytes 798728 | tf_op jit(solution)/shard_map/ppermute | solution.py:143
  15.2 2.8 %collective-permute-done.6.refs_5_.refs_4_ = bf16[528,128]{1,0:T(8,128)(2,1)S(1)} collective-permute-done((bf16[528,128]{1,0:T(8,128)(2,1)S(1)}, bf16[528,128]{1,0:T(8,128)(2,1)S(1)}, u32[]{:S(2)}, u32[]{:S(2)}) %collective-permute-start.6) | collective-permute-done | bytes 135200 | tf_op jit(solution)/shard_map/ppermute | solution.py:143
  18.0 2.5 %collective-permute-start.9 = (bf16[528,128]{1,0:T(8,128)(2,1)S(1)}, bf16[528,128]{1,0:T(8,128)(2,1)S(1)}, u32[]{:S(2)}, u32[]{:S(2)}) collective-permute-start(bf16[528,128]{1,0:T(8,128)(2,1)S(1)} %get-tuple-element.32), channel_id=1, source_target_pairs={{0,6},{1,7},{2,4},{3,5},{4,2},{5,3},{6,0},{7,1},{8,14},{9,15},{10,... | collective-permute-start | bytes 405512 | tf_op jit(solution)/shard_map/ppermute | solution.py:143
  20.5 3.1 %collective-permute-done.7.refs_6_.refs_5_ = bf16[528,128]{1,0:T(8,128)(2,1)S(1)} collective-permute-done((bf16[528,128]{1,0:T(8,128)(2,1)S(1)}, bf16[528,128]{1,0:T(8,128)(2,1)S(1)}, u32[]{:S(2)}, u32[]{:S(2)}) %collective-permute-start.7) | collective-permute-done | bytes 135200 | tf_op jit(solution)/shard_map/ppermute | solution.py:143
  23.6 2.4 %collective-permute-start.10 = (bf16[528,128]{1,0:T(8,128)(2,1)S(1)}, bf16[528,128]{1,0:T(8,128)(2,1)S(1)}, u32[]{:S(2)}, u32[]{:S(2)}) collective-permute-start(bf16[528,128]{1,0:T(8,128)(2,1)S(1)} %get-tuple-element.28), channel_id=1, source_target_pairs={{0,7},{1,6},{2,5},{3,4},{4,3},{5,2},{6,1},{7,0},{8,15},{9,14},{10,... | collective-permute-start | bytes 405512 | tf_op jit(solution)/shard_map/ppermute | solution.py:143
  26.1 5.8 %collective-permute-done.9.refs_8_.refs_7_ = bf16[528,128]{1,0:T(8,128)(2,1)S(1)} collective-permute-done((bf16[528,128]{1,0:T(8,128)(2,1)S(1)}, bf16[528,128]{1,0:T(8,128)(2,1)S(1)}, u32[]{:S(2)}, u32[]{:S(2)}) %collective-permute-start.9) | collective-permute-done | bytes 135200 | tf_op jit(solution)/shard_map/ppermute | solution.py:143
  32.0 2.7 %collective-permute-done.10.refs_9_.refs_8_ = bf16[528,128]{1,0:T(8,128)(2,1)S(1)} collective-permute-done((bf16[528,128]{1,0:T(8,128)(2,1)S(1)}, bf16[528,128]{1,0:T(8,128)(2,1)S(1)}, u32[]{:S(2)}, u32[]{:S(2)}) %collective-permute-start.10) | collective-permute-done | bytes 135200 | tf_op jit(solution)/shard_map/ppermute | solution.py:143
  34.7 2.8 %collective-permute-done.5.refs_4_.refs_3_ = bf16[528,128]{1,0:T(8,128)(2,1)S(1)} collective-permute-done((bf16[528,128]{1,0:T(8,128)(2,1)S(1)}, bf16[528,128]{1,0:T(8,128)(2,1)S(1)}, u32[]{:S(2)}, u32[]{:S(2)}) %collective-permute-start.5) | collective-permute-done | bytes 135200 | tf_op jit(solution)/shard_map/ppermute | solution.py:143
  37.5 3.1 %sums.1 = (bf16[1024,128]{1,0:T(8,128)(2,1)S(1)}, bf16[1024,128]{1,0:T(8,128)(2,1)}, bf16[1024,128]{1,0:T(8,128)(2,1)S(1)}, bf16[1024,128]{1,0:T(8,128)(2,1)}) custom-call(s32[3]{0:T(128)S(1)} %pad_add_fusion.place_ref.refs_0_, bf16[1040,128]{1,0:T(8,128)(2,1)S(1)} %get-tuple-element.25.refs_1_.refs_0_, ...), custom_call_target="tpu_custom_call" | custom-call | flops 1000 | bytes 1000 | tf_op jit(solution)/shard_map/sums/pallas_call | solution.py:474
  40.7 3.2 %collective-permute-start.13 = (bf16[1024,128]{1,0:T(8,128)(2,1)}, bf16[1024,128]{1,0:T(8,128)(2,1)S(1)}, u32[]{:S(2)}, u32[]{:S(2)}) collective-permute-start(bf16[1024,128]{1,0:T(8,128)(2,1)} %get-tuple-element.36), channel_id=1, source_target_pairs={{0,3},{1,2},{2,1},{3,0},{4,7},{5,6},{6,5},{7,4},{8,11},{9,10},{10,... | collective-permute-start | bytes 786440 | tf_op jit(solution)/shard_map/ppermute | solution.py:143
  44.5 2.9 %lags.1 = f32[32,128]{1,0:T(8,128)} custom-call(s32[3]{0:T(128)S(1)} %pad_add_fusion.place_ref.refs_0_, bf16[1040,128]{1,0:T(8,128)(2,1)S(1)} %get-tuple-element.25.refs_1_.refs_0_, bf16[1040,128]{1,0:T(8,128)(2,1)S(1)} %collective-permute-done.3.refs_2_.refs_1_, bf16[1040,128]{1,0:T(8,128)(2,1)S(1)} %collective-permute-done.4.refs_3_.refs_2_, ...), custom_call_target="tpu_custom_call" | custom-call | flops 1000 | bytes 1000 | tf_op jit(solution)/shard_map/lags/pallas_call | solution.py:158
  47.5 4.3 %all-to-all-start = ((f32[32,1,128]{2,1,0:T(1,128)}), f32[32,1,128]{2,1,0:T(1,128)S(1)}, u32[]{:S(2)}, u32[]{:S(2)}) async-start(f32[32,1,128]{2,1,0:T(1,128)} %bitcast.7), calls=%async_computation | async-start | bytes 32768 | tf_op jit(solution)/shard_map/all_to_all | solution.py:494
  51.8 1.7 %outputs.2 = (bf16[1,128,2048]{2,1,0:T(8,128)(2,1)}, bf16[1,128,2048]{2,1,0:T(8,128)(2,1)}, bf16[1,128,2048]{2,1,0:T(8,128)(2,1)}, bf16[1,128,2048]{2,1,0:T(8,128)(2,1)}) custom-call(s32[3]{0:T(128)S(1)} %pad_add_fusion.place_ref.refs_0_, bf16[1024,128]{1,0:T(8,128)(2,1)S(1)} %get-tuple-element.35.refs_1_, ...), custom_call_target="tpu_custom_call" | custom-call | flops 1000 | bytes 1000 | tf_op jit(solution)/shard_map/outputs/pallas_call | solution.py:423
  53.5 3.2 %collective-permute-done.11.refs_1_ = bf16[1024,128]{1,0:T(8,128)(2,1)S(1)} collective-permute-done((bf16[1024,128]{1,0:T(8,128)(2,1)}, bf16[1024,128]{1,0:T(8,128)(2,1)S(1)}, u32[]{:S(2)}, u32[]{:S(2)}) %collective-permute-start.11) | collective-permute-done | bytes 262176 | tf_op jit(solution)/shard_map/ppermute | solution.py:143
  56.8 1.7 %outputs.3 = (bf16[1,128,2048]{2,1,0:T(8,128)(2,1)}, bf16[1,128,2048]{2,1,0:T(8,128)(2,1)}, bf16[1,128,2048]{2,1,0:T(8,128)(2,1)}, bf16[1,128,2048]{2,1,0:T(8,128)(2,1)}) custom-call(s32[3]{0:T(128)S(1)} %pad_add_fusion.place_ref.refs_0_, ...), custom_call_target="tpu_custom_call", output_to_operand_aliasing={{0}: (7, {}), {1}: (8, {}), {2}: (9, {}), {3}: (10, {})} | custom-call | flops 1000 | bytes 1000 | tf_op jit(solution)/shard_map/outputs/pallas_call | solution.py:423
  58.5 0.8 %all-to-all-done = f32[32,1,128]{2,1,0:T(1,128)S(1)} async-done(((f32[32,1,128]{2,1,0:T(1,128)}), f32[32,1,128]{2,1,0:T(1,128)S(1)}, u32[]{:S(2)}, u32[]{:S(2)}) %all-to-all-start) | async-done | bytes 16416 | tf_op jit(solution)/shard_map/all_to_all | solution.py:494
  59.2 1.2 %owned.1 = f32[16,32]{1,0:T(8,128)} custom-call(s32[3]{0:T(128)S(1)} %pad_add_fusion.place_ref.refs_0_, f32[32,128]{1,0:T(8,128)S(1)} %bitcast.13), custom_call_target="tpu_custom_call" | custom-call | flops 1000 | bytes 1000 | tf_op jit(solution)/shard_map/owned/pallas_call | solution.py:158
  (26 shorter events, 1.8 us)
Async XLA Ops:
  0.6 5.2 %collective-permute-start.2 = (bf16[16,32]{1,0:T(8,128)(2,1)}, bf16[16,32]{1,0:T(8,128)(2,1)S(1)}, u32[]{:S(2)}, u32[]{:S(2)}) collective-permute-start(bf16[16,32]{1,0:T(8,128)(2,1)} %bitcast.14), channel_id=1, source_target_pairs={{0,24},{8,0},{16,8},{24,16},{1,25},{9,1},{17,9},{25,17},{2,26},{10... | collective-permute-start | bytes 3080 | tf_op jit(solution)/shard_map/ppermute | solution.py:451
  3.1 3.8 %collective-permute-start.1 = (bf16[16,32]{1,0:T(8,128)(2,1)}, bf16[16,32]{1,0:T(8,128)(2,1)S(1)}, u32[]{:S(2)}, u32[]{:S(2)}) collective-permute-start(bf16[16,32]{1,0:T(8,128)(2,1)} %bitcast.15), channel_id=1, source_target_pairs={{0,16},{8,24},{16,0},{24,8},{1,17},{9,25},{17,1},{25,9},{2,18},{10... | collective-permute-start | bytes 3080 | tf_op jit(solution)/shard_map/ppermute | solution.py:451
  3.7 3.2 %collective-permute-start = (bf16[16,32]{1,0:T(8,128)(2,1)}, bf16[16,32]{1,0:T(8,128)(2,1)S(1)}, u32[]{:S(2)}, u32[]{:S(2)}) collective-permute-start(bf16[16,32]{1,0:T(8,128)(2,1)} %bitcast.16), channel_id=1, source_target_pairs={{0,8},{8,16},{16,24},{24,0},{1,9},{9,17},{17,25},{25,1},{2,10},{10... | collective-permute-start | bytes 3080 | tf_op jit(solution)/shard_map/ppermute | solution.py:451
  5.8 1.2 %copy-start.4 = (bf16[32,16]{0,1:T(8,128)(2,1)S(1)}, bf16[32,16]{0,1:T(8,128)(2,1)}, u32[]{:S(2)}) copy-start(bf16[32,16]{0,1:T(8,128)(2,1)} %param.9) | copy-start | bytes 3076
  7.8 10.2 %collective-permute-start.6 = (bf16[528,128]{1,0:T(8,128)(2,1)S(1)}, bf16[528,128]{1,0:T(8,128)(2,1)S(1)}, u32[]{:S(2)}, u32[]{:S(2)}) collective-permute-start(bf16[528,128]{1,0:T(8,128)(2,1)S(1)} %get-tuple-element.29), channel_id=1, source_target_pairs={{0,3},{1,2},{2,1},{3,0},{4,7},{5,6},{6,5},{7,4},{8,11},{9,10},{10,... | collective-permute-start | bytes 405512 | tf_op jit(solution)/shard_map/ppermute | solution.py:143
  10.4 13.2 %collective-permute-start.7 = (bf16[528,128]{1,0:T(8,128)(2,1)S(1)}, bf16[528,128]{1,0:T(8,128)(2,1)S(1)}, u32[]{:S(2)}, u32[]{:S(2)}) collective-permute-start(bf16[528,128]{1,0:T(8,128)(2,1)S(1)} %get-tuple-element.30), channel_id=1, source_target_pairs={{0,4},{1,5},{2,6},{3,7},{4,0},{5,1},{6,2},{7,3},{8,12},{9,13},{10,... | collective-permute-start | bytes 405512 | tf_op jit(solution)/shard_map/ppermute | solution.py:143
  13.0 13.2 %collective-permute-start.8 = (bf16[528,128]{1,0:T(8,128)(2,1)S(1)}, bf16[528,128]{1,0:T(8,128)(2,1)S(1)}, u32[]{:S(2)}, u32[]{:S(2)}) collective-permute-start(bf16[528,128]{1,0:T(8,128)(2,1)S(1)} %get-tuple-element.31), channel_id=1, source_target_pairs={{0,5},{1,4},{2,7},{3,6},{4,1},{5,0},{6,3},{7,2},{8,13},{9,12},{10,... | collective-permute-start | bytes 405512 | tf_op jit(solution)/shard_map/ppermute | solution.py:143
  13.2 24.3 %collective-permute-start.3 = (bf16[1040,128]{1,0:T(8,128)(2,1)S(1)}, bf16[1040,128]{1,0:T(8,128)(2,1)S(1)}, u32[]{:S(2)}, u32[]{:S(2)}) collective-permute-start(bf16[1040,128]{1,0:T(8,128)(2,1)S(1)} %get-tuple-element.26), channel_id=1, source_target_pairs={{0,1},{1,0},{2,3},{3,2},{4,5},{5,4},{6,7},{7,6},{8,9},{9,8},{10,11... | collective-permute-start | bytes 798728 | tf_op jit(solution)/shard_map/ppermute | solution.py:143
  14.8 22.7 %collective-permute-start.4 = (bf16[1040,128]{1,0:T(8,128)(2,1)S(1)}, bf16[1040,128]{1,0:T(8,128)(2,1)S(1)}, u32[]{:S(2)}, u32[]{:S(2)}) collective-permute-start(bf16[1040,128]{1,0:T(8,128)(2,1)S(1)} %get-tuple-element.27), channel_id=1, source_target_pairs={{0,2},{1,3},{2,0},{3,1},{4,6},{5,7},{6,4},{7,5},{8,10},{9,11},{10,... | collective-permute-start | bytes 798728 | tf_op jit(solution)/shard_map/ppermute | solution.py:143
  18.0 14.0 %collective-permute-start.9 = (bf16[528,128]{1,0:T(8,128)(2,1)S(1)}, bf16[528,128]{1,0:T(8,128)(2,1)S(1)}, u32[]{:S(2)}, u32[]{:S(2)}) collective-permute-start(bf16[528,128]{1,0:T(8,128)(2,1)S(1)} %get-tuple-element.32), channel_id=1, source_target_pairs={{0,6},{1,7},{2,4},{3,5},{4,2},{5,3},{6,0},{7,1},{8,14},{9,15},{10,... | collective-permute-start | bytes 405512 | tf_op jit(solution)/shard_map/ppermute | solution.py:143
  23.6 11.1 %collective-permute-start.10 = (bf16[528,128]{1,0:T(8,128)(2,1)S(1)}, bf16[528,128]{1,0:T(8,128)(2,1)S(1)}, u32[]{:S(2)}, u32[]{:S(2)}) collective-permute-start(bf16[528,128]{1,0:T(8,128)(2,1)S(1)} %get-tuple-element.28), channel_id=1, source_target_pairs={{0,7},{1,6},{2,5},{3,4},{4,3},{5,2},{6,1},{7,0},{8,15},{9,14},{10,... | collective-permute-start | bytes 405512 | tf_op jit(solution)/shard_map/ppermute | solution.py:143
  26.1 11.4 %collective-permute-start.5 = (bf16[528,128]{1,0:T(8,128)(2,1)S(1)}, bf16[528,128]{1,0:T(8,128)(2,1)S(1)}, u32[]{:S(2)}, u32[]{:S(2)}) collective-permute-start(bf16[528,128]{1,0:T(8,128)(2,1)S(1)} %get-tuple-element.28), channel_id=1, source_target_pairs={{0,3},{1,2},{2,1},{3,0},{4,7},{5,6},{6,5},{7,4},{8,11},{9,10},{10,... | collective-permute-start | bytes 405512 | tf_op jit(solution)/shard_map/ppermute | solution.py:143
  37.5 14.3 %copy-start.3 = (bf16[1,128,2048]{2,1,0:T(8,128)(2,1)S(1)}, bf16[1,128,2048]{2,1,0:T(8,128)(2,1)}, u32[]{:S(2)}) copy-start(bf16[1,128,2048]{2,1,0:T(8,128)(2,1)} %refs_6_.3) | copy-start | bytes 1572868
  40.6 3.9 %collective-permute-start.14 = (bf16[1024,128]{1,0:T(8,128)(2,1)S(1)}, bf16[1024,128]{1,0:T(8,128)(2,1)S(1)}, u32[]{:S(2)}, u32[]{:S(2)}) collective-permute-start(bf16[1024,128]{1,0:T(8,128)(2,1)S(1)} %get-tuple-element.35.refs_1_), channel_id=1, source_target_pairs={{0,8},{8,0},{16,24},{24,16},{1,9},{9,1},{17,25},{25,17},{2,10},{10... | collective-permute-start | bytes 786440 | tf_op jit(solution)/shard_map/ppermute | solution.py:488
  40.7 11.1 %collective-permute-start.13 = (bf16[1024,128]{1,0:T(8,128)(2,1)}, bf16[1024,128]{1,0:T(8,128)(2,1)S(1)}, u32[]{:S(2)}, u32[]{:S(2)}) collective-permute-start(bf16[1024,128]{1,0:T(8,128)(2,1)} %get-tuple-element.36), channel_id=1, source_target_pairs={{0,3},{1,2},{2,1},{3,0},{4,7},{5,6},{6,5},{7,4},{8,11},{9,10},{10,... | collective-permute-start | bytes 786440 | tf_op jit(solution)/shard_map/ppermute | solution.py:143
  43.9 12.9 %collective-permute-start.11 = (bf16[1024,128]{1,0:T(8,128)(2,1)}, bf16[1024,128]{1,0:T(8,128)(2,1)S(1)}, u32[]{:S(2)}, u32[]{:S(2)}) collective-permute-start(bf16[1024,128]{1,0:T(8,128)(2,1)} %get-tuple-element.33), channel_id=1, source_target_pairs={{0,1},{1,0},{2,3},{3,2},{4,5},{5,4},{6,7},{7,6},{8,9},{9,8},{10,11... | collective-permute-start | bytes 786440 | tf_op jit(solution)/shard_map/ppermute | solution.py:143
  44.5 7.3 %copy-start = (bf16[1,128,2048]{2,1,0:T(8,128)(2,1)S(1)}, bf16[1,128,2048]{2,1,0:T(8,128)(2,1)}, u32[]{:S(2)}) copy-start(bf16[1,128,2048]{2,1,0:T(8,128)(2,1)} %refs_5_.3) | copy-start | bytes 1572868
  44.5 7.3 %copy-start.1 = (bf16[1,128,2048]{2,1,0:T(8,128)(2,1)S(1)}, bf16[1,128,2048]{2,1,0:T(8,128)(2,1)}, u32[]{:S(2)}) copy-start(bf16[1,128,2048]{2,1,0:T(8,128)(2,1)} %refs_3_.3) | copy-start | bytes 1572868
  44.5 7.3 %copy-start.2 = (bf16[1,128,2048]{2,1,0:T(8,128)(2,1)S(1)}, bf16[1,128,2048]{2,1,0:T(8,128)(2,1)}, u32[]{:S(2)}) copy-start(bf16[1,128,2048]{2,1,0:T(8,128)(2,1)} %refs_4_.3) | copy-start | bytes 1572868
  44.5 12.3 %collective-permute-start.12 = (bf16[1024,128]{1,0:T(8,128)(2,1)S(1)}, bf16[1024,128]{1,0:T(8,128)(2,1)S(1)}, u32[]{:S(2)}, u32[]{:S(2)}) collective-permute-start(bf16[1024,128]{1,0:T(8,128)(2,1)S(1)} %get-tuple-element.34), channel_id=1, source_target_pairs={{0,2},{1,3},{2,0},{3,1},{4,6},{5,7},{6,4},{7,5},{8,10},{9,11},{10,... | collective-permute-start | bytes 786440 | tf_op jit(solution)/shard_map/ppermute | solution.py:143
  47.5 11.8 %all-to-all-start = ((f32[32,1,128]{2,1,0:T(1,128)}), f32[32,1,128]{2,1,0:T(1,128)S(1)}, u32[]{:S(2)}, u32[]{:S(2)}) async-start(f32[32,1,128]{2,1,0:T(1,128)} %bitcast.7), calls=%async_computation | async-start | bytes 32768 | tf_op jit(solution)/shard_map/all_to_all | solution.py:494

commit v6 on v5

--- a/solution.py
+++ b/solution.py
@@ -206,7 +206,7 @@
     part = lax.broadcasted_iota(jnp.int32, (1, BLOCK), 1) // rows
     blocks = []
     for d in range(dp_count):
-        way = lax.rem(dp_index + dp_count - d, dp_count)
+        way = dp_index ^ d
         for h in range(2):
             block = None
             for q in range(quarters):
@@ -327,15 +327,17 @@
             lines_ref[g : g + 1] = lag_lines(mixed[first * BLOCK :], first, gated, quarters)
 
     step = BLOCK // local
-    lane = lax.broadcasted_iota(jnp.int32, (1, K), 1) % BLOCK // step
-    lines = lines_ref[...]
-    moved = {d: pltpu.roll(lines, d * step % K, 1) if d else lines for d in range(1 - local, local)}
-    for u in range(local):
-        row = moved[-u][:1]
-        for g in range(1, local):
-            row = jnp.where(lane == g, moved[g - u][g : g + 1], row)
-        for block in range(K // BLOCK):
-            shares_ref[block * local + u : block * local + u + 1] = row[:, block * BLOCK : (block + 1) * BLOCK]
+    owners = shares_ref.shape[0]
+    for block in range(K // BLOCK):
+        shares_ref[block * local : (block + 1) * local] = lines_ref[:, block * BLOCK : (block + 1) * BLOCK]
+    rows = shares_ref[...]
+    way = lax.broadcasted_iota(jnp.int32, rows.shape, 1) // step - lax.broadcasted_iota(jnp.int32, rows.shape, 0) % local
+    sorted_rows = rows
+    for d in range(1 - local, local):
+        if d:
+            moved = pltpu.roll(pltpu.roll(rows, -d % owners, 0), d * step % BLOCK, 1)
+            sorted_rows = jnp.where(way == d, moved, sorted_rows)
+    shares_ref[...] = sorted_rows
 
 
 def sums_kernel(quarters, dp_count, place_ref, *refs):
@@ -448,7 +450,7 @@
     taps = filters.T
     pieces = [taps]
     for p in range(1, dp_count):
-        pieces.append(lax.ppermute(taps, "dp", [(i, (i + p) % dp_count) for i in range(dp_count)]))
+        pieces.append(lax.ppermute(taps, "dp", [(i, i ^ p) for i in range(dp_count)]))
 
     gates = [pre_gate, post_gate, values, cotangent]
     lower = seq_index < quarters

time: 60.6 us -> 60 us (0.990)
  waiting for transfers between devices: 22.5 us -> 20 us
  starting transfers between devices: 23.8 us -> 25.6 us
    ppermute x11, waiting for transfers between devices: 20.6 us -> 17.2 us  [swap(): return lax.ppermute(chunk, 'seq', [(i, i ^ flip) for i in range(count)])]
    ppermute x11, starting transfers between devices: 16.2 us -> 17.5 us  [swap(): return lax.ppermute(chunk, 'seq', [(i, i ^ flip) for i in range(count)])]
    all_to_all x1, waiting for transfers between devices: 0.79 us -> 1.69 us  [swapped(): arrived = lax.all_to_all(shares, every, 0, 0, tiled=True)]
    all_to_all x1, starting transfers between devices: 4.32 us -> 5.03 us  [swapped(): arrived = lax.all_to_all(shares, every, 0, 0, tiled=True)]
  transfers between devices with their start and end apart: 16 -> 16, of which waited for: 10 -> 8; matrix products, arithmetic and copies ran while one was open for 3% -> 3% of each run, Pallas kernels for 10% -> 10%
where the time goes in v6:
time: 60 us; the launch traced here: 59.9 us
  starting transfers between devices  25.6 us (43%)
  waiting for transfers between devices  20 us (33%)
  Pallas kernels  11.5 us (19%)
  other arithmetic  1.98 us (3%)
  between operations  0.75 us (1%)
    ppermute x11, starting transfers between devices, swap(): return lax.ppermute(chunk, 'seq', [(i, i ^ flip) for i in range(count)])  17.5 us
    ppermute x11, waiting for transfers between devices, swap(): return lax.ppermute(chunk, 'seq', [(i, i ^ flip) for i in range(count)])  17.2 us
    all_to_all x1, starting transfers between devices, swapped(): arrived = lax.all_to_all(shares, every, 0, 0, tiled=True)  5.03 us
    pallas_call x3, Pallas kernels, call(): pl.pallas_call(body, in_specs=[pl.BlockSpec(memory_space=pltpu.SMEM)] + v...  4.96 us
    pallas_call x2, Pallas kernels, gate_outputs(): pl.pallas_call(lambda *refs: outputs_kernel(js, *refs), in_specs=[pl.Bloc...  3.36 us
    pallas_call x1, Pallas kernels, swapped(): pl.pallas_call(lambda *refs: sums_kernel(quarters, dp_count, *refs), in_s...  3.15 us
    ppermute x3, starting transfers between devices, swapped(): lax.ppermute(taps, 'dp', [(i, i ^ p) for i in range(dp_count)])  3.12 us
    select_n x1, other arithmetic, swapped(): a, b = (jnp.where(lower, mixed, gated), jnp.where(lower, gated, mixed))  1.9 us
  transfers between devices with their start and end apart: 16, of which 8 were waited for; matrix products, arithmetic and copies ran while one was open for 3% of the time, Pallas kernels for 10%

profile of v6, /device:TPU:0, one launch (start us, length us, event | category | flops | bytes accessed | tf_op | source)
XLA Modules:
  0.0 59.9 jit_solution(17007172833427690685)
XLA Ops:
  0.6 2.4 %collective-permute-start.2 = (bf16[16,32]{1,0:T(8,128)(2,1)}, bf16[16,32]{1,0:T(8,128)(2,1)S(1)}, u32[]{:S(2)}, u32[]{:S(2)}) collective-permute-start(bf16[16,32]{1,0:T(8,128)(2,1)} %bitcast.14), channel_id=1, source_target_pairs={{0,24},{8,16},{16,8},{24,0},{1,25},{9,17},{17,9},{25,1},{2,26},{10... | collective-permute-start | bytes 3080 | tf_op jit(solution)/shard_map/ppermute | solution.py:453
  3.8 1.9 %select_bitcast_fusion = (bf16[128,2048]{1,0:T(8,128)(2,1)S(1)}, bf16[128,2048]{1,0:T(8,128)(2,1)S(1)}) fusion(pred[]{:T(512)S(6)} %lt.10, bf16[1,128,2048]{2,1,0:T(8,128)(2,1)} %refs_5_.3, bf16[1,128,2048]{2,1,0:T(8,128)(2,1)} %refs_3_.3, bf16[1,128,2048]{2,1,0:T(8,128)(2,1)} %refs_4_.3, bf16[1,128,2048]{2,1,0:T(8,128)(2,1)} %refs_6_.3), kind=kLoop, calls=%fused_computation.2 | loop fusion | flops 2621440 | bytes 3145729 | tf_op jit(solution)/shard_map/jit(_where)/select_n | solution.py:459
  5.8 1.1 %collective-permute-done.1.refs_2_ = bf16[16,32]{1,0:T(8,128)(2,1)S(1)} collective-permute-done((bf16[16,32]{1,0:T(8,128)(2,1)}, bf16[16,32]{1,0:T(8,128)(2,1)S(1)}, u32[]{:S(2)}, u32[]{:S(2)}) %collective-permute-start.1) | collective-permute-done | bytes 1056 | tf_op jit(solution)/shard_map/ppermute | solution.py:453
  6.9 0.8 %pack.1 = (bf16[528,128]{1,0:T(8,128)(2,1)S(1)}, bf16[528,128]{1,0:T(8,128)(2,1)S(1)}, bf16[528,128]{1,0:T(8,128)(2,1)S(1)}, bf16[528,128]{1,0:T(8,128)(2,1)S(1)...) custom-call(s32[3]{0:T(128)S(1)} %pad_add_fusion.place_ref.refs_0_, ...), custom_call_target="tpu_custom_call" | custom-call | flops 1000 | bytes 1000 | tf_op jit(solution)/shard_map/pack/pallas_call | solution.py:158
  7.7 2.6 %collective-permute-start.6 = (bf16[528,128]{1,0:T(8,128)(2,1)S(1)}, bf16[528,128]{1,0:T(8,128)(2,1)S(1)}, u32[]{:S(2)}, u32[]{:S(2)}) collective-permute-start(bf16[528,128]{1,0:T(8,128)(2,1)S(1)} %get-tuple-element.29), channel_id=1, source_target_pairs={{0,3},{1,2},{2,1},{3,0},{4,7},{5,6},{6,5},{7,4},{8,11},{9,10},{10,... | collective-permute-start | bytes 405512 | tf_op jit(solution)/shard_map/ppermute | solution.py:143
  10.3 2.6 %collective-permute-start.7 = (bf16[528,128]{1,0:T(8,128)(2,1)S(1)}, bf16[528,128]{1,0:T(8,128)(2,1)S(1)}, u32[]{:S(2)}, u32[]{:S(2)}) collective-permute-start(bf16[528,128]{1,0:T(8,128)(2,1)S(1)} %get-tuple-element.30), channel_id=1, source_target_pairs={{0,4},{1,5},{2,6},{3,7},{4,0},{5,1},{6,2},{7,3},{8,12},{9,13},{10,... | collective-permute-start | bytes 405512 | tf_op jit(solution)/shard_map/ppermute | solution.py:143
  13.2 1.5 %collective-permute-start.3 = (bf16[1040,128]{1,0:T(8,128)(2,1)S(1)}, bf16[1040,128]{1,0:T(8,128)(2,1)S(1)}, u32[]{:S(2)}, u32[]{:S(2)}) collective-permute-start(bf16[1040,128]{1,0:T(8,128)(2,1)S(1)} %get-tuple-element.26), channel_id=1, source_target_pairs={{0,1},{1,0},{2,3},{3,2},{4,5},{5,4},{6,7},{7,6},{8,9},{9,8},{10,11... | collective-permute-start | bytes 798728 | tf_op jit(solution)/shard_map/ppermute | solution.py:143
  15.2 1.4 %collective-permute-done.6.refs_5_.refs_4_ = bf16[528,128]{1,0:T(8,128)(2,1)S(1)} collective-permute-done((bf16[528,128]{1,0:T(8,128)(2,1)S(1)}, bf16[528,128]{1,0:T(8,128)(2,1)S(1)}, u32[]{:S(2)}, u32[]{:S(2)}) %collective-permute-start.6) | collective-permute-done | bytes 135200 | tf_op jit(solution)/shard_map/ppermute | solution.py:143
  16.6 3.5 %collective-permute-start.9 = (bf16[528,128]{1,0:T(8,128)(2,1)S(1)}, bf16[528,128]{1,0:T(8,128)(2,1)S(1)}, u32[]{:S(2)}, u32[]{:S(2)}) collective-permute-start(bf16[528,128]{1,0:T(8,128)(2,1)S(1)} %get-tuple-element.32), channel_id=1, source_target_pairs={{0,6},{1,7},{2,4},{3,5},{4,2},{5,3},{6,0},{7,1},{8,14},{9,15},{10,... | collective-permute-start | bytes 405512 | tf_op jit(solution)/shard_map/ppermute | solution.py:143
  20.1 3.2 %collective-permute-done.7.refs_6_.refs_5_ = bf16[528,128]{1,0:T(8,128)(2,1)S(1)} collective-permute-done((bf16[528,128]{1,0:T(8,128)(2,1)S(1)}, bf16[528,128]{1,0:T(8,128)(2,1)S(1)}, u32[]{:S(2)}, u32[]{:S(2)}) %collective-permute-start.7) | collective-permute-done | bytes 135200 | tf_op jit(solution)/shard_map/ppermute | solution.py:143
  23.3 2.6 %collective-permute-start.10 = (bf16[528,128]{1,0:T(8,128)(2,1)S(1)}, bf16[528,128]{1,0:T(8,128)(2,1)S(1)}, u32[]{:S(2)}, u32[]{:S(2)}) collective-permute-start(bf16[528,128]{1,0:T(8,128)(2,1)S(1)} %get-tuple-element.28), channel_id=1, source_target_pairs={{0,7},{1,6},{2,5},{3,4},{4,3},{5,2},{6,1},{7,0},{8,15},{9,14},{10,... | collective-permute-start | bytes 405512 | tf_op jit(solution)/shard_map/ppermute | solution.py:143
  25.9 5.9 %collective-permute-done.9.refs_8_.refs_7_ = bf16[528,128]{1,0:T(8,128)(2,1)S(1)} collective-permute-done((bf16[528,128]{1,0:T(8,128)(2,1)S(1)}, bf16[528,128]{1,0:T(8,128)(2,1)S(1)}, u32[]{:S(2)}, u32[]{:S(2)}) %collective-permute-start.9) | collective-permute-done | bytes 135200 | tf_op jit(solution)/shard_map/ppermute | solution.py:143
  31.8 2.8 %collective-permute-done.10.refs_9_.refs_8_ = bf16[528,128]{1,0:T(8,128)(2,1)S(1)} collective-permute-done((bf16[528,128]{1,0:T(8,128)(2,1)S(1)}, bf16[528,128]{1,0:T(8,128)(2,1)S(1)}, u32[]{:S(2)}, u32[]{:S(2)}) %collective-permute-start.10) | collective-permute-done | bytes 135200 | tf_op jit(solution)/shard_map/ppermute | solution.py:143
  34.6 1.6 %collective-permute-done.5.refs_4_.refs_3_ = bf16[528,128]{1,0:T(8,128)(2,1)S(1)} collective-permute-done((bf16[528,128]{1,0:T(8,128)(2,1)S(1)}, bf16[528,128]{1,0:T(8,128)(2,1)S(1)}, u32[]{:S(2)}, u32[]{:S(2)}) %collective-permute-start.5) | collective-permute-done | bytes 135200 | tf_op jit(solution)/shard_map/ppermute | solution.py:143
  36.2 3.1 %sums.1 = (bf16[1024,128]{1,0:T(8,128)(2,1)S(1)}, bf16[1024,128]{1,0:T(8,128)(2,1)}, bf16[1024,128]{1,0:T(8,128)(2,1)S(1)}, bf16[1024,128]{1,0:T(8,128)(2,1)}) custom-call(s32[3]{0:T(128)S(1)} %pad_add_fusion.place_ref.refs_0_, bf16[1040,128]{1,0:T(8,128)(2,1)S(1)} %get-tuple-element.25.refs_1_.refs_0_, ...), custom_call_target="tpu_custom_call" | custom-call | flops 1000 | bytes 1000 | tf_op jit(solution)/shard_map/sums/pallas_call | solution.py:476
  39.3 3.1 %collective-permute-start.13 = (bf16[1024,128]{1,0:T(8,128)(2,1)}, bf16[1024,128]{1,0:T(8,128)(2,1)S(1)}, u32[]{:S(2)}, u32[]{:S(2)}) collective-permute-start(bf16[1024,128]{1,0:T(8,128)(2,1)} %get-tuple-element.36), channel_id=1, source_target_pairs={{0,3},{1,2},{2,1},{3,0},{4,7},{5,6},{6,5},{7,4},{8,11},{9,10},{10,... | collective-permute-start | bytes 786440 | tf_op jit(solution)/shard_map/ppermute | solution.py:143
  42.4 0.8 %collective-permute-start.11 = (bf16[1024,128]{1,0:T(8,128)(2,1)}, bf16[1024,128]{1,0:T(8,128)(2,1)S(1)}, u32[]{:S(2)}, u32[]{:S(2)}) collective-permute-start(bf16[1024,128]{1,0:T(8,128)(2,1)} %get-tuple-element.33), channel_id=1, source_target_pairs={{0,1},{1,0},{2,3},{3,2},{4,5},{5,4},{6,7},{7,6},{8,9},{9,8},{10,11... | collective-permute-start | bytes 786440 | tf_op jit(solution)/shard_map/ppermute | solution.py:143
  43.2 2.9 %lags.1 = f32[32,128]{1,0:T(8,128)} custom-call(s32[3]{0:T(128)S(1)} %pad_add_fusion.place_ref.refs_0_, bf16[1040,128]{1,0:T(8,128)(2,1)S(1)} %get-tuple-element.25.refs_1_.refs_0_, bf16[1040,128]{1,0:T(8,128)(2,1)S(1)} %collective-permute-done.3.refs_2_.refs_1_, bf16[1040,128]{1,0:T(8,128)(2,1)S(1)} %collective-permute-done.4.refs_3_.refs_2_, ...), custom_call_target="tpu_custom_call" | custom-call | flops 1000 | bytes 1000 | tf_op jit(solution)/shard_map/lags/pallas_call | solution.py:158
  46.2 5.0 %all-to-all-start = ((f32[32,1,128]{2,1,0:T(1,128)}), f32[32,1,128]{2,1,0:T(1,128)S(1)}, u32[]{:S(2)}, u32[]{:S(2)}) async-start(f32[32,1,128]{2,1,0:T(1,128)} %bitcast.7), calls=%async_computation | async-start | bytes 32768 | tf_op jit(solution)/shard_map/all_to_all | solution.py:496
  51.3 1.7 %outputs.2 = (bf16[1,128,2048]{2,1,0:T(8,128)(2,1)}, bf16[1,128,2048]{2,1,0:T(8,128)(2,1)}, bf16[1,128,2048]{2,1,0:T(8,128)(2,1)}, bf16[1,128,2048]{2,1,0:T(8,128)(2,1)}) custom-call(s32[3]{0:T(128)S(1)} %pad_add_fusion.place_ref.refs_0_, bf16[1024,128]{1,0:T(8,128)(2,1)S(1)} %get-tuple-element.35.refs_1_, ...), custom_call_target="tpu_custom_call" | custom-call | flops 1000 | bytes 1000 | tf_op jit(solution)/shard_map/outputs/pallas_call | solution.py:425
  52.9 2.3 %collective-permute-done.11.refs_1_ = bf16[1024,128]{1,0:T(8,128)(2,1)S(1)} collective-permute-done((bf16[1024,128]{1,0:T(8,128)(2,1)}, bf16[1024,128]{1,0:T(8,128)(2,1)S(1)}, u32[]{:S(2)}, u32[]{:S(2)}) %collective-permute-start.11) | collective-permute-done | bytes 262176 | tf_op jit(solution)/shard_map/ppermute | solution.py:143
  55.3 1.7 %outputs.3 = (bf16[1,128,2048]{2,1,0:T(8,128)(2,1)}, bf16[1,128,2048]{2,1,0:T(8,128)(2,1)}, bf16[1,128,2048]{2,1,0:T(8,128)(2,1)}, bf16[1,128,2048]{2,1,0:T(8,128)(2,1)}) custom-call(s32[3]{0:T(128)S(1)} %pad_add_fusion.place_ref.refs_0_, ...), custom_call_target="tpu_custom_call", output_to_operand_aliasing={{0}: (7, {}), {1}: (8, {}), {2}: (9, {}), {3}: (10, {})} | custom-call | flops 1000 | bytes 1000 | tf_op jit(solution)/shard_map/outputs/pallas_call | solution.py:425
  56.9 1.7 %all-to-all-done = f32[32,1,128]{2,1,0:T(1,128)S(1)} async-done(((f32[32,1,128]{2,1,0:T(1,128)}), f32[32,1,128]{2,1,0:T(1,128)S(1)}, u32[]{:S(2)}, u32[]{:S(2)}) %all-to-all-start) | async-done | bytes 16416 | tf_op jit(solution)/shard_map/all_to_all | solution.py:496
  58.6 1.2 %owned.1 = f32[16,32]{1,0:T(8,128)} custom-call(s32[3]{0:T(128)S(1)} %pad_add_fusion.place_ref.refs_0_, f32[32,128]{1,0:T(8,128)S(1)} %bitcast.13), custom_call_target="tpu_custom_call" | custom-call | flops 1000 | bytes 1000 | tf_op jit(solution)/shard_map/owned/pallas_call | solution.py:158
  (26 shorter events, 1.5 us)
Async XLA Ops:
  0.6 5.1 %collective-permute-start.2 = (bf16[16,32]{1,0:T(8,128)(2,1)}, bf16[16,32]{1,0:T(8,128)(2,1)S(1)}, u32[]{:S(2)}, u32[]{:S(2)}) collective-permute-start(bf16[16,32]{1,0:T(8,128)(2,1)} %bitcast.14), channel_id=1, source_target_pairs={{0,24},{8,16},{16,8},{24,0},{1,25},{9,17},{17,9},{25,1},{2,26},{10... | collective-permute-start | bytes 3080 | tf_op jit(solution)/shard_map/ppermute | solution.py:453
  3.1 3.8 %collective-permute-start.1 = (bf16[16,32]{1,0:T(8,128)(2,1)}, bf16[16,32]{1,0:T(8,128)(2,1)S(1)}, u32[]{:S(2)}, u32[]{:S(2)}) collective-permute-start(bf16[16,32]{1,0:T(8,128)(2,1)} %bitcast.15), channel_id=1, source_target_pairs={{0,16},{8,24},{16,0},{24,8},{1,17},{9,25},{17,1},{25,9},{2,18},{10... | collective-permute-start | bytes 3080 | tf_op jit(solution)/shard_map/ppermute | solution.py:453
  3.7 3.2 %collective-permute-start = (bf16[16,32]{1,0:T(8,128)(2,1)}, bf16[16,32]{1,0:T(8,128)(2,1)S(1)}, u32[]{:S(2)}, u32[]{:S(2)}) collective-permute-start(bf16[16,32]{1,0:T(8,128)(2,1)} %bitcast.16), channel_id=1, source_target_pairs={{0,8},{8,0},{16,24},{24,16},{1,9},{9,1},{17,25},{25,17},{2,10},{10... | collective-permute-start | bytes 3080 | tf_op jit(solution)/shard_map/ppermute | solution.py:453
  5.7 1.2 %copy-start.4 = (bf16[32,16]{0,1:T(8,128)(2,1)S(1)}, bf16[32,16]{0,1:T(8,128)(2,1)}, u32[]{:S(2)}) copy-start(bf16[32,16]{0,1:T(8,128)(2,1)} %param.9) | copy-start | bytes 3076
  7.7 8.9 %collective-permute-start.6 = (bf16[528,128]{1,0:T(8,128)(2,1)S(1)}, bf16[528,128]{1,0:T(8,128)(2,1)S(1)}, u32[]{:S(2)}, u32[]{:S(2)}) collective-permute-start(bf16[528,128]{1,0:T(8,128)(2,1)S(1)} %get-tuple-element.29), channel_id=1, source_target_pairs={{0,3},{1,2},{2,1},{3,0},{4,7},{5,6},{6,5},{7,4},{8,11},{9,10},{10,... | collective-permute-start | bytes 405512 | tf_op jit(solution)/shard_map/ppermute | solution.py:143
  10.3 13.0 %collective-permute-start.7 = (bf16[528,128]{1,0:T(8,128)(2,1)S(1)}, bf16[528,128]{1,0:T(8,128)(2,1)S(1)}, u32[]{:S(2)}, u32[]{:S(2)}) collective-permute-start(bf16[528,128]{1,0:T(8,128)(2,1)S(1)} %get-tuple-element.30), channel_id=1, source_target_pairs={{0,4},{1,5},{2,6},{3,7},{4,0},{5,1},{6,2},{7,3},{8,12},{9,13},{10,... | collective-permute-start | bytes 405512 | tf_op jit(solution)/shard_map/ppermute | solution.py:143
  12.9 12.9 %collective-permute-start.8 = (bf16[528,128]{1,0:T(8,128)(2,1)S(1)}, bf16[528,128]{1,0:T(8,128)(2,1)S(1)}, u32[]{:S(2)}, u32[]{:S(2)}) collective-permute-start(bf16[528,128]{1,0:T(8,128)(2,1)S(1)} %get-tuple-element.31), channel_id=1, source_target_pairs={{0,5},{1,4},{2,7},{3,6},{4,1},{5,0},{6,3},{7,2},{8,13},{9,12},{10,... | collective-permute-start | bytes 405512 | tf_op jit(solution)/shard_map/ppermute | solution.py:143
  13.2 23.0 %collective-permute-start.3 = (bf16[1040,128]{1,0:T(8,128)(2,1)S(1)}, bf16[1040,128]{1,0:T(8,128)(2,1)S(1)}, u32[]{:S(2)}, u32[]{:S(2)}) collective-permute-start(bf16[1040,128]{1,0:T(8,128)(2,1)S(1)} %get-tuple-element.26), channel_id=1, source_target_pairs={{0,1},{1,0},{2,3},{3,2},{4,5},{5,4},{6,7},{7,6},{8,9},{9,8},{10,11... | collective-permute-start | bytes 798728 | tf_op jit(solution)/shard_map/ppermute | solution.py:143
  14.7 21.4 %collective-permute-start.4 = (bf16[1040,128]{1,0:T(8,128)(2,1)S(1)}, bf16[1040,128]{1,0:T(8,128)(2,1)S(1)}, u32[]{:S(2)}, u32[]{:S(2)}) collective-permute-start(bf16[1040,128]{1,0:T(8,128)(2,1)S(1)} %get-tuple-element.27), channel_id=1, source_target_pairs={{0,2},{1,3},{2,0},{3,1},{4,6},{5,7},{6,4},{7,5},{8,10},{9,11},{10,... | collective-permute-start | bytes 798728 | tf_op jit(solution)/shard_map/ppermute | solution.py:143
  16.6 15.2 %collective-permute-start.9 = (bf16[528,128]{1,0:T(8,128)(2,1)S(1)}, bf16[528,128]{1,0:T(8,128)(2,1)S(1)}, u32[]{:S(2)}, u32[]{:S(2)}) collective-permute-start(bf16[528,128]{1,0:T(8,128)(2,1)S(1)} %get-tuple-element.32), channel_id=1, source_target_pairs={{0,6},{1,7},{2,4},{3,5},{4,2},{5,3},{6,0},{7,1},{8,14},{9,15},{10,... | collective-permute-start | bytes 405512 | tf_op jit(solution)/shard_map/ppermute | solution.py:143
  23.3 11.3 %collective-permute-start.10 = (bf16[528,128]{1,0:T(8,128)(2,1)S(1)}, bf16[528,128]{1,0:T(8,128)(2,1)S(1)}, u32[]{:S(2)}, u32[]{:S(2)}) collective-permute-start(bf16[528,128]{1,0:T(8,128)(2,1)S(1)} %get-tuple-element.28), channel_id=1, source_target_pairs={{0,7},{1,6},{2,5},{3,4},{4,3},{5,2},{6,1},{7,0},{8,15},{9,14},{10,... | collective-permute-start | bytes 405512 | tf_op jit(solution)/shard_map/ppermute | solution.py:143
  25.8 10.3 %collective-permute-start.5 = (bf16[528,128]{1,0:T(8,128)(2,1)S(1)}, bf16[528,128]{1,0:T(8,128)(2,1)S(1)}, u32[]{:S(2)}, u32[]{:S(2)}) collective-permute-start(bf16[528,128]{1,0:T(8,128)(2,1)S(1)} %get-tuple-element.28), channel_id=1, source_target_pairs={{0,3},{1,2},{2,1},{3,0},{4,7},{5,6},{6,5},{7,4},{8,11},{9,10},{10,... | collective-permute-start | bytes 405512 | tf_op jit(solution)/shard_map/ppermute | solution.py:143
  36.1 15.1 %copy-start.3 = (bf16[1,128,2048]{2,1,0:T(8,128)(2,1)S(1)}, bf16[1,128,2048]{2,1,0:T(8,128)(2,1)}, u32[]{:S(2)}) copy-start(bf16[1,128,2048]{2,1,0:T(8,128)(2,1)} %refs_6_.3) | copy-start | bytes 1572868
  39.3 3.9 %collective-permute-start.14 = (bf16[1024,128]{1,0:T(8,128)(2,1)S(1)}, bf16[1024,128]{1,0:T(8,128)(2,1)S(1)}, u32[]{:S(2)}, u32[]{:S(2)}) collective-permute-start(bf16[1024,128]{1,0:T(8,128)(2,1)S(1)} %get-tuple-element.35.refs_1_), channel_id=1, source_target_pairs={{0,8},{8,0},{16,24},{24,16},{1,9},{9,1},{17,25},{25,17},{2,10},{10... | collective-permute-start | bytes 786440 | tf_op jit(solution)/shard_map/ppermute | solution.py:490
  39.3 11.9 %collective-permute-start.13 = (bf16[1024,128]{1,0:T(8,128)(2,1)}, bf16[1024,128]{1,0:T(8,128)(2,1)S(1)}, u32[]{:S(2)}, u32[]{:S(2)}) collective-permute-start(bf16[1024,128]{1,0:T(8,128)(2,1)} %get-tuple-element.36), channel_id=1, source_target_pairs={{0,3},{1,2},{2,1},{3,0},{4,7},{5,6},{6,5},{7,4},{8,11},{9,10},{10,... | collective-permute-start | bytes 786440 | tf_op jit(solution)/shard_map/ppermute | solution.py:143
  42.4 12.8 %collective-permute-start.11 = (bf16[1024,128]{1,0:T(8,128)(2,1)}, bf16[1024,128]{1,0:T(8,128)(2,1)S(1)}, u32[]{:S(2)}, u32[]{:S(2)}) collective-permute-start(bf16[1024,128]{1,0:T(8,128)(2,1)} %get-tuple-element.33), channel_id=1, source_target_pairs={{0,1},{1,0},{2,3},{3,2},{4,5},{5,4},{6,7},{7,6},{8,9},{9,8},{10,11... | collective-permute-start | bytes 786440 | tf_op jit(solution)/shard_map/ppermute | solution.py:143
  43.2 8.0 %copy-start = (bf16[1,128,2048]{2,1,0:T(8,128)(2,1)S(1)}, bf16[1,128,2048]{2,1,0:T(8,128)(2,1)}, u32[]{:S(2)}) copy-start(bf16[1,128,2048]{2,1,0:T(8,128)(2,1)} %refs_5_.3) | copy-start | bytes 1572868
  43.2 8.0 %copy-start.1 = (bf16[1,128,2048]{2,1,0:T(8,128)(2,1)S(1)}, bf16[1,128,2048]{2,1,0:T(8,128)(2,1)}, u32[]{:S(2)}) copy-start(bf16[1,128,2048]{2,1,0:T(8,128)(2,1)} %refs_3_.3) | copy-start | bytes 1572868
  43.2 8.0 %copy-start.2 = (bf16[1,128,2048]{2,1,0:T(8,128)(2,1)S(1)}, bf16[1,128,2048]{2,1,0:T(8,128)(2,1)}, u32[]{:S(2)}) copy-start(bf16[1,128,2048]{2,1,0:T(8,128)(2,1)} %refs_4_.3) | copy-start | bytes 1572868
  43.2 12.0 %collective-permute-start.12 = (bf16[1024,128]{1,0:T(8,128)(2,1)S(1)}, bf16[1024,128]{1,0:T(8,128)(2,1)S(1)}, u32[]{:S(2)}, u32[]{:S(2)}) collective-permute-start(bf16[1024,128]{1,0:T(8,128)(2,1)S(1)} %get-tuple-element.34), channel_id=1, source_target_pairs={{0,2},{1,3},{2,0},{3,1},{4,6},{5,7},{6,4},{7,5},{8,10},{9,11},{10,... | collective-permute-start | bytes 786440 | tf_op jit(solution)/shard_map/ppermute | solution.py:143
  46.2 12.5 %all-to-all-start = ((f32[32,1,128]{2,1,0:T(1,128)}), f32[32,1,128]{2,1,0:T(1,128)S(1)}, u32[]{:S(2)}, u32[]{:S(2)}) async-start(f32[32,1,128]{2,1,0:T(1,128)} %bitcast.7), calls=%async_computation | async-start | bytes 32768 | tf_op jit(solution)/shard_map/all_to_all | solution.py:496

commit v7 on v6

--- a/solution.py
+++ b/solution.py
@@ -170,6 +170,7 @@
 
 
 TAIL = 16
+SPLIT = 2
 
 
 def pack_kernel(quarters, pieces, place_ref, *refs):
@@ -186,7 +187,7 @@
             columns = pl.ds(pl.multiple_of(((quarter ^ j) * local + g) * BLOCK, BLOCK), BLOCK)
             a = a_ref[:, columns]
             a_outs[j][g * BLOCK : (g + 1) * BLOCK] = a
-            if j < quarters - 1:
+            if j != SPLIT:
                 outs[j][g * BLOCK : (g + 1) * BLOCK] = a
                 outs[j][(local + g) * BLOCK : (local + g + 1) * BLOCK] = b_ref[:, columns]
             else:
@@ -294,7 +295,7 @@
     half, quarter = place_ref[0], place_ref[1]
     local = a_ref.shape[2] // BLOCK
     for j in range(quarters):
-        b_in, b_row = (ab_in[j], local) if j < quarters - 1 else (ab_in[j + 1], 0)
+        b_in, b_row = (ab_in[j], local) if j != SPLIT else (ab_in[quarters], 0)
         for g in range(local):
             lanes = slice(g * BLOCK, (g + 1) * BLOCK)
             a_ref[quarter ^ j, :, lanes] = ab_in[j][g * BLOCK : (g + 1) * BLOCK]
@@ -462,13 +463,13 @@
     message = jax.ShapeDtypeStruct((2 * local * BLOCK + TAIL, BLOCK), bf16)
     chunks = call(
         lambda *refs: pack_kernel(quarters, dp_count, *refs), "pack", place, pieces + [a, b],
-        [short] * quarters + [message] * (quarters - 1) + [short], [pltpu.VMEM((quarters, local, BLOCK), f32)],
+        [short] * quarters + [short if j == SPLIT else message for j in range(quarters)], [pltpu.VMEM((quarters, local, BLOCK), f32)],
         flops=1000, nbytes=1000,
     )
     a_own, ab_own = chunks[:quarters], chunks[quarters:]
     r_in = [swap(a_own[j], quarters + j) for j in range(quarters)]
-    ab_in = [ab_own[0]] + [swap(ab_own[j], j) for j in range(1, quarters - 1)]
-    ab_in += [swap(a_own[-1], quarters - 1), swap(ab_own[-1], quarters - 1)]
+    ab_in = [ab_own[0]] + [swap(a_own[j] if j == SPLIT else ab_own[j], j) for j in range(1, quarters)]
+    ab_in.append(swap(ab_own[SPLIT], SPLIT))
 
     band = pltpu.VMEM((local, 2 * BLOCK, K), bf16)
     store = pltpu.VMEM((quarters, BLOCK, width), bf16)

time: 60 us -> 58.3 us (0.972)
  waiting for transfers between devices: 20 us -> 16.5 us
  starting transfers between devices: 25.6 us -> 27.4 us
    ppermute x11, starting transfers between devices: 17.5 us -> 19.9 us  [swap(): return lax.ppermute(chunk, 'seq', [(i, i ^ flip) for i in range(count)])]
    ppermute x11, waiting for transfers between devices: 17.2 us -> 14.8 us  [swap(): return lax.ppermute(chunk, 'seq', [(i, i ^ flip) for i in range(count)])]
    all_to_all x1, waiting for transfers between devices: 1.69 us -> 0.59 us  [swapped(): arrived = lax.all_to_all(shares, every, 0, 0, tiled=True)]
    all_to_all x1, starting transfers between devices: 5.03 us -> 4.33 us  [swapped(): arrived = lax.all_to_all(shares, every, 0, 0, tiled=True)]
  transfers between devices with their start and end apart: 16 -> 16, of which waited for: 8 -> 9; matrix products, arithmetic and copies ran while one was open for 3% -> 3% of each run, Pallas kernels for 10% -> 11%
where the time goes in v7:
time: 58.3 us; the launch traced here: 58.1 us
  starting transfers between devices  27.4 us (47%)
  waiting for transfers between devices  16.5 us (28%)
  Pallas kernels  11.5 us (20%)
  other arithmetic  1.98 us (3%)
  between operations  0.74 us (1%)
    ppermute x11, starting transfers between devices, swap(): return lax.ppermute(chunk, 'seq', [(i, i ^ flip) for i in range(count)])  19.9 us
    ppermute x11, waiting for transfers between devices, swap(): return lax.ppermute(chunk, 'seq', [(i, i ^ flip) for i in range(count)])  14.8 us
    pallas_call x3, Pallas kernels, call(): pl.pallas_call(body, in_specs=[pl.BlockSpec(memory_space=pltpu.SMEM)] + v...  4.94 us
    all_to_all x1, starting transfers between devices, swapped(): arrived = lax.all_to_all(shares, every, 0, 0, tiled=True)  4.33 us
    pallas_call x2, Pallas kernels, gate_outputs(): pl.pallas_call(lambda *refs: outputs_kernel(js, *refs), in_specs=[pl.Bloc...  3.36 us
    pallas_call x1, Pallas kernels, swapped(): pl.pallas_call(lambda *refs: sums_kernel(quarters, dp_count, *refs), in_s...  3.15 us
    ppermute x3, starting transfers between devices, swapped(): lax.ppermute(taps, 'dp', [(i, i ^ p) for i in range(dp_count)])  3.12 us
    select_n x1, other arithmetic, swapped(): a, b = (jnp.where(lower, mixed, gated), jnp.where(lower, gated, mixed))  1.9 us
  transfers between devices with their start and end apart: 16, of which 9 were waited for; matrix products, arithmetic and copies ran while one was open for 3% of the time, Pallas kernels for 11%

profile of v7, /device:TPU:0, one launch (start us, length us, event | category | flops | bytes accessed | tf_op | source)
XLA Modules:
  0.0 58.1 jit_solution(17750934589675343306)
XLA Ops:
  0.6 2.4 %collective-permute-start.2 = (bf16[16,32]{1,0:T(8,128)(2,1)}, bf16[16,32]{1,0:T(8,128)(2,1)S(1)}, u32[]{:S(2)}, u32[]{:S(2)}) collective-permute-start(bf16[16,32]{1,0:T(8,128)(2,1)} %bitcast.14), channel_id=1, source_target_pairs={{0,24},{8,16},{16,8},{24,0},{1,25},{9,17},{17,9},{25,1},{2,26},{10... | collective-permute-start | bytes 3080 | tf_op jit(solution)/shard_map/ppermute | solution.py:454
  3.1 0.6 %collective-permute-start.1 = (bf16[16,32]{1,0:T(8,128)(2,1)}, bf16[16,32]{1,0:T(8,128)(2,1)S(1)}, u32[]{:S(2)}, u32[]{:S(2)}) collective-permute-start(bf16[16,32]{1,0:T(8,128)(2,1)} %bitcast.15), channel_id=1, source_target_pairs={{0,16},{8,24},{16,0},{24,8},{1,17},{9,25},{17,1},{25,9},{2,18},{10... | collective-permute-start | bytes 3080 | tf_op jit(solution)/shard_map/ppermute | solution.py:454
  3.8 1.9 %select_bitcast_fusion = (bf16[128,2048]{1,0:T(8,128)(2,1)S(1)}, bf16[128,2048]{1,0:T(8,128)(2,1)S(1)}) fusion(pred[]{:T(512)S(6)} %lt.10, bf16[1,128,2048]{2,1,0:T(8,128)(2,1)} %refs_5_.3, bf16[1,128,2048]{2,1,0:T(8,128)(2,1)} %refs_3_.3, bf16[1,128,2048]{2,1,0:T(8,128)(2,1)} %refs_4_.3, bf16[1,128,2048]{2,1,0:T(8,128)(2,1)} %refs_6_.3), kind=kLoop, calls=%fused_computation.2 | loop fusion | flops 2621440 | bytes 3145729 | tf_op jit(solution)/shard_map/jit(_where)/select_n | solution.py:460
  5.8 1.1 %collective-permute-done.1.refs_2_ = bf16[16,32]{1,0:T(8,128)(2,1)S(1)} collective-permute-done((bf16[16,32]{1,0:T(8,128)(2,1)}, bf16[16,32]{1,0:T(8,128)(2,1)S(1)}, u32[]{:S(2)}, u32[]{:S(2)}) %collective-permute-start.1) | collective-permute-done | bytes 1056 | tf_op jit(solution)/shard_map/ppermute | solution.py:454
  6.9 0.8 %pack.1 = (bf16[528,128]{1,0:T(8,128)(2,1)S(1)}, bf16[528,128]{1,0:T(8,128)(2,1)S(1)}, bf16[528,128]{1,0:T(8,128)(2,1)S(1)}, bf16[528,128]{1,0:T(8,128)(2,1)S(1)...) custom-call(s32[3]{0:T(128)S(1)} %pad_add_fusion.place_ref.refs_0_, ...), custom_call_target="tpu_custom_call" | custom-call | flops 1000 | bytes 1000 | tf_op jit(solution)/shard_map/pack/pallas_call | solution.py:158
  7.7 1.6 %collective-permute-start.6 = (bf16[528,128]{1,0:T(8,128)(2,1)S(1)}, bf16[528,128]{1,0:T(8,128)(2,1)S(1)}, u32[]{:S(2)}, u32[]{:S(2)}) collective-permute-start(bf16[528,128]{1,0:T(8,128)(2,1)S(1)} %get-tuple-element.29), channel_id=1, source_target_pairs={{0,2},{1,3},{2,0},{3,1},{4,6},{5,7},{6,4},{7,5},{8,10},{9,11},{10,... | collective-permute-start | bytes 405512 | tf_op jit(solution)/shard_map/ppermute | solution.py:143
  9.4 2.6 %collective-permute-start.7 = (bf16[528,128]{1,0:T(8,128)(2,1)S(1)}, bf16[528,128]{1,0:T(8,128)(2,1)S(1)}, u32[]{:S(2)}, u32[]{:S(2)}) collective-permute-start(bf16[528,128]{1,0:T(8,128)(2,1)S(1)} %get-tuple-element.30), channel_id=1, source_target_pairs={{0,4},{1,5},{2,6},{3,7},{4,0},{5,1},{6,2},{7,3},{8,12},{9,13},{10,... | collective-permute-start | bytes 405512 | tf_op jit(solution)/shard_map/ppermute | solution.py:143
  12.0 1.3 %collective-permute-start.8 = (bf16[528,128]{1,0:T(8,128)(2,1)S(1)}, bf16[528,128]{1,0:T(8,128)(2,1)S(1)}, u32[]{:S(2)}, u32[]{:S(2)}) collective-permute-start(bf16[528,128]{1,0:T(8,128)(2,1)S(1)} %get-tuple-element.31), channel_id=1, source_target_pairs={{0,5},{1,4},{2,7},{3,6},{4,1},{5,0},{6,3},{7,2},{8,13},{9,12},{10,... | collective-permute-start | bytes 405512 | tf_op jit(solution)/shard_map/ppermute | solution.py:143
  13.8 1.4 %collective-permute-start.5 = (bf16[1040,128]{1,0:T(8,128)(2,1)S(1)}, bf16[1040,128]{1,0:T(8,128)(2,1)S(1)}, u32[]{:S(2)}, u32[]{:S(2)}) collective-permute-start(bf16[1040,128]{1,0:T(8,128)(2,1)S(1)} %get-tuple-element.28), channel_id=1, source_target_pairs={{0,3},{1,2},{2,1},{3,0},{4,7},{5,6},{6,5},{7,4},{8,11},{9,10},{10,... | collective-permute-start | bytes 798728 | tf_op jit(solution)/shard_map/ppermute | solution.py:143
  15.5 4.8 %collective-permute-start.10 = (bf16[528,128]{1,0:T(8,128)(2,1)S(1)}, bf16[528,128]{1,0:T(8,128)(2,1)S(1)}, u32[]{:S(2)}, u32[]{:S(2)}) collective-permute-start(bf16[528,128]{1,0:T(8,128)(2,1)S(1)} %get-tuple-element.32), channel_id=1, source_target_pairs={{0,7},{1,6},{2,5},{3,4},{4,3},{5,2},{6,1},{7,0},{8,15},{9,14},{10,... | collective-permute-start | bytes 405512 | tf_op jit(solution)/shard_map/ppermute | solution.py:143
  20.2 0.9 %collective-permute-done.7.refs_6_.refs_5_ = bf16[528,128]{1,0:T(8,128)(2,1)S(1)} collective-permute-done((bf16[528,128]{1,0:T(8,128)(2,1)S(1)}, bf16[528,128]{1,0:T(8,128)(2,1)S(1)}, u32[]{:S(2)}, u32[]{:S(2)}) %collective-permute-start.7) | collective-permute-done | bytes 135200 | tf_op jit(solution)/shard_map/ppermute | solution.py:143
  21.2 3.7 %collective-permute-start.9 = (bf16[528,128]{1,0:T(8,128)(2,1)S(1)}, bf16[528,128]{1,0:T(8,128)(2,1)S(1)}, u32[]{:S(2)}, u32[]{:S(2)}) collective-permute-start(bf16[528,128]{1,0:T(8,128)(2,1)S(1)} %get-tuple-element.27), channel_id=1, source_target_pairs={{0,6},{1,7},{2,4},{3,5},{4,2},{5,3},{6,0},{7,1},{8,14},{9,15},{10,... | collective-permute-start | bytes 405512 | tf_op jit(solution)/shard_map/ppermute | solution.py:143
  24.9 1.2 %collective-permute-done.8.refs_7_.refs_6_ = bf16[528,128]{1,0:T(8,128)(2,1)S(1)} collective-permute-done((bf16[528,128]{1,0:T(8,128)(2,1)S(1)}, bf16[528,128]{1,0:T(8,128)(2,1)S(1)}, u32[]{:S(2)}, u32[]{:S(2)}) %collective-permute-start.8) | collective-permute-done | bytes 135200 | tf_op jit(solution)/shard_map/ppermute | solution.py:143
  26.1 6.0 %collective-permute-done.10.refs_9_.refs_8_ = bf16[528,128]{1,0:T(8,128)(2,1)S(1)} collective-permute-done((bf16[528,128]{1,0:T(8,128)(2,1)S(1)}, bf16[528,128]{1,0:T(8,128)(2,1)S(1)}, u32[]{:S(2)}, u32[]{:S(2)}) %collective-permute-start.10) | collective-permute-done | bytes 135200 | tf_op jit(solution)/shard_map/ppermute | solution.py:143
  32.1 1.9 %collective-permute-done.9.refs_8_.refs_7_ = bf16[528,128]{1,0:T(8,128)(2,1)S(1)} collective-permute-done((bf16[528,128]{1,0:T(8,128)(2,1)S(1)}, bf16[528,128]{1,0:T(8,128)(2,1)S(1)}, u32[]{:S(2)}, u32[]{:S(2)}) %collective-permute-start.9) | collective-permute-done | bytes 135200 | tf_op jit(solution)/shard_map/ppermute | solution.py:143
  34.1 1.1 %collective-permute-done.4.refs_3_.refs_2_ = bf16[528,128]{1,0:T(8,128)(2,1)S(1)} collective-permute-done((bf16[528,128]{1,0:T(8,128)(2,1)S(1)}, bf16[528,128]{1,0:T(8,128)(2,1)S(1)}, u32[]{:S(2)}, u32[]{:S(2)}) %collective-permute-start.4) | collective-permute-done | bytes 135200 | tf_op jit(solution)/shard_map/ppermute | solution.py:143
  35.2 3.1 %sums.1 = (bf16[1024,128]{1,0:T(8,128)(2,1)S(1)}, bf16[1024,128]{1,0:T(8,128)(2,1)}, bf16[1024,128]{1,0:T(8,128)(2,1)S(1)}, bf16[1024,128]{1,0:T(8,128)(2,1)}) custom-call(s32[3]{0:T(128)S(1)} %pad_add_fusion.place_ref.refs_0_, bf16[1040,128]{1,0:T(8,128)(2,1)S(1)} %get-tuple-element.25.refs_1_.refs_0_, ...), custom_call_target="tpu_custom_call" | custom-call | flops 1000 | bytes 1000 | tf_op jit(solution)/shard_map/sums/pallas_call | solution.py:477
  38.3 3.4 %collective-permute-start.13 = (bf16[1024,128]{1,0:T(8,128)(2,1)}, bf16[1024,128]{1,0:T(8,128)(2,1)S(1)}, u32[]{:S(2)}, u32[]{:S(2)}) collective-permute-start(bf16[1024,128]{1,0:T(8,128)(2,1)} %get-tuple-element.36), channel_id=1, source_target_pairs={{0,3},{1,2},{2,1},{3,0},{4,7},{5,6},{6,5},{7,4},{8,11},{9,10},{10,... | collective-permute-start | bytes 786440 | tf_op jit(solution)/shard_map/ppermute | solution.py:143
  42.4 2.9 %lags.1 = f32[32,128]{1,0:T(8,128)} custom-call(s32[3]{0:T(128)S(1)} %pad_add_fusion.place_ref.refs_0_, bf16[1040,128]{1,0:T(8,128)(2,1)S(1)} %get-tuple-element.25.refs_1_.refs_0_, bf16[1040,128]{1,0:T(8,128)(2,1)S(1)} %collective-permute-done.3.refs_2_.refs_1_, bf16[528,128]{1,0:T(8,128)(2,1)S(1)} %collective-permute-done.4.refs_3_.refs_2_, ...), custom_call_target="tpu_custom_call" | custom-call | flops 1000 | bytes 1000 | tf_op jit(solution)/shard_map/lags/pallas_call | solution.py:158
  45.3 4.3 %all-to-all-start = ((f32[32,1,128]{2,1,0:T(1,128)}), f32[32,1,128]{2,1,0:T(1,128)S(1)}, u32[]{:S(2)}, u32[]{:S(2)}) async-start(f32[32,1,128]{2,1,0:T(1,128)} %bitcast.7), calls=%async_computation | async-start | bytes 32768 | tf_op jit(solution)/shard_map/all_to_all | solution.py:497
  49.7 1.7 %outputs.2 = (bf16[1,128,2048]{2,1,0:T(8,128)(2,1)}, bf16[1,128,2048]{2,1,0:T(8,128)(2,1)}, bf16[1,128,2048]{2,1,0:T(8,128)(2,1)}, bf16[1,128,2048]{2,1,0:T(8,128)(2,1)}) custom-call(s32[3]{0:T(128)S(1)} %pad_add_fusion.place_ref.refs_0_, bf16[1024,128]{1,0:T(8,128)(2,1)S(1)} %get-tuple-element.35.refs_1_, ...), custom_call_target="tpu_custom_call" | custom-call | flops 1000 | bytes 1000 | tf_op jit(solution)/shard_map/outputs/pallas_call | solution.py:426
  51.3 3.3 %collective-permute-done.11.refs_1_ = bf16[1024,128]{1,0:T(8,128)(2,1)S(1)} collective-permute-done((bf16[1024,128]{1,0:T(8,128)(2,1)}, bf16[1024,128]{1,0:T(8,128)(2,1)S(1)}, u32[]{:S(2)}, u32[]{:S(2)}) %collective-permute-start.11) | collective-permute-done | bytes 262176 | tf_op jit(solution)/shard_map/ppermute | solution.py:143
  54.6 1.7 %outputs.3 = (bf16[1,128,2048]{2,1,0:T(8,128)(2,1)}, bf16[1,128,2048]{2,1,0:T(8,128)(2,1)}, bf16[1,128,2048]{2,1,0:T(8,128)(2,1)}, bf16[1,128,2048]{2,1,0:T(8,128)(2,1)}) custom-call(s32[3]{0:T(128)S(1)} %pad_add_fusion.place_ref.refs_0_, ...), custom_call_target="tpu_custom_call", output_to_operand_aliasing={{0}: (7, {}), {1}: (8, {}), {2}: (9, {}), {3}: (10, {})} | custom-call | flops 1000 | bytes 1000 | tf_op jit(solution)/shard_map/outputs/pallas_call | solution.py:426
  56.9 1.2 %owned.1 = f32[16,32]{1,0:T(8,128)} custom-call(s32[3]{0:T(128)S(1)} %pad_add_fusion.place_ref.refs_0_, f32[32,128]{1,0:T(8,128)S(1)} %bitcast.13), custom_call_target="tpu_custom_call" | custom-call | flops 1000 | bytes 1000 | tf_op jit(solution)/shard_map/owned/pallas_call | solution.py:158
  (26 shorter events, 2.2 us)
Async XLA Ops:
  0.6 5.1 %collective-permute-start.2 = (bf16[16,32]{1,0:T(8,128)(2,1)}, bf16[16,32]{1,0:T(8,128)(2,1)S(1)}, u32[]{:S(2)}, u32[]{:S(2)}) collective-permute-start(bf16[16,32]{1,0:T(8,128)(2,1)} %bitcast.14), channel_id=1, source_target_pairs={{0,24},{8,16},{16,8},{24,0},{1,25},{9,17},{17,9},{25,1},{2,26},{10... | collective-permute-start | bytes 3080 | tf_op jit(solution)/shard_map/ppermute | solution.py:454
  3.1 3.8 %collective-permute-start.1 = (bf16[16,32]{1,0:T(8,128)(2,1)}, bf16[16,32]{1,0:T(8,128)(2,1)S(1)}, u32[]{:S(2)}, u32[]{:S(2)}) collective-permute-start(bf16[16,32]{1,0:T(8,128)(2,1)} %bitcast.15), channel_id=1, source_target_pairs={{0,16},{8,24},{16,0},{24,8},{1,17},{9,25},{17,1},{25,9},{2,18},{10... | collective-permute-start | bytes 3080 | tf_op jit(solution)/shard_map/ppermute | solution.py:454
  3.7 3.2 %collective-permute-start = (bf16[16,32]{1,0:T(8,128)(2,1)}, bf16[16,32]{1,0:T(8,128)(2,1)S(1)}, u32[]{:S(2)}, u32[]{:S(2)}) collective-permute-start(bf16[16,32]{1,0:T(8,128)(2,1)} %bitcast.16), channel_id=1, source_target_pairs={{0,8},{8,0},{16,24},{24,16},{1,9},{9,1},{17,25},{25,17},{2,10},{10... | collective-permute-start | bytes 3080 | tf_op jit(solution)/shard_map/ppermute | solution.py:454
  5.7 1.2 %copy-start.4 = (bf16[32,16]{0,1:T(8,128)(2,1)S(1)}, bf16[32,16]{0,1:T(8,128)(2,1)}, u32[]{:S(2)}) copy-start(bf16[32,16]{0,1:T(8,128)(2,1)} %param.9) | copy-start | bytes 3076
  7.7 7.8 %collective-permute-start.6 = (bf16[528,128]{1,0:T(8,128)(2,1)S(1)}, bf16[528,128]{1,0:T(8,128)(2,1)S(1)}, u32[]{:S(2)}, u32[]{:S(2)}) collective-permute-start(bf16[528,128]{1,0:T(8,128)(2,1)S(1)} %get-tuple-element.29), channel_id=1, source_target_pairs={{0,2},{1,3},{2,0},{3,1},{4,6},{5,7},{6,4},{7,5},{8,10},{9,11},{10,... | collective-permute-start | bytes 405512 | tf_op jit(solution)/shard_map/ppermute | solution.py:143
  9.4 11.8 %collective-permute-start.7 = (bf16[528,128]{1,0:T(8,128)(2,1)S(1)}, bf16[528,128]{1,0:T(8,128)(2,1)S(1)}, u32[]{:S(2)}, u32[]{:S(2)}) collective-permute-start(bf16[528,128]{1,0:T(8,128)(2,1)S(1)} %get-tuple-element.30), channel_id=1, source_target_pairs={{0,4},{1,5},{2,6},{3,7},{4,0},{5,1},{6,2},{7,3},{8,12},{9,13},{10,... | collective-permute-start | bytes 405512 | tf_op jit(solution)/shard_map/ppermute | solution.py:143
  12.0 14.2 %collective-permute-start.8 = (bf16[528,128]{1,0:T(8,128)(2,1)S(1)}, bf16[528,128]{1,0:T(8,128)(2,1)S(1)}, u32[]{:S(2)}, u32[]{:S(2)}) collective-permute-start(bf16[528,128]{1,0:T(8,128)(2,1)S(1)} %get-tuple-element.31), channel_id=1, source_target_pairs={{0,5},{1,4},{2,7},{3,6},{4,1},{5,0},{6,3},{7,2},{8,13},{9,12},{10,... | collective-permute-start | bytes 405512 | tf_op jit(solution)/shard_map/ppermute | solution.py:143
  13.3 21.9 %collective-permute-start.3 = (bf16[1040,128]{1,0:T(8,128)(2,1)S(1)}, bf16[1040,128]{1,0:T(8,128)(2,1)S(1)}, u32[]{:S(2)}, u32[]{:S(2)}) collective-permute-start(bf16[1040,128]{1,0:T(8,128)(2,1)S(1)} %get-tuple-element.26), channel_id=1, source_target_pairs={{0,1},{1,0},{2,3},{3,2},{4,5},{5,4},{6,7},{7,6},{8,9},{9,8},{10,11... | collective-permute-start | bytes 798728 | tf_op jit(solution)/shard_map/ppermute | solution.py:143
  13.8 21.4 %collective-permute-start.5 = (bf16[1040,128]{1,0:T(8,128)(2,1)S(1)}, bf16[1040,128]{1,0:T(8,128)(2,1)S(1)}, u32[]{:S(2)}, u32[]{:S(2)}) collective-permute-start(bf16[1040,128]{1,0:T(8,128)(2,1)S(1)} %get-tuple-element.28), channel_id=1, source_target_pairs={{0,3},{1,2},{2,1},{3,0},{4,7},{5,6},{6,5},{7,4},{8,11},{9,10},{10,... | collective-permute-start | bytes 798728 | tf_op jit(solution)/shard_map/ppermute | solution.py:143
  15.5 16.6 %collective-permute-start.10 = (bf16[528,128]{1,0:T(8,128)(2,1)S(1)}, bf16[528,128]{1,0:T(8,128)(2,1)S(1)}, u32[]{:S(2)}, u32[]{:S(2)}) collective-permute-start(bf16[528,128]{1,0:T(8,128)(2,1)S(1)} %get-tuple-element.32), channel_id=1, source_target_pairs={{0,7},{1,6},{2,5},{3,4},{4,3},{5,2},{6,1},{7,0},{8,15},{9,14},{10,... | collective-permute-start | bytes 405512 | tf_op jit(solution)/shard_map/ppermute | solution.py:143
  21.2 12.9 %collective-permute-start.9 = (bf16[528,128]{1,0:T(8,128)(2,1)S(1)}, bf16[528,128]{1,0:T(8,128)(2,1)S(1)}, u32[]{:S(2)}, u32[]{:S(2)}) collective-permute-start(bf16[528,128]{1,0:T(8,128)(2,1)S(1)} %get-tuple-element.27), channel_id=1, source_target_pairs={{0,6},{1,7},{2,4},{3,5},{4,2},{5,3},{6,0},{7,1},{8,14},{9,15},{10,... | collective-permute-start | bytes 405512 | tf_op jit(solution)/shard_map/ppermute | solution.py:143
  26.1 9.0 %collective-permute-start.4 = (bf16[528,128]{1,0:T(8,128)(2,1)S(1)}, bf16[528,128]{1,0:T(8,128)(2,1)S(1)}, u32[]{:S(2)}, u32[]{:S(2)}) collective-permute-start(bf16[528,128]{1,0:T(8,128)(2,1)S(1)} %get-tuple-element.27), channel_id=1, source_target_pairs={{0,2},{1,3},{2,0},{3,1},{4,6},{5,7},{6,4},{7,5},{8,10},{9,11},{10,... | collective-permute-start | bytes 405512 | tf_op jit(solution)/shard_map/ppermute | solution.py:143
  35.2 14.4 %copy-start.3 = (bf16[1,128,2048]{2,1,0:T(8,128)(2,1)S(1)}, bf16[1,128,2048]{2,1,0:T(8,128)(2,1)}, u32[]{:S(2)}) copy-start(bf16[1,128,2048]{2,1,0:T(8,128)(2,1)} %refs_6_.3) | copy-start | bytes 1572868
  38.3 4.0 %collective-permute-start.14 = (bf16[1024,128]{1,0:T(8,128)(2,1)S(1)}, bf16[1024,128]{1,0:T(8,128)(2,1)S(1)}, u32[]{:S(2)}, u32[]{:S(2)}) collective-permute-start(bf16[1024,128]{1,0:T(8,128)(2,1)S(1)} %get-tuple-element.35.refs_1_), channel_id=1, source_target_pairs={{0,8},{8,0},{16,24},{24,16},{1,9},{9,1},{17,25},{25,17},{2,10},{10... | collective-permute-start | bytes 786440 | tf_op jit(solution)/shard_map/ppermute | solution.py:491
  38.3 11.3 %collective-permute-start.13 = (bf16[1024,128]{1,0:T(8,128)(2,1)}, bf16[1024,128]{1,0:T(8,128)(2,1)S(1)}, u32[]{:S(2)}, u32[]{:S(2)}) collective-permute-start(bf16[1024,128]{1,0:T(8,128)(2,1)} %get-tuple-element.36), channel_id=1, source_target_pairs={{0,3},{1,2},{2,1},{3,0},{4,7},{5,6},{6,5},{7,4},{8,11},{9,10},{10,... | collective-permute-start | bytes 786440 | tf_op jit(solution)/shard_map/ppermute | solution.py:143
  41.7 12.9 %collective-permute-start.11 = (bf16[1024,128]{1,0:T(8,128)(2,1)}, bf16[1024,128]{1,0:T(8,128)(2,1)S(1)}, u32[]{:S(2)}, u32[]{:S(2)}) collective-permute-start(bf16[1024,128]{1,0:T(8,128)(2,1)} %get-tuple-element.33), channel_id=1, source_target_pairs={{0,1},{1,0},{2,3},{3,2},{4,5},{5,4},{6,7},{7,6},{8,9},{9,8},{10,11... | collective-permute-start | bytes 786440 | tf_op jit(solution)/shard_map/ppermute | solution.py:143
  42.0 7.7 %copy-start = (bf16[1,128,2048]{2,1,0:T(8,128)(2,1)S(1)}, bf16[1,128,2048]{2,1,0:T(8,128)(2,1)}, u32[]{:S(2)}) copy-start(bf16[1,128,2048]{2,1,0:T(8,128)(2,1)} %refs_5_.3) | copy-start | bytes 1572868
  42.0 7.7 %copy-start.1 = (bf16[1,128,2048]{2,1,0:T(8,128)(2,1)S(1)}, bf16[1,128,2048]{2,1,0:T(8,128)(2,1)}, u32[]{:S(2)}) copy-start(bf16[1,128,2048]{2,1,0:T(8,128)(2,1)} %refs_3_.3) | copy-start | bytes 1572868
  42.0 7.7 %copy-start.2 = (bf16[1,128,2048]{2,1,0:T(8,128)(2,1)S(1)}, bf16[1,128,2048]{2,1,0:T(8,128)(2,1)}, u32[]{:S(2)}) copy-start(bf16[1,128,2048]{2,1,0:T(8,128)(2,1)} %refs_4_.3) | copy-start | bytes 1572868
  42.0 12.6 %collective-permute-start.12 = (bf16[1024,128]{1,0:T(8,128)(2,1)S(1)}, bf16[1024,128]{1,0:T(8,128)(2,1)S(1)}, u32[]{:S(2)}, u32[]{:S(2)}) collective-permute-start(bf16[1024,128]{1,0:T(8,128)(2,1)S(1)} %get-tuple-element.34), channel_id=1, source_target_pairs={{0,2},{1,3},{2,0},{3,1},{4,6},{5,7},{6,4},{7,5},{8,10},{9,11},{10,... | collective-permute-start | bytes 786440 | tf_op jit(solution)/shard_map/ppermute | solution.py:143
  45.3 11.6 %all-to-all-start = ((f32[32,1,128]{2,1,0:T(1,128)}), f32[32,1,128]{2,1,0:T(1,128)S(1)}, u32[]{:S(2)}, u32[]{:S(2)}) async-start(f32[32,1,128]{2,1,0:T(1,128)} %bitcast.7), calls=%async_computation | async-start | bytes 32768 | tf_op jit(solution)/shard_map/all_to_all | solution.py:497

commit v8 on v7

--- a/solution.py
+++ b/solution.py
@@ -291,7 +291,7 @@
     return line
 
 
-def gather(quarters, place_ref, ab_in, r_in, a_ref, data_ref):
+def gather(quarters, place_ref, ab_in, r_in, a_ref, data_ref, far=None):
     half, quarter = place_ref[0], place_ref[1]
     local = a_ref.shape[2] // BLOCK
     for j in range(quarters):
@@ -301,19 +301,28 @@
             a_ref[quarter ^ j, :, lanes] = ab_in[j][g * BLOCK : (g + 1) * BLOCK]
             b_rows = slice((b_row + g) * BLOCK, (b_row + g + 1) * BLOCK)
             data_ref[half * quarters + (quarter ^ j), :, lanes] = b_in[b_rows]
-            data_ref[(1 - half) * quarters + (quarter ^ j), :, lanes] = r_in[j][g * BLOCK : (g + 1) * BLOCK]
+            if far is None:
+                data_ref[(1 - half) * quarters + (quarter ^ j), :, lanes] = r_in[j][g * BLOCK : (g + 1) * BLOCK]
 
 
 def lags_kernel(quarters, place_ref, *refs):
     ab_in, r_in, refs = refs[: quarters + 1], refs[quarters + 1 : 2 * quarters + 1], refs[2 * quarters + 1 :]
     shares_ref, a_ref, data_ref, lines_ref = refs
-    gather(quarters, place_ref, ab_in, r_in, a_ref, data_ref)
-    half = place_ref[0]
+    gather(quarters, place_ref, ab_in, r_in, a_ref, data_ref, ())
+    half, quarter = place_ref[0], place_ref[1]
+
+    def fetch(first, groups):
+        for j in range(quarters):
+            for g in groups:
+                lanes = slice(g * BLOCK, (g + 1) * BLOCK)
+                data_ref[first + (quarter ^ j), :, lanes] = r_in[j][g * BLOCK : (g + 1) * BLOCK]
+
     local = lines_ref.shape[0]
     length = quarters * BLOCK
 
     @pl.when(half == 0)
     def lower():
+        fetch(quarters, range(local // 2))
         for g in range(local):
             lanes = slice(g * BLOCK, (g + 1) * BLOCK)
             mixed, gated = rows_of(a_ref, lanes), rows_of(data_ref, lanes)
@@ -321,6 +330,7 @@
 
     @pl.when(half != 0)
     def upper():
+        fetch(0, range(local // 2, local))
         for g in range(local):
             lanes = slice(g * BLOCK, (g + 1) * BLOCK)
             gated, mixed = rows_of(a_ref, lanes), rows_of(data_ref, lanes)

time: 58.3 us -> 58.3 us (level)
  no operation moved by 1% of the time
where the time goes in v8:
time: 58.3 us; the launch traced here: 58.1 us
  starting transfers between devices  27.4 us (47%)
  waiting for transfers between devices  16.6 us (28%)
  Pallas kernels  11.4 us (20%)
  other arithmetic  1.98 us (3%)
  between operations  0.74 us (1%)
    ppermute x11, starting transfers between devices, swap(): return lax.ppermute(chunk, 'seq', [(i, i ^ flip) for i in range(count)])  19.9 us
    ppermute x11, waiting for transfers between devices, swap(): return lax.ppermute(chunk, 'seq', [(i, i ^ flip) for i in range(count)])  14.9 us
    pallas_call x3, Pallas kernels, call(): pl.pallas_call(body, in_specs=[pl.BlockSpec(memory_space=pltpu.SMEM)] + v...  4.91 us
    all_to_all x1, starting transfers between devices, swapped(): arrived = lax.all_to_all(shares, every, 0, 0, tiled=True)  4.32 us
    pallas_call x2, Pallas kernels, gate_outputs(): pl.pallas_call(lambda *refs: outputs_kernel(js, *refs), in_specs=[pl.Bloc...  3.36 us
    pallas_call x1, Pallas kernels, swapped(): pl.pallas_call(lambda *refs: sums_kernel(quarters, dp_count, *refs), in_s...  3.15 us
    ppermute x3, starting transfers between devices, swapped(): lax.ppermute(taps, 'dp', [(i, i ^ p) for i in range(dp_count)])  3.12 us
    select_n x1, other arithmetic, swapped(): a, b = (jnp.where(lower, mixed, gated), jnp.where(lower, gated, mixed))  1.9 us
  transfers between devices with their start and end apart: 16, of which 9 were waited for; matrix products, arithmetic and copies ran while one was open for 3% of the time, Pallas kernels for 11%

profile of v8, /device:TPU:0, one launch (start us, length us, event | category | flops | bytes accessed | tf_op | source)
XLA Modules:
  0.0 58.1 jit_solution(1139862229355735276)
XLA Ops:
  0.6 2.4 %collective-permute-start.2 = (bf16[16,32]{1,0:T(8,128)(2,1)}, bf16[16,32]{1,0:T(8,128)(2,1)S(1)}, u32[]{:S(2)}, u32[]{:S(2)}) collective-permute-start(bf16[16,32]{1,0:T(8,128)(2,1)} %bitcast.14), channel_id=1, source_target_pairs={{0,24},{8,16},{16,8},{24,0},{1,25},{9,17},{17,9},{25,1},{2,26},{10... | collective-permute-start | bytes 3080 | tf_op jit(solution)/shard_map/ppermute | solution.py:464
  3.1 0.6 %collective-permute-start.1 = (bf16[16,32]{1,0:T(8,128)(2,1)}, bf16[16,32]{1,0:T(8,128)(2,1)S(1)}, u32[]{:S(2)}, u32[]{:S(2)}) collective-permute-start(bf16[16,32]{1,0:T(8,128)(2,1)} %bitcast.15), channel_id=1, source_target_pairs={{0,16},{8,24},{16,0},{24,8},{1,17},{9,25},{17,1},{25,9},{2,18},{10... | collective-permute-start | bytes 3080 | tf_op jit(solution)/shard_map/ppermute | solution.py:464
  3.8 1.9 %select_bitcast_fusion = (bf16[128,2048]{1,0:T(8,128)(2,1)S(1)}, bf16[128,2048]{1,0:T(8,128)(2,1)S(1)}) fusion(pred[]{:T(512)S(6)} %lt.10, bf16[1,128,2048]{2,1,0:T(8,128)(2,1)} %refs_5_.3, bf16[1,128,2048]{2,1,0:T(8,128)(2,1)} %refs_3_.3, bf16[1,128,2048]{2,1,0:T(8,128)(2,1)} %refs_4_.3, bf16[1,128,2048]{2,1,0:T(8,128)(2,1)} %refs_6_.3), kind=kLoop, calls=%fused_computation.2 | loop fusion | flops 2621440 | bytes 3145729 | tf_op jit(solution)/shard_map/jit(_where)/select_n | solution.py:470
  5.8 1.1 %collective-permute-done.1.refs_2_ = bf16[16,32]{1,0:T(8,128)(2,1)S(1)} collective-permute-done((bf16[16,32]{1,0:T(8,128)(2,1)}, bf16[16,32]{1,0:T(8,128)(2,1)S(1)}, u32[]{:S(2)}, u32[]{:S(2)}) %collective-permute-start.1) | collective-permute-done | bytes 1056 | tf_op jit(solution)/shard_map/ppermute | solution.py:464
  6.9 0.8 %pack.1 = (bf16[528,128]{1,0:T(8,128)(2,1)S(1)}, bf16[528,128]{1,0:T(8,128)(2,1)S(1)}, bf16[528,128]{1,0:T(8,128)(2,1)S(1)}, bf16[528,128]{1,0:T(8,128)(2,1)S(1)...) custom-call(s32[3]{0:T(128)S(1)} %pad_add_fusion.place_ref.refs_0_, ...), custom_call_target="tpu_custom_call" | custom-call | flops 1000 | bytes 1000 | tf_op jit(solution)/shard_map/pack/pallas_call | solution.py:158
  7.7 1.6 %collective-permute-start.6 = (bf16[528,128]{1,0:T(8,128)(2,1)S(1)}, bf16[528,128]{1,0:T(8,128)(2,1)S(1)}, u32[]{:S(2)}, u32[]{:S(2)}) collective-permute-start(bf16[528,128]{1,0:T(8,128)(2,1)S(1)} %get-tuple-element.29), channel_id=1, source_target_pairs={{0,2},{1,3},{2,0},{3,1},{4,6},{5,7},{6,4},{7,5},{8,10},{9,11},{10,... | collective-permute-start | bytes 405512 | tf_op jit(solution)/shard_map/ppermute | solution.py:143
  9.4 2.6 %collective-permute-start.7 = (bf16[528,128]{1,0:T(8,128)(2,1)S(1)}, bf16[528,128]{1,0:T(8,128)(2,1)S(1)}, u32[]{:S(2)}, u32[]{:S(2)}) collective-permute-start(bf16[528,128]{1,0:T(8,128)(2,1)S(1)} %get-tuple-element.30), channel_id=1, source_target_pairs={{0,4},{1,5},{2,6},{3,7},{4,0},{5,1},{6,2},{7,3},{8,12},{9,13},{10,... | collective-permute-start | bytes 405512 | tf_op jit(solution)/shard_map/ppermute | solution.py:143
  12.0 1.3 %collective-permute-start.8 = (bf16[528,128]{1,0:T(8,128)(2,1)S(1)}, bf16[528,128]{1,0:T(8,128)(2,1)S(1)}, u32[]{:S(2)}, u32[]{:S(2)}) collective-permute-start(bf16[528,128]{1,0:T(8,128)(2,1)S(1)} %get-tuple-element.31), channel_id=1, source_target_pairs={{0,5},{1,4},{2,7},{3,6},{4,1},{5,0},{6,3},{7,2},{8,13},{9,12},{10,... | collective-permute-start | bytes 405512 | tf_op jit(solution)/shard_map/ppermute | solution.py:143
  13.8 1.4 %collective-permute-start.5 = (bf16[1040,128]{1,0:T(8,128)(2,1)S(1)}, bf16[1040,128]{1,0:T(8,128)(2,1)S(1)}, u32[]{:S(2)}, u32[]{:S(2)}) collective-permute-start(bf16[1040,128]{1,0:T(8,128)(2,1)S(1)} %get-tuple-element.28), channel_id=1, source_target_pairs={{0,3},{1,2},{2,1},{3,0},{4,7},{5,6},{6,5},{7,4},{8,11},{9,10},{10,... | collective-permute-start | bytes 798728 | tf_op jit(solution)/shard_map/ppermute | solution.py:143
  15.5 4.8 %collective-permute-start.10 = (bf16[528,128]{1,0:T(8,128)(2,1)S(1)}, bf16[528,128]{1,0:T(8,128)(2,1)S(1)}, u32[]{:S(2)}, u32[]{:S(2)}) collective-permute-start(bf16[528,128]{1,0:T(8,128)(2,1)S(1)} %get-tuple-element.32), channel_id=1, source_target_pairs={{0,7},{1,6},{2,5},{3,4},{4,3},{5,2},{6,1},{7,0},{8,15},{9,14},{10,... | collective-permute-start | bytes 405512 | tf_op jit(solution)/shard_map/ppermute | solution.py:143
  20.2 0.9 %collective-permute-done.7.refs_6_.refs_5_ = bf16[528,128]{1,0:T(8,128)(2,1)S(1)} collective-permute-done((bf16[528,128]{1,0:T(8,128)(2,1)S(1)}, bf16[528,128]{1,0:T(8,128)(2,1)S(1)}, u32[]{:S(2)}, u32[]{:S(2)}) %collective-permute-start.7) | collective-permute-done | bytes 135200 | tf_op jit(solution)/shard_map/ppermute | solution.py:143
  21.2 3.7 %collective-permute-start.9 = (bf16[528,128]{1,0:T(8,128)(2,1)S(1)}, bf16[528,128]{1,0:T(8,128)(2,1)S(1)}, u32[]{:S(2)}, u32[]{:S(2)}) collective-permute-start(bf16[528,128]{1,0:T(8,128)(2,1)S(1)} %get-tuple-element.27), channel_id=1, source_target_pairs={{0,6},{1,7},{2,4},{3,5},{4,2},{5,3},{6,0},{7,1},{8,14},{9,15},{10,... | collective-permute-start | bytes 405512 | tf_op jit(solution)/shard_map/ppermute | solution.py:143
  24.9 1.2 %collective-permute-done.8.refs_7_.refs_6_ = bf16[528,128]{1,0:T(8,128)(2,1)S(1)} collective-permute-done((bf16[528,128]{1,0:T(8,128)(2,1)S(1)}, bf16[528,128]{1,0:T(8,128)(2,1)S(1)}, u32[]{:S(2)}, u32[]{:S(2)}) %collective-permute-start.8) | collective-permute-done | bytes 135200 | tf_op jit(solution)/shard_map/ppermute | solution.py:143
  26.1 6.0 %collective-permute-done.10.refs_9_.refs_8_ = bf16[528,128]{1,0:T(8,128)(2,1)S(1)} collective-permute-done((bf16[528,128]{1,0:T(8,128)(2,1)S(1)}, bf16[528,128]{1,0:T(8,128)(2,1)S(1)}, u32[]{:S(2)}, u32[]{:S(2)}) %collective-permute-start.10) | collective-permute-done | bytes 135200 | tf_op jit(solution)/shard_map/ppermute | solution.py:143
  32.1 1.9 %collective-permute-done.9.refs_8_.refs_7_ = bf16[528,128]{1,0:T(8,128)(2,1)S(1)} collective-permute-done((bf16[528,128]{1,0:T(8,128)(2,1)S(1)}, bf16[528,128]{1,0:T(8,128)(2,1)S(1)}, u32[]{:S(2)}, u32[]{:S(2)}) %collective-permute-start.9) | collective-permute-done | bytes 135200 | tf_op jit(solution)/shard_map/ppermute | solution.py:143
  34.1 1.1 %collective-permute-done.4.refs_3_.refs_2_ = bf16[528,128]{1,0:T(8,128)(2,1)S(1)} collective-permute-done((bf16[528,128]{1,0:T(8,128)(2,1)S(1)}, bf16[528,128]{1,0:T(8,128)(2,1)S(1)}, u32[]{:S(2)}, u32[]{:S(2)}) %collective-permute-start.4) | collective-permute-done | bytes 135200 | tf_op jit(solution)/shard_map/ppermute | solution.py:143
  35.2 3.1 %sums.1 = (bf16[1024,128]{1,0:T(8,128)(2,1)S(1)}, bf16[1024,128]{1,0:T(8,128)(2,1)}, bf16[1024,128]{1,0:T(8,128)(2,1)S(1)}, bf16[1024,128]{1,0:T(8,128)(2,1)}) custom-call(s32[3]{0:T(128)S(1)} %pad_add_fusion.place_ref.refs_0_, bf16[1040,128]{1,0:T(8,128)(2,1)S(1)} %get-tuple-element.25.refs_1_.refs_0_, ...), custom_call_target="tpu_custom_call" | custom-call | flops 1000 | bytes 1000 | tf_op jit(solution)/shard_map/sums/pallas_call | solution.py:487
  38.3 3.4 %collective-permute-start.13 = (bf16[1024,128]{1,0:T(8,128)(2,1)}, bf16[1024,128]{1,0:T(8,128)(2,1)S(1)}, u32[]{:S(2)}, u32[]{:S(2)}) collective-permute-start(bf16[1024,128]{1,0:T(8,128)(2,1)} %get-tuple-element.36), channel_id=1, source_target_pairs={{0,3},{1,2},{2,1},{3,0},{4,7},{5,6},{6,5},{7,4},{8,11},{9,10},{10,... | collective-permute-start | bytes 786440 | tf_op jit(solution)/shard_map/ppermute | solution.py:143
  42.4 2.9 %lags.1 = f32[32,128]{1,0:T(8,128)} custom-call(s32[3]{0:T(128)S(1)} %pad_add_fusion.place_ref.refs_0_, bf16[1040,128]{1,0:T(8,128)(2,1)S(1)} %get-tuple-element.25.refs_1_.refs_0_, bf16[1040,128]{1,0:T(8,128)(2,1)S(1)} %collective-permute-done.3.refs_2_.refs_1_, bf16[528,128]{1,0:T(8,128)(2,1)S(1)} %collective-permute-done.4.refs_3_.refs_2_, ...), custom_call_target="tpu_custom_call" | custom-call | flops 1000 | bytes 1000 | tf_op jit(solution)/shard_map/lags/pallas_call | solution.py:158
  45.2 4.3 %all-to-all-start = ((f32[32,1,128]{2,1,0:T(1,128)}), f32[32,1,128]{2,1,0:T(1,128)S(1)}, u32[]{:S(2)}, u32[]{:S(2)}) async-start(f32[32,1,128]{2,1,0:T(1,128)} %bitcast.7), calls=%async_computation | async-start | bytes 32768 | tf_op jit(solution)/shard_map/all_to_all | solution.py:507
  49.6 1.7 %outputs.2 = (bf16[1,128,2048]{2,1,0:T(8,128)(2,1)}, bf16[1,128,2048]{2,1,0:T(8,128)(2,1)}, bf16[1,128,2048]{2,1,0:T(8,128)(2,1)}, bf16[1,128,2048]{2,1,0:T(8,128)(2,1)}) custom-call(s32[3]{0:T(128)S(1)} %pad_add_fusion.place_ref.refs_0_, bf16[1024,128]{1,0:T(8,128)(2,1)S(1)} %get-tuple-element.35.refs_1_, ...), custom_call_target="tpu_custom_call" | custom-call | flops 1000 | bytes 1000 | tf_op jit(solution)/shard_map/outputs/pallas_call | solution.py:436
  51.3 3.3 %collective-permute-done.11.refs_1_ = bf16[1024,128]{1,0:T(8,128)(2,1)S(1)} collective-permute-done((bf16[1024,128]{1,0:T(8,128)(2,1)}, bf16[1024,128]{1,0:T(8,128)(2,1)S(1)}, u32[]{:S(2)}, u32[]{:S(2)}) %collective-permute-start.11) | collective-permute-done | bytes 262176 | tf_op jit(solution)/shard_map/ppermute | solution.py:143
  54.6 1.7 %outputs.3 = (bf16[1,128,2048]{2,1,0:T(8,128)(2,1)}, bf16[1,128,2048]{2,1,0:T(8,128)(2,1)}, bf16[1,128,2048]{2,1,0:T(8,128)(2,1)}, bf16[1,128,2048]{2,1,0:T(8,128)(2,1)}) custom-call(s32[3]{0:T(128)S(1)} %pad_add_fusion.place_ref.refs_0_, ...), custom_call_target="tpu_custom_call", output_to_operand_aliasing={{0}: (7, {}), {1}: (8, {}), {2}: (9, {}), {3}: (10, {})} | custom-call | flops 1000 | bytes 1000 | tf_op jit(solution)/shard_map/outputs/pallas_call | solution.py:436
  56.9 1.2 %owned.1 = f32[16,32]{1,0:T(8,128)} custom-call(s32[3]{0:T(128)S(1)} %pad_add_fusion.place_ref.refs_0_, f32[32,128]{1,0:T(8,128)S(1)} %bitcast.13), custom_call_target="tpu_custom_call" | custom-call | flops 1000 | bytes 1000 | tf_op jit(solution)/shard_map/owned/pallas_call | solution.py:158
  (26 shorter events, 2.2 us)
Async XLA Ops:
  0.6 5.1 %collective-permute-start.2 = (bf16[16,32]{1,0:T(8,128)(2,1)}, bf16[16,32]{1,0:T(8,128)(2,1)S(1)}, u32[]{:S(2)}, u32[]{:S(2)}) collective-permute-start(bf16[16,32]{1,0:T(8,128)(2,1)} %bitcast.14), channel_id=1, source_target_pairs={{0,24},{8,16},{16,8},{24,0},{1,25},{9,17},{17,9},{25,1},{2,26},{10... | collective-permute-start | bytes 3080 | tf_op jit(solution)/shard_map/ppermute | solution.py:464
  3.1 3.8 %collective-permute-start.1 = (bf16[16,32]{1,0:T(8,128)(2,1)}, bf16[16,32]{1,0:T(8,128)(2,1)S(1)}, u32[]{:S(2)}, u32[]{:S(2)}) collective-permute-start(bf16[16,32]{1,0:T(8,128)(2,1)} %bitcast.15), channel_id=1, source_target_pairs={{0,16},{8,24},{16,0},{24,8},{1,17},{9,25},{17,1},{25,9},{2,18},{10... | collective-permute-start | bytes 3080 | tf_op jit(solution)/shard_map/ppermute | solution.py:464
  3.7 3.2 %collective-permute-start = (bf16[16,32]{1,0:T(8,128)(2,1)}, bf16[16,32]{1,0:T(8,128)(2,1)S(1)}, u32[]{:S(2)}, u32[]{:S(2)}) collective-permute-start(bf16[16,32]{1,0:T(8,128)(2,1)} %bitcast.16), channel_id=1, source_target_pairs={{0,8},{8,0},{16,24},{24,16},{1,9},{9,1},{17,25},{25,17},{2,10},{10... | collective-permute-start | bytes 3080 | tf_op jit(solution)/shard_map/ppermute | solution.py:464
  5.7 1.2 %copy-start.4 = (bf16[32,16]{0,1:T(8,128)(2,1)S(1)}, bf16[32,16]{0,1:T(8,128)(2,1)}, u32[]{:S(2)}) copy-start(bf16[32,16]{0,1:T(8,128)(2,1)} %param.9) | copy-start | bytes 3076
  7.7 7.8 %collective-permute-start.6 = (bf16[528,128]{1,0:T(8,128)(2,1)S(1)}, bf16[528,128]{1,0:T(8,128)(2,1)S(1)}, u32[]{:S(2)}, u32[]{:S(2)}) collective-permute-start(bf16[528,128]{1,0:T(8,128)(2,1)S(1)} %get-tuple-element.29), channel_id=1, source_target_pairs={{0,2},{1,3},{2,0},{3,1},{4,6},{5,7},{6,4},{7,5},{8,10},{9,11},{10,... | collective-permute-start | bytes 405512 | tf_op jit(solution)/shard_map/ppermute | solution.py:143
  9.4 11.8 %collective-permute-start.7 = (bf16[528,128]{1,0:T(8,128)(2,1)S(1)}, bf16[528,128]{1,0:T(8,128)(2,1)S(1)}, u32[]{:S(2)}, u32[]{:S(2)}) collective-permute-start(bf16[528,128]{1,0:T(8,128)(2,1)S(1)} %get-tuple-element.30), channel_id=1, source_target_pairs={{0,4},{1,5},{2,6},{3,7},{4,0},{5,1},{6,2},{7,3},{8,12},{9,13},{10,... | collective-permute-start | bytes 405512 | tf_op jit(solution)/shard_map/ppermute | solution.py:143
  12.0 14.2 %collective-permute-start.8 = (bf16[528,128]{1,0:T(8,128)(2,1)S(1)}, bf16[528,128]{1,0:T(8,128)(2,1)S(1)}, u32[]{:S(2)}, u32[]{:S(2)}) collective-permute-start(bf16[528,128]{1,0:T(8,128)(2,1)S(1)} %get-tuple-element.31), channel_id=1, source_target_pairs={{0,5},{1,4},{2,7},{3,6},{4,1},{5,0},{6,3},{7,2},{8,13},{9,12},{10,... | collective-permute-start | bytes 405512 | tf_op jit(solution)/shard_map/ppermute | solution.py:143
  13.3 21.9 %collective-permute-start.3 = (bf16[1040,128]{1,0:T(8,128)(2,1)S(1)}, bf16[1040,128]{1,0:T(8,128)(2,1)S(1)}, u32[]{:S(2)}, u32[]{:S(2)}) collective-permute-start(bf16[1040,128]{1,0:T(8,128)(2,1)S(1)} %get-tuple-element.26), channel_id=1, source_target_pairs={{0,1},{1,0},{2,3},{3,2},{4,5},{5,4},{6,7},{7,6},{8,9},{9,8},{10,11... | collective-permute-start | bytes 798728 | tf_op jit(solution)/shard_map/ppermute | solution.py:143
  13.8 21.4 %collective-permute-start.5 = (bf16[1040,128]{1,0:T(8,128)(2,1)S(1)}, bf16[1040,128]{1,0:T(8,128)(2,1)S(1)}, u32[]{:S(2)}, u32[]{:S(2)}) collective-permute-start(bf16[1040,128]{1,0:T(8,128)(2,1)S(1)} %get-tuple-element.28), channel_id=1, source_target_pairs={{0,3},{1,2},{2,1},{3,0},{4,7},{5,6},{6,5},{7,4},{8,11},{9,10},{10,... | collective-permute-start | bytes 798728 | tf_op jit(solution)/shard_map/ppermute | solution.py:143
  15.5 16.6 %collective-permute-start.10 = (bf16[528,128]{1,0:T(8,128)(2,1)S(1)}, bf16[528,128]{1,0:T(8,128)(2,1)S(1)}, u32[]{:S(2)}, u32[]{:S(2)}) collective-permute-start(bf16[528,128]{1,0:T(8,128)(2,1)S(1)} %get-tuple-element.32), channel_id=1, source_target_pairs={{0,7},{1,6},{2,5},{3,4},{4,3},{5,2},{6,1},{7,0},{8,15},{9,14},{10,... | collective-permute-start | bytes 405512 | tf_op jit(solution)/shard_map/ppermute | solution.py:143
  21.2 12.9 %collective-permute-start.9 = (bf16[528,128]{1,0:T(8,128)(2,1)S(1)}, bf16[528,128]{1,0:T(8,128)(2,1)S(1)}, u32[]{:S(2)}, u32[]{:S(2)}) collective-permute-start(bf16[528,128]{1,0:T(8,128)(2,1)S(1)} %get-tuple-element.27), channel_id=1, source_target_pairs={{0,6},{1,7},{2,4},{3,5},{4,2},{5,3},{6,0},{7,1},{8,14},{9,15},{10,... | collective-permute-start | bytes 405512 | tf_op jit(solution)/shard_map/ppermute | solution.py:143
  26.1 9.0 %collective-permute-start.4 = (bf16[528,128]{1,0:T(8,128)(2,1)S(1)}, bf16[528,128]{1,0:T(8,128)(2,1)S(1)}, u32[]{:S(2)}, u32[]{:S(2)}) collective-permute-start(bf16[528,128]{1,0:T(8,128)(2,1)S(1)} %get-tuple-element.27), channel_id=1, source_target_pairs={{0,2},{1,3},{2,0},{3,1},{4,6},{5,7},{6,4},{7,5},{8,10},{9,11},{10,... | collective-permute-start | bytes 405512 | tf_op jit(solution)/shard_map/ppermute | solution.py:143
  35.2 14.4 %copy-start.3 = (bf16[1,128,2048]{2,1,0:T(8,128)(2,1)S(1)}, bf16[1,128,2048]{2,1,0:T(8,128)(2,1)}, u32[]{:S(2)}) copy-start(bf16[1,128,2048]{2,1,0:T(8,128)(2,1)} %refs_6_.3) | copy-start | bytes 1572868
  38.3 4.0 %collective-permute-start.14 = (bf16[1024,128]{1,0:T(8,128)(2,1)S(1)}, bf16[1024,128]{1,0:T(8,128)(2,1)S(1)}, u32[]{:S(2)}, u32[]{:S(2)}) collective-permute-start(bf16[1024,128]{1,0:T(8,128)(2,1)S(1)} %get-tuple-element.35.refs_1_), channel_id=1, source_target_pairs={{0,8},{8,0},{16,24},{24,16},{1,9},{9,1},{17,25},{25,17},{2,10},{10... | collective-permute-start | bytes 786440 | tf_op jit(solution)/shard_map/ppermute | solution.py:501
  38.3 11.2 %collective-permute-start.13 = (bf16[1024,128]{1,0:T(8,128)(2,1)}, bf16[1024,128]{1,0:T(8,128)(2,1)S(1)}, u32[]{:S(2)}, u32[]{:S(2)}) collective-permute-start(bf16[1024,128]{1,0:T(8,128)(2,1)} %get-tuple-element.36), channel_id=1, source_target_pairs={{0,3},{1,2},{2,1},{3,0},{4,7},{5,6},{6,5},{7,4},{8,11},{9,10},{10,... | collective-permute-start | bytes 786440 | tf_op jit(solution)/shard_map/ppermute | solution.py:143
  41.7 12.9 %collective-permute-start.11 = (bf16[1024,128]{1,0:T(8,128)(2,1)}, bf16[1024,128]{1,0:T(8,128)(2,1)S(1)}, u32[]{:S(2)}, u32[]{:S(2)}) collective-permute-start(bf16[1024,128]{1,0:T(8,128)(2,1)} %get-tuple-element.33), channel_id=1, source_target_pairs={{0,1},{1,0},{2,3},{3,2},{4,5},{5,4},{6,7},{7,6},{8,9},{9,8},{10,11... | collective-permute-start | bytes 786440 | tf_op jit(solution)/shard_map/ppermute | solution.py:143
  42.0 7.6 %copy-start = (bf16[1,128,2048]{2,1,0:T(8,128)(2,1)S(1)}, bf16[1,128,2048]{2,1,0:T(8,128)(2,1)}, u32[]{:S(2)}) copy-start(bf16[1,128,2048]{2,1,0:T(8,128)(2,1)} %refs_5_.3) | copy-start | bytes 1572868
  42.0 7.6 %copy-start.1 = (bf16[1,128,2048]{2,1,0:T(8,128)(2,1)S(1)}, bf16[1,128,2048]{2,1,0:T(8,128)(2,1)}, u32[]{:S(2)}) copy-start(bf16[1,128,2048]{2,1,0:T(8,128)(2,1)} %refs_3_.3) | copy-start | bytes 1572868
  42.0 7.6 %copy-start.2 = (bf16[1,128,2048]{2,1,0:T(8,128)(2,1)S(1)}, bf16[1,128,2048]{2,1,0:T(8,128)(2,1)}, u32[]{:S(2)}) copy-start(bf16[1,128,2048]{2,1,0:T(8,128)(2,1)} %refs_4_.3) | copy-start | bytes 1572868
  42.0 12.6 %collective-permute-start.12 = (bf16[1024,128]{1,0:T(8,128)(2,1)S(1)}, bf16[1024,128]{1,0:T(8,128)(2,1)S(1)}, u32[]{:S(2)}, u32[]{:S(2)}) collective-permute-start(bf16[1024,128]{1,0:T(8,128)(2,1)S(1)} %get-tuple-element.34), channel_id=1, source_target_pairs={{0,2},{1,3},{2,0},{3,1},{4,6},{5,7},{6,4},{7,5},{8,10},{9,11},{10,... | collective-permute-start | bytes 786440 | tf_op jit(solution)/shard_map/ppermute | solution.py:143
  45.2 11.7 %all-to-all-start = ((f32[32,1,128]{2,1,0:T(1,128)}), f32[32,1,128]{2,1,0:T(1,128)S(1)}, u32[]{:S(2)}, u32[]{:S(2)}) async-start(f32[32,1,128]{2,1,0:T(1,128)} %bitcast.7), calls=%async_computation | async-start | bytes 32768 | tf_op jit(solution)/shard_map/all_to_all | solution.py:507
